TPU v7x, 32 devices: a whole 2x2x4 slice. The times are simulated.
32 devices in a mesh: dp: 16 (over z, y, x), tensor: 2 (over core).
Axes of the slice: x: 2, y: 2, z: 4, core: 2. Of those that a mesh axis runs over, the one named last changes fastest.
Arguments:
- inputs: bfloat16 [3, 16384, 1024], P(None, ('dp', 'tensor')), may hold values from -6 to 6
- gain_attn: bfloat16 [1024], P('dp'), may hold values from 0.5 to 1.5
- gain_mlp: bfloat16 [1024], P('dp'), may hold values from 0.5 to 1.5
- w_query: bfloat16 [1024, 256], P('dp', 'tensor'), may hold values from -0.1875 to 0.1875
- w_key: bfloat16 [1024, 256], P('dp', 'tensor'), may hold values from -0.1875 to 0.1875
- w_value: bfloat16 [1024, 1024], P('dp', 'tensor'), may hold values from -0.1875 to 0.1875
- w_out: bfloat16 [1024, 1024], P('tensor', 'dp'), may hold values from -3 to 3
- w_gate: bfloat16 [1024, 2752], P('dp', 'tensor'), may hold values from -0.1875 to 0.1875
- w_up: bfloat16 [1024, 2752], P('dp', 'tensor'), may hold values from -0.1875 to 0.1875
- w_down: bfloat16 [2752, 1024], P('tensor', 'dp'), may hold values from -0.109375 to 0.109375
- out_grad: bfloat16 [3, 16384, 1024], P(None, ('dp', 'tensor')), may hold values from -6 to 6
- lengths: int32 [3, 16, 8], P(None, 'dp'), may hold values from 1 to 512, 1024 in all within a row
Outputs:
- mixed_out: bfloat16 [3, 16384, 1024], P(None, ('dp', 'tensor'))
- input_grad: float32 [3, 16384, 1024], P(None, ('dp', 'tensor'))
- grad_gain_attn: float32 [1024], P('dp')
- grad_gain_mlp: float32 [1024], P('dp')
- grad_query: float32 [1024, 256], P('dp', 'tensor')
- grad_key: float32 [1024, 256], P('dp', 'tensor')
- grad_value: float32 [1024, 1024], P('dp', 'tensor')
- grad_out: float32 [1024, 1024], P('tensor', 'dp')
- grad_gate: float32 [1024, 2752], P('dp', 'tensor')
- grad_up: float32 [1024, 2752], P('dp', 'tensor')
- grad_down: float32 [2752, 1024], P('tensor', 'dp')
Inputs may be any that keep to these rules, and one draw needn't show every extreme that they name: Each group's 8 lengths sum to 1024, and the longest is exactly 512.
All inputs are finite; a program needn't handle non-finite values.
Results may differ from a plain program's by a relative error of at most 0.025.
Values may be sent and summed in bfloat16 or wider, within the bound.
A program may use at most 320 MiB of HBM per device.

v0:
```python
import math

import jax
import jax.numpy as jnp
import numpy as np
from jax import lax
from jax.sharding import PartitionSpec as P

FEAT = 16
VD = 64
BLK = 512


EXACT = lax.Precision.HIGHEST


def taylor(halved):
    feature_dim = halved.shape[-1]
    upper_idx, lower_idx = np.triu_indices(feature_dim)
    flat_index = jnp.asarray(upper_idx * feature_dim + lower_idx, jnp.int32)
    factors = jnp.asarray(np.where(upper_idx == lower_idx, math.sqrt(0.5), 1.0), jnp.float32)
    outer = (halved[..., :, None] * halved[..., None, :]).reshape(
        halved.shape[:-1] + (feature_dim * feature_dim,)
    )
    second = jnp.take(outer, flat_index, axis=-1) * factors
    ones_col = jnp.ones(halved.shape[:-1] + (1,), jnp.float32)
    return jnp.concatenate([ones_col, halved, second], axis=-1)


def attend_block(carry_in, block_in):
    kv_state, totals, previous = carry_in
    queries, keys_in, values_in, doc_ids = block_in
    half_q = 0.5 * queries
    half_k = 0.5 * keys_in
    scores = jnp.einsum("rhf,chf->hrc", half_q, half_k, preferred_element_type=jnp.float32)
    places = jnp.arange(doc_ids.shape[0], dtype=jnp.int32)
    allowed = (doc_ids[:, None] == doc_ids[None, :]) & (places[None, :] <= places[:, None])
    weights = jnp.where(allowed[None], 1.0 + scores + 0.5 * scores * scores, 0.0)
    feat_q = taylor(half_q)
    feat_k = taylor(half_k)
    carried_in = (doc_ids == previous).astype(jnp.float32)
    numerator = jnp.einsum("hrc,chv->rhv", weights, values_in, precision=EXACT) + carried_in[
        :, None, None
    ] * jnp.einsum("rhf,hfv->rhv", feat_q, kv_state, precision=EXACT)
    denominator = jnp.sum(weights, axis=2).T + carried_in[:, None] * jnp.einsum(
        "rhf,hf->rh", feat_q, totals, precision=EXACT
    )
    mixed_rows = numerator / denominator[:, :, None]
    final_doc = doc_ids[-1]
    staying = (doc_ids == final_doc).astype(jnp.float32)[:, None, None] * feat_k
    joined = (final_doc == previous).astype(jnp.float32)
    kv_state = jnp.einsum("rhf,rhv->hfv", staying, values_in, precision=EXACT) + joined * kv_state
    totals = jnp.sum(staying, axis=0) + joined * totals
    return ((kv_state, totals, final_doc), mixed_rows)


def attend(queries, keys_in, values_in, doc_ids):
    row_total, head_count, feature_dim = queries.shape
    value_dim = values_in.shape[2]
    block_count = row_total // BLK
    feature_total = 1 + feature_dim + feature_dim * (feature_dim + 1) // 2
    initial = (
        jnp.zeros((head_count, feature_total, value_dim), jnp.float32),
        jnp.zeros((head_count, feature_total), jnp.float32),
        jnp.array(-1, jnp.int32),
    )
    pieces = (
        queries.reshape(block_count, BLK, head_count, feature_dim),
        keys_in.reshape(block_count, BLK, head_count, feature_dim),
        values_in.reshape(block_count, BLK, head_count, value_dim),
        doc_ids.reshape(block_count, BLK),
    )
    last_carry, mixed_rows = lax.scan(jax.checkpoint(attend_block), initial, pieces)
    return mixed_rows.reshape(row_total, head_count * value_dim)


def document_ids(lengths_row, row_total):
    doc_ends = jnp.cumsum(lengths_row)
    places = jnp.arange(row_total, dtype=jnp.int32)
    return jnp.sum((places[:, None] >= doc_ends[None, :]).astype(jnp.int32), axis=1)


def rows_product(left, right):
    return lax.dot_general(
        left, right, (((0,), (0,)), ((), ())), preferred_element_type=jnp.float32
    )


def back_product(left, right):
    return lax.dot_general(
        left, right, (((1,), (1,)), ((), ())), preferred_element_type=jnp.float32
    )


def norm_back(grad_normed, normed, inverse, gain_full):
    scaled = grad_normed * gain_full
    return inverse * (scaled - normed * jnp.mean(scaled * normed, axis=-1, keepdims=True))


def row_slice(matrix, first_row, row_count):
    return lax.dynamic_slice_in_dim(matrix, first_row, row_count, 0)


def inverse_root(values):
    return lax.rsqrt(jnp.mean(values * values, axis=-1, keepdims=True) + 1e-05)


def fetch_weights(gain_attn, gain_mlp, w_query, w_key, w_value, w_out, w_gate, w_up, w_down):
    row_parts = (
        lax.all_gather(w_query, "dp", axis=0, tiled=True),
        lax.all_gather(w_key, "dp", axis=0, tiled=True),
        lax.all_gather(w_value, "dp", axis=0, tiled=True),
        lax.all_gather(w_gate, "dp", axis=0, tiled=True),
        lax.all_gather(w_up, "dp", axis=0, tiled=True),
        lax.all_gather(gain_attn, "dp", axis=0, tiled=True),
        lax.all_gather(gain_mlp, "dp", axis=0, tiled=True),
    )
    col_parts = (
        lax.all_gather(w_out, "dp", axis=1, tiled=True),
        lax.all_gather(w_down, "dp", axis=1, tiled=True),
    )
    return tuple(row_parts) + tuple(col_parts)


def body(
    inputs,
    gain_attn,
    gain_mlp,
    w_query,
    w_key,
    w_value,
    w_out,
    w_gate,
    w_up,
    w_down,
    out_grad,
    lengths,
):
    micro_count = inputs.shape[0]
    shard_rows = inputs.shape[1]
    model_dim = inputs.shape[2]
    group_rows = shard_rows * lax.axis_size("tensor")
    local_heads = w_query.shape[1] // FEAT
    grad_query_sum = jnp.zeros((model_dim, w_query.shape[1]), jnp.float32)
    grad_key_sum = jnp.zeros((model_dim, w_key.shape[1]), jnp.float32)
    grad_value_sum = jnp.zeros((model_dim, w_value.shape[1]), jnp.float32)
    grad_gate_sum = jnp.zeros((model_dim, w_gate.shape[1]), jnp.float32)
    grad_up_sum = jnp.zeros((model_dim, w_up.shape[1]), jnp.float32)
    grad_out_sum = jnp.zeros((w_out.shape[0], model_dim), jnp.float32)
    grad_down_sum = jnp.zeros((w_down.shape[0], model_dim), jnp.float32)
    gain_attn_sum = jnp.zeros((model_dim,), jnp.float32)
    gain_mlp_sum = jnp.zeros((model_dim,), jnp.float32)
    outputs = []
    input_grads = []
    for micro_step in range(micro_count):
        (
            full_query,
            full_key,
            full_value,
            full_gate,
            full_up,
            full_gain_attn,
            full_gain_mlp,
            full_out,
            full_down,
        ) = fetch_weights(gain_attn, gain_mlp, w_query, w_key, w_value, w_out, w_gate, w_up, w_down)
        gain_in = full_gain_attn.astype(jnp.float32)
        gain_mid = full_gain_mlp.astype(jnp.float32)
        doc_ids = document_ids(lengths[micro_step, 0], group_rows)
        values = inputs[micro_step].astype(jnp.float32)
        inverse_in = inverse_root(values)
        normed_in = values * inverse_in
        gathered_in = lax.all_gather(
            (normed_in * gain_in).astype(jnp.bfloat16), "tensor", axis=0, tiled=True
        )
        query_low = jnp.dot(gathered_in, full_query, preferred_element_type=jnp.float32).astype(
            jnp.bfloat16
        )
        key_low = jnp.dot(gathered_in, full_key, preferred_element_type=jnp.float32).astype(
            jnp.bfloat16
        )
        value_low = jnp.dot(gathered_in, full_value, preferred_element_type=jnp.float32).astype(
            jnp.bfloat16
        )
        query_full = query_low.astype(jnp.float32).reshape(group_rows, local_heads, FEAT)
        key_full = key_low.astype(jnp.float32).reshape(group_rows, local_heads, FEAT)
        value_full = value_low.astype(jnp.float32).reshape(group_rows, local_heads, VD)

        def local_attend(query_arg, key_arg, value_arg):
            return attend(query_arg, key_arg, value_arg, doc_ids)

        mixed_full, pullback = jax.vjp(local_attend, query_full, key_full, value_full)
        mixed_low = mixed_full.astype(jnp.bfloat16)
        residual = values + lax.psum_scatter(
            jnp.dot(
                row_slice(mixed_low, jnp.int32(0), shard_rows * lax.axis_size("tensor")),
                full_out,
                preferred_element_type=jnp.float32,
            ),
            "tensor",
            scatter_dimension=0,
            tiled=True,
        )
        inverse_mid = inverse_root(residual)
        normed_mid = residual * inverse_mid
        gathered_mid = lax.all_gather(
            (normed_mid * gain_mid).astype(jnp.bfloat16), "tensor", axis=0, tiled=True
        )
        gate_pre = jnp.dot(gathered_mid, full_gate, preferred_element_type=jnp.float32)
        up_pre = jnp.dot(gathered_mid, full_up, preferred_element_type=jnp.float32)
        sigmoid_gate = jax.nn.sigmoid(gate_pre)
        silu_gate = gate_pre * sigmoid_gate
        hidden = (silu_gate * up_pre).astype(jnp.bfloat16)
        mlp_part = lax.psum_scatter(
            jnp.dot(
                row_slice(hidden, jnp.int32(0), shard_rows * lax.axis_size("tensor")),
                full_down,
                preferred_element_type=jnp.float32,
            ).astype(jnp.bfloat16),
            "tensor",
            scatter_dimension=0,
            tiled=True,
        ).astype(jnp.float32)
        outputs.append((residual + mlp_part).astype(jnp.bfloat16))
        cotangent = out_grad[micro_step]
        gathered_grad = lax.all_gather(cotangent, "tensor", axis=0, tiled=True)
        grad_down_sum += rows_product(hidden, gathered_grad)
        grad_hidden = back_product(gathered_grad, full_down)
        grad_gate_low = (
            grad_hidden * up_pre * sigmoid_gate * (1.0 + gate_pre * (1.0 - sigmoid_gate))
        ).astype(jnp.bfloat16)
        grad_up_low = (grad_hidden * silu_gate).astype(jnp.bfloat16)
        grad_gate_sum += rows_product(gathered_mid, grad_gate_low)
        grad_up_sum += rows_product(gathered_mid, grad_up_low)
        first_row = jnp.int32(0)
        grad_mid = lax.psum_scatter(
            back_product(
                row_slice(grad_gate_low, first_row, shard_rows * lax.axis_size("tensor")), full_gate
            )
            + back_product(
                row_slice(grad_up_low, first_row, shard_rows * lax.axis_size("tensor")), full_up
            ),
            "tensor",
            scatter_dimension=0,
            tiled=True,
        )
        gain_mlp_sum += jnp.sum(grad_mid * normed_mid, axis=0)
        grad_resid = cotangent.astype(jnp.float32) + norm_back(
            grad_mid, normed_mid, inverse_mid, gain_mid
        )
        gathered_resid = lax.all_gather(
            grad_resid.astype(jnp.bfloat16), "tensor", axis=0, tiled=True
        )
        grad_out_sum += rows_product(mixed_low, gathered_resid)
        grad_mixed = back_product(gathered_resid, full_out).astype(jnp.bfloat16).astype(jnp.float32)
        grad_query_full, grad_key_full, grad_value_full = pullback(grad_mixed)
        grad_query_low = grad_query_full.reshape(group_rows, -1).astype(jnp.bfloat16)
        grad_key_low = grad_key_full.reshape(group_rows, -1).astype(jnp.bfloat16)
        grad_value_low = grad_value_full.reshape(group_rows, -1).astype(jnp.bfloat16)
        grad_query_sum += rows_product(gathered_in, grad_query_low)
        grad_key_sum += rows_product(gathered_in, grad_key_low)
        grad_value_sum += rows_product(gathered_in, grad_value_low)
        attn_first_row = jnp.int32(0)
        grad_in = lax.psum_scatter(
            (
                back_product(
                    row_slice(grad_query_low, attn_first_row, shard_rows * lax.axis_size("tensor")),
                    full_query,
                )
                + back_product(
                    row_slice(grad_key_low, attn_first_row, shard_rows * lax.axis_size("tensor")),
                    full_key,
                )
                + back_product(
                    row_slice(grad_value_low, attn_first_row, shard_rows * lax.axis_size("tensor")),
                    full_value,
                )
            ).astype(jnp.bfloat16),
            "tensor",
            scatter_dimension=0,
            tiled=True,
        ).astype(jnp.float32)
        gain_attn_sum += jnp.sum(grad_in * normed_in, axis=0)
        input_grads.append(grad_resid + norm_back(grad_in, normed_in, inverse_in, gain_in))
    row_grads = (
        lax.psum_scatter(
            grad_query_sum.astype(jnp.bfloat16), "dp", scatter_dimension=0, tiled=True
        ).astype(jnp.float32),
        lax.psum_scatter(
            grad_key_sum.astype(jnp.bfloat16), "dp", scatter_dimension=0, tiled=True
        ).astype(jnp.float32),
        lax.psum_scatter(
            grad_value_sum.astype(jnp.bfloat16), "dp", scatter_dimension=0, tiled=True
        ).astype(jnp.float32),
        lax.psum_scatter(
            grad_gate_sum.astype(jnp.bfloat16), "dp", scatter_dimension=0, tiled=True
        ).astype(jnp.float32),
        lax.psum_scatter(
            grad_up_sum.astype(jnp.bfloat16), "dp", scatter_dimension=0, tiled=True
        ).astype(jnp.float32),
        lax.psum_scatter(
            gain_attn_sum.astype(jnp.bfloat16), "dp", scatter_dimension=0, tiled=True
        ).astype(jnp.float32),
        lax.psum_scatter(
            gain_mlp_sum.astype(jnp.bfloat16), "dp", scatter_dimension=0, tiled=True
        ).astype(jnp.float32),
    )
    col_grads = (
        lax.psum_scatter(
            grad_out_sum.astype(jnp.bfloat16), "dp", scatter_dimension=1, tiled=True
        ).astype(jnp.float32),
        lax.psum_scatter(
            grad_down_sum.astype(jnp.bfloat16), "dp", scatter_dimension=1, tiled=True
        ).astype(jnp.float32),
    )
    gain_grads = lax.psum((row_grads[5], row_grads[6]), "tensor")
    return (
        jnp.stack(outputs, 0),
        jnp.stack(input_grads, 0),
        gain_grads[0],
        gain_grads[1],
        row_grads[0],
        row_grads[1],
        row_grads[2],
        col_grads[0],
        row_grads[3],
        row_grads[4],
        col_grads[1],
    )


def solution(mesh):
    in_specs = (
        P(None, ("dp", "tensor"), None),
        P("dp"),
        P("dp"),
        P("dp", "tensor"),
        P("dp", "tensor"),
        P("dp", "tensor"),
        P("tensor", "dp"),
        P("dp", "tensor"),
        P("dp", "tensor"),
        P("tensor", "dp"),
        P(None, ("dp", "tensor"), None),
        P(None, "dp", None),
    )
    out_specs = (
        P(None, ("dp", "tensor"), None),
        P(None, ("dp", "tensor"), None),
        P("dp"),
        P("dp"),
        P("dp", "tensor"),
        P("dp", "tensor"),
        P("dp", "tensor"),
        P("tensor", "dp"),
        P("dp", "tensor"),
        P("dp", "tensor"),
        P("tensor", "dp"),
    )
    return jax.shard_map(body, mesh=mesh, in_specs=in_specs, out_specs=out_specs, check_vma=False)
```

profile of v0, /device:TPU:0, one launch (start us, length us, event | category | flops | bytes accessed | tf_op | source)
XLA Modules:
  0.0 2320.7 jit_solution(1262514424219461189)
XLA Ops:
  11.8 44.3 %all-reduce.6 = (bf16[1024]{0:T(1024)(128)(2,1)S(1)}, bf16[1024]{0:T(1024)(128)(2,1)}) all-reduce(bf16[1024]{0:T(1024)(128)(2,1)S(1)} %dynamic-update-slice, bf16[1024]{0:T(1024)(128)(2,1)S(1)} %dynamic-update-slice.1), channel_id=1, replica_groups=mesh['dp'=16,'tensor'=2] {'dp'}, use_global_device_ids=true, to_apply=%add | all-reduce | flops 2048 | bytes 8192
  63.2 36.9 %all_gather.83 = bf16[1024,128]{1,0:T(8,128)(2,1)S(1)} all-gather(bf16[64,128]{1,0:T(8,128)(2,1)S(1)} %copy-done.239), channel_id=1, replica_groups=mesh['dp'=16,'tensor'=2] {'dp'}, dimensions={0}, use_global_device_ids=true | all-gather | bytes 278528 | tf_op jit(solution)/shard_map/all_gather | solution.py:111
  100.0 39.1 %all_gather.85 = bf16[1024,128]{1,0:T(8,128)(2,1)S(1)} all-gather(bf16[64,128]{1,0:T(8,128)(2,1)S(1)} %copy-done.240), channel_id=1, replica_groups=mesh['dp'=16,'tensor'=2] {'dp'}, dimensions={0}, use_global_device_ids=true | all-gather | bytes 278528 | tf_op jit(solution)/shard_map/all_gather | solution.py:110
  165.4 121.6 %while.160 = (s32[]{:T(128)}, f32[8,153,64]{1,2,0:T(8,128)S(1)}, f32[8,153]{1,0:T(8,128)S(1)}, s32[]{:T(128)}, bf16[2,512,8,64]{1,3,2,0:T(8,128)(2,1)}, /*index=...) while((s32[]{:T(128)}, f32[8,153,64]{1,2,0:T(8,128)S(1)}, ...), condition=%wide.region_16.17_spmd.clone.clone.clone.clone, body=%wide.region_13.16_spmd.clone.clone.clone.clone.sunk | while | flops 2683114752 | bytes 106233200 | solution.py:73
  311.9 105.6 %while.161 = (s32[]{:T(128)}, f32[8,153,64]{1,2,0:T(8,128)S(1)}, f32[8,153]{1,0:T(8,128)S(1)}, s32[]{:T(128)}, bf16[2,512,8,64]{1,3,2,0:T(8,128)(2,1)}, /*index=...) while((s32[]{:T(128)}, f32[8,153,64]{1,2,0:T(8,128)S(1)}, ...), condition=%wide.region_26.27_spmd.clone.clone.clone.clone, body=%wide.region_23.26_spmd.clone.clone.clone.clone.sunk | while | flops 2683114752 | bytes 106233200 | solution.py:73
  442.4 106.5 %while.159 = (s32[]{:T(128)}, f32[8,153,64]{1,2,0:T(8,128)S(1)}, f32[8,153]{1,0:T(8,128)S(1)}, s32[]{:T(128)}, bf16[2,512,8,64]{1,3,2,0:T(8,128)(2,1)}, /*index=...) while((s32[]{:T(128)}, f32[8,153,64]{1,2,0:T(8,128)S(1)}, ...), condition=%wide.region_6.7_spmd.clone.clone.clone.clone, body=%wide.region_3.6_spmd.clone.clone.clone.clone.sunk | while | flops 2683114752 | bytes 106233200 | solution.py:73
  577.0 58.8 %all-gather.29.cloned.1.call-done = bf16[1024,1376]{1,0:T(8,128)(2,1)} async-done(((bf16[64,1376]{1,0:T(8,128)(2,1)}), bf16[1024,1376]{1,0:T(8,128)(2,1)}) %all-gather.29.cloned.1.call-update) | async-done | bytes 2818064 | tf_op jit(solution)/shard_map/all_gather | solution.py:113
  635.8 11.7 all-gather.27.cloned.1.call-done
  655.7 62.0 %all-gather.31.cloned.1.call-done = bf16[1024,1376]{1,0:T(8,128)(2,1)} async-done(((bf16[64,1376]{1,0:T(8,128)(2,1)}), bf16[1024,1376]{1,0:T(8,128)(2,1)}) %all-gather.31.cloned.1.call-update) | async-done | bytes 2818064 | tf_op jit(solution)/shard_map/all_gather | solution.py:114
  728.8 70.2 %all-gather.33.cloned.1.call-done = bf16[1376,1024]{0,1:T(8,128)(2,1)} async-done(((bf16[1376,64]{0,1:T(8,128)(2,1)}), bf16[1376,1024]{0,1:T(8,128)(2,1)}) %all-gather.33.cloned.1.call-update) | async-done | bytes 2818064 | tf_op jit(solution)/shard_map/all_gather | solution.py:120
  799.1 11.5 multiply_convert_fusion.4
  819.7 11.1 reduce-scatter.32.cloned.1.call-done
  838.6 9.8 all-gather.41.cloned.1.call-done
  861.7 11.5 multiply_convert_fusion
  896.0 13.0 multiply_convert_fusion.2
  944.5 13.1 reduce-scatter.26.cloned.1.call-done
  1025.7 281.0 %while.157 = (s32[]{:T(128)}, f32[8,153,64]{1,2,0:T(8,128)}, f32[8,153]{1,0:T(8,128)}, bf16[2,512,8,16]{1,3,2,0:T(8,128)(2,1)}, bf16[2,512,8,16]{1,3,2,0:T(8,128...) while((s32[]{:T(128)}, f32[8,153,64]{1,2,0:T(8,128)}, ...), condition=%wide.region_55.57_spmd.clone.clone.clone, body=%wide.region_46.56_spmd.sunk.clone.clone.clone.sunk | while | flops 7536320512 | bytes 292638848 | solution.py:73
  1043.8 17.6 scatter_fusion.3
  1089.0 9.3 fusion.793
  1109.7 10.0 fusion.788
  1129.9 17.6 scatter_fusion.2
  1183.8 17.9 scatter_fusion.3
  1229.2 9.3 fusion.793
  1249.7 10.1 fusion.788
  1270.0 17.8 scatter_fusion.2
  1318.7 280.7 %while.158 = (s32[]{:T(128)}, f32[8,153,64]{1,2,0:T(8,128)}, f32[8,153]{1,0:T(8,128)}, bf16[2,512,8,16]{1,3,2,0:T(8,128)(2,1)}, bf16[2,512,8,16]{1,3,2,0:T(8,128...) while((s32[]{:T(128)}, f32[8,153,64]{1,2,0:T(8,128)}, ...), condition=%wide.region_69.71_spmd.clone.clone.clone, body=%wide.region_60.70_spmd.sunk.clone.clone.clone.sunk | while | flops 7536320512 | bytes 292643264 | solution.py:73
  1336.6 17.9 scatter_fusion.5
  1402.6 10.1 fusion.819
  1422.8 17.9 scatter_fusion.4
  1476.8 17.6 scatter_fusion.5
  1521.9 9.5 fusion.824
  1542.6 10.1 fusion.819
  1562.8 17.6 scatter_fusion.4
  1611.4 285.5 %while.156 = (s32[]{:T(128)}, f32[8,153,64]{1,2,0:T(8,128)}, f32[8,153]{1,0:T(8,128)}, bf16[2,512,8,16]{1,3,2,0:T(8,128)(2,1)}, bf16[2,512,8,16]{1,3,2,0:T(8,128...) while((s32[]{:T(128)}, f32[8,153,64]{1,2,0:T(8,128)}, ...), condition=%wide.region_41.43_spmd.clone.clone.clone, body=%wide.region_32.42_spmd.sunk.clone.clone.clone.sunk | while | flops 7536320512 | bytes 292643264 | solution.py:73
  1629.5 17.6 scatter_fusion.1
  1674.6 9.3 fusion.762
  1695.3 10.0 fusion.757
  1715.4 17.6 scatter_fusion
  1769.0 17.9 scatter_fusion.1
  1834.8 10.1 fusion.757
  1855.0 17.9 scatter_fusion
  1958.5 25.8 %reduce-scatter.46.cloned.1.call-done = bf16[64,128]{1,0:T(8,128)(2,1)} async-done(((bf16[1024,128]{1,0:T(8,128)(2,1)}), bf16[64,128]{1,0:T(8,128)(2,1)}) %reduce-scatter.46.cloned.1.call-update) | async-done | bytes 16400 | tf_op jit(solution)/shard_map/reduce_scatter | solution.py:289
  1985.6 73.3 %reduce-scatter.44.cloned.1.call-done = bf16[64,128]{1,0:T(8,128)(2,1)} async-done(((bf16[1024,128]{1,0:T(8,128)(2,1)}), bf16[64,128]{1,0:T(8,128)(2,1)}) %reduce-scatter.44.cloned.1.call-update) | async-done | bytes 16400 | tf_op jit(solution)/shard_map/reduce_scatter | solution.py:286
  2060.3 75.1 %reduce-scatter.50.cloned.1.call-done = bf16[512,64]{0,1:T(8,128)(2,1)} async-done(((bf16[512,1024]{0,1:T(8,128)(2,1)}), bf16[512,64]{0,1:T(8,128)(2,1)}) %reduce-scatter.50.cloned.1.call-update) | async-done | bytes 65552 | tf_op jit(solution)/shard_map/reduce_scatter | solution.py:309
  2136.8 74.9 %reduce-scatter.48.cloned.1.call-done = bf16[64,512]{1,0:T(8,128)(2,1)} async-done(((bf16[1024,512]{1,0:T(8,128)(2,1)}), bf16[64,512]{1,0:T(8,128)(2,1)}) %reduce-scatter.48.cloned.1.call-update) | async-done | bytes 65552 | tf_op jit(solution)/shard_map/reduce_scatter | solution.py:292
  2219.9 13.2 reduce-scatter.42.cloned.1.call-done
  2233.1 13.6 reduce-scatter.34.cloned.1.call-done
  2250.4 42.0 %all-reduce.5 = (bf16[1024]{0:T(1024)(128)(2,1)S(1)}, bf16[1024]{0:T(1024)(128)(2,1)S(1)}) all-reduce(bf16[1024]{0:T(1024)(128)(2,1)S(1)} %add_convert_fusion.12, bf16[1024]{0:T(1024)(128)(2,1)S(1)} %add_convert_fusion.11), channel_id=17, replica_groups=mesh['dp'=16,'tensor'=2] {'dp'}, use_global_device_ids=true, to_apply=%region_75.77.clone | all-reduce | flops 2048 | bytes 8192
  (1624 shorter events, 1228.0 us)
Async XLA Ops:
  7.2 134.0 %all-gather.23.cloned.1.call-start = ((), (), s32[]{:S(2)}) async-start(), calls=%async_computation.20 | async-start | bytes 1114112 | tf_op jit(solution)/shard_map/all_gather | solution.py:112
  7.9 133.2 %all-gather.35.cloned.1.call-start = ((), (), s32[]{:S(2)}) async-start(), calls=%async_computation.28 | async-start | bytes 3145728 | tf_op jit(solution)/shard_map/all_gather | solution.py:173
  61.2 229.5 %all-gather.39.cloned.1.call-start = ((), (), s32[]{:S(2)}) async-start(), calls=%async_computation.32 | async-start | bytes 3145728 | tf_op jit(solution)/shard_map/all_gather | solution.py:173
  61.9 242.6 %all-gather.25.cloned.1.call-start = ((), (), s32[]{:S(2)}) async-start(), calls=%async_computation.21 | async-start | bytes 1114112 | tf_op jit(solution)/shard_map/all_gather | solution.py:119
  62.5 358.7 %all-gather.21.cloned.1.call-start = ((), (), s32[]{:S(2)}) async-start(), calls=%async_computation.19 | async-start | bytes 3145728 | tf_op jit(solution)/shard_map/all_gather | solution.py:173
  63.1 493.6 %reduce-scatter.24.cloned.1.call-start = ((), (), s32[]{:S(2)}) async-start(), calls=%async_computation.29 | async-start | bytes 6291456 | tf_op jit(solution)/shard_map/reduce_scatter | solution.py:194
  309.0 247.7 %reduce-scatter.28.cloned.1.call-start = ((), (), s32[]{:S(2)}) async-start(), calls=%async_computation.33 | async-start | bytes 6291456 | tf_op jit(solution)/shard_map/reduce_scatter | solution.py:194
  439.6 125.8 %reduce-scatter.20.cloned.1.call-start = ((), (), s32[]{:S(2)}) async-start(), calls=%async_computation.22 | async-start | bytes 6291456 | tf_op jit(solution)/shard_map/reduce_scatter | solution.py:194
  555.9 79.9 %all-gather.29.cloned.1.call-start = ((), (), s32[]{:S(2)}) async-start(), calls=%async_computation.24 | async-start | bytes 3063808 | tf_op jit(solution)/shard_map/all_gather | solution.py:113
  556.6 90.9 %all-gather.27.cloned.1.call-start = ((), (), s32[]{:S(2)}) async-start(), calls=%async_computation.23 | async-start | bytes 3145728 | tf_op jit(solution)/shard_map/all_gather | solution.py:206
  556.7 401.0 %copy-start.188 = (f32[1024]{0:T(1024)}, f32[1024]{0:T(1024)S(1)}, u32[]{:S(2)}) copy-start(f32[1024]{0:T(1024)S(1)} %convert_element_type.497) | copy-start | bytes 12292
  571.1 386.6 %copy-start.222 = (f32[512]{0:T(512)}, f32[512]{0:T(512)S(1)}, u32[]{:S(2)}) copy-start(f32[512]{0:T(512)S(1)} %add_rsqrt_fusion.4) | copy-start | bytes 6148
  573.7 144.1 %all-gather.31.cloned.1.call-start = ((), (), s32[]{:S(2)}) async-start(), calls=%async_computation.25 | async-start | bytes 3063808 | tf_op jit(solution)/shard_map/all_gather | solution.py:114
  574.4 154.4 %all-gather.49.cloned.1.call-start = ((), (), s32[]{:S(2)}) async-start(), calls=%async_computation.52 | async-start | bytes 3145728 | tf_op jit(solution)/shard_map/all_gather | solution.py:226
  576.2 222.9 %all-gather.33.cloned.1.call-start = ((), (), s32[]{:S(2)}) async-start(), calls=%async_computation.26 | async-start | bytes 3063808 | tf_op jit(solution)/shard_map/all_gather | solution.py:120
  576.9 253.9 %reduce-scatter.32.cloned.1.call-start = ((), (), s32[]{:S(2)}) async-start(), calls=%async_computation.36 | async-start | bytes 6291456 | tf_op jit(solution)/shard_map/reduce_scatter | solution.py:236
  724.7 85.9 %copy-start.243 = (bf16[1024,1376]{1,0:T(8,128)(2,1)S(1)}, bf16[1024,1376]{1,0:T(8,128)(2,1)}, u32[]{:S(2)}) copy-start(bf16[1024,1376]{1,0:T(8,128)(2,1)} %all-gather.29.cloned.1.call-done) | copy-start | bytes 8454148
  819.6 28.9 %all-gather.41.cloned.1.call-start = ((), (), s32[]{:S(2)}) async-start(), calls=%async_computation.34 | async-start | bytes 3145728 | tf_op jit(solution)/shard_map/all_gather | solution.py:206
  819.6 138.0 %copy-start.218 = (f32[512]{0:T(512)}, f32[512]{0:T(512)S(1)}, u32[]{:S(2)}) copy-start(f32[512]{0:T(512)S(1)} %add_rsqrt_fusion) | copy-start | bytes 6148
  819.6 138.0 %copy-start.220 = (f32[512]{0:T(512)}, f32[512]{0:T(512)S(1)}, u32[]{:S(2)}) copy-start(f32[512]{0:T(512)S(1)} %add_rsqrt_fusion.2) | copy-start | bytes 6148
  836.4 25.2 %all-gather.53.cloned.1.call-start = ((), (), s32[]{:S(2)}) async-start(), calls=%async_computation.54 | async-start | bytes 3145728 | tf_op jit(solution)/shard_map/all_gather | solution.py:226
  837.0 45.4 %all-gather.37.cloned.1.call-start = ((), (), s32[]{:S(2)}) async-start(), calls=%async_computation.30 | async-start | bytes 3145728 | tf_op jit(solution)/shard_map/all_gather | solution.py:206
  837.6 58.4 %all-gather.51.cloned.1.call-start = ((), (), s32[]{:S(2)}) async-start(), calls=%async_computation.53 | async-start | bytes 3145728 | tf_op jit(solution)/shard_map/all_gather | solution.py:226
  838.2 95.8 %reduce-scatter.40.cloned.1.call-start = ((), (), s32[]{:S(2)}) async-start(), calls=%async_computation.42 | async-start | bytes 6291456 | tf_op jit(solution)/shard_map/reduce_scatter | solution.py:236
  882.1 51.9 %reduce-scatter.36.cloned.1.call-start = ((), (), s32[]{:S(2)}) async-start(), calls=%async_computation.39 | async-start | bytes 6291456 | tf_op jit(solution)/shard_map/reduce_scatter | solution.py:236
  917.9 26.6 %reduce-scatter.30.cloned.1.call-start = ((), (), s32[]{:S(2)}) async-start(), calls=%async_computation.35 | async-start | bytes 3145728 | tf_op jit(solution)/shard_map/reduce_scatter | solution.py:214
  925.7 32.0 %reduce-scatter.26.cloned.1.call-start = ((), (), s32[]{:S(2)}) async-start(), calls=%async_computation.31 | async-start | bytes 3145728 | tf_op jit(solution)/shard_map/reduce_scatter | solution.py:214
  933.9 78.9 %all-gather.45.cloned.1.call-start = ((), (), s32[]{:S(2)}) async-start(), calls=%async_computation.40 | async-start | bytes 3145728 | tf_op jit(solution)/shard_map/all_gather | solution.py:251
  966.6 340.2 %all-gather.47.cloned.1.call-start = ((), (), s32[]{:S(2)}) async-start(), calls=%async_computation.43 | async-start | bytes 3145728 | tf_op jit(solution)/shard_map/all_gather | solution.py:251
  967.2 632.3 %all-gather.43.cloned.1.call-start = ((), (), s32[]{:S(2)}) async-start(), calls=%async_computation.37 | async-start | bytes 3145728 | tf_op jit(solution)/shard_map/all_gather | solution.py:251
  967.9 985.4 %reduce-scatter.56.cloned.1.call-start = ((), (), s32[]{:S(2)}) async-start(), calls=%async_computation.51 | async-start | bytes 3063808 | tf_op jit(solution)/shard_map/reduce_scatter | solution.py:312
  983.0 972.0 %reduce-scatter.54.cloned.1.call-start = ((), (), s32[]{:S(2)}) async-start(), calls=%async_computation.50 | async-start | bytes 3063808 | tf_op jit(solution)/shard_map/reduce_scatter | solution.py:298
  998.4 958.3 %reduce-scatter.52.cloned.1.call-start = ((), (), s32[]{:S(2)}) async-start(), calls=%async_computation.49 | async-start | bytes 3063808 | tf_op jit(solution)/shard_map/reduce_scatter | solution.py:295
  1012.8 971.5 %reduce-scatter.46.cloned.1.call-start = ((), (), s32[]{:S(2)}) async-start(), calls=%async_computation.46 | async-start | bytes 278528 | tf_op jit(solution)/shard_map/reduce_scatter | solution.py:289
  1906.8 152.2 %reduce-scatter.44.cloned.1.call-start = ((), (), s32[]{:S(2)}) async-start(), calls=%async_computation.45 | async-start | bytes 278528 | tf_op jit(solution)/shard_map/reduce_scatter | solution.py:286
  1912.3 223.1 %reduce-scatter.50.cloned.1.call-start = ((), (), s32[]{:S(2)}) async-start(), calls=%async_computation.48 | async-start | bytes 1114112 | tf_op jit(solution)/shard_map/reduce_scatter | solution.py:309
  1919.9 291.8 %reduce-scatter.48.cloned.1.call-start = ((), (), s32[]{:S(2)}) async-start(), calls=%async_computation.47 | async-start | bytes 1114112 | tf_op jit(solution)/shard_map/reduce_scatter | solution.py:292
  1930.2 289.7 %reduce-scatter.38.cloned.1.call-start = ((), (), s32[]{:S(2)}) async-start(), calls=%async_computation.41 | async-start | bytes 3145728 | tf_op jit(solution)/shard_map/reduce_scatter | solution.py:264
  1935.5 297.5 %reduce-scatter.42.cloned.1.call-start = ((), (), s32[]{:S(2)}) async-start(), calls=%async_computation.44 | async-start | bytes 3145728 | tf_op jit(solution)/shard_map/reduce_scatter | solution.py:264
  1940.5 306.3 %reduce-scatter.34.cloned.1.call-start = ((), (), s32[]{:S(2)}) async-start(), calls=%async_computation.38 | async-start | bytes 3145728 | tf_op jit(solution)/shard_map/reduce_scatter | solution.py:264
  1944.8 359.4 %reduce-scatter.22.cloned.1.call-start = ((), (), s32[]{:S(2)}) async-start(), calls=%async_computation.27 | async-start | bytes 3145728 | tf_op jit(solution)/shard_map/reduce_scatter | solution.py:214
  1952.4 294.3 %copy-start.32 = (bf16[3,512,1024]{2,1,0:T(8,128)(2,1)S(1)}, bf16[3,512,1024]{2,1,0:T(8,128)(2,1)}, u32[]{:S(2)}) copy-start(bf16[3,512,1024]{2,1,0:T(8,128)(2,1)} %param.30) | copy-start | bytes 9437188
  1952.4 294.3 %copy-start.217 = (f32[1024]{0:T(1024)S(1)}, f32[1024]{0:T(1024)}, u32[]{:S(2)}) copy-start(f32[1024]{0:T(1024)} %copy-done.216) | copy-start | bytes 12292
  1952.5 294.3 %copy-start.225 = (f32[512]{0:T(512)S(1)}, f32[512]{0:T(512)}, u32[]{:S(2)}) copy-start(f32[512]{0:T(512)} %copy-done.224) | copy-start | bytes 6148
  1952.5 294.3 %copy-start.227 = (f32[512]{0:T(512)S(1)}, f32[512]{0:T(512)}, u32[]{:S(2)}) copy-start(f32[512]{0:T(512)} %copy-done.226) | copy-start | bytes 6148
  1952.5 294.2 %copy-start.229 = (f32[512]{0:T(512)S(1)}, f32[512]{0:T(512)}, u32[]{:S(2)}) copy-start(f32[512]{0:T(512)} %copy-done.228) | copy-start | bytes 6148
  2213.3 82.5 %copy-start.221 = (f32[512]{0:T(512)S(1)}, f32[512]{0:T(512)}, u32[]{:S(2)}) copy-start(f32[512]{0:T(512)} %copy-done.220) | copy-start | bytes 6148
  2213.3 82.5 %copy-start.233 = (f32[512]{0:T(512)S(1)}, f32[512]{0:T(512)}, u32[]{:S(2)}) copy-start(f32[512]{0:T(512)} %copy-done.232) | copy-start | bytes 6148
  (423 other events, 3777.1 us)
Sparse Core Ops, SparseCore 0:
  10.8 58.2 all-gather.22
  71.2 9.8 all-gather.34
  82.7 11.7 all-gather.38
  97.1 56.8 all-gather.24
  155.4 9.3 all-gather.20
  309.1 7.9 reduce-scatter.23
  439.7 8.5 reduce-scatter.27
  556.0 9.3 reduce-scatter.19
  568.6 67.1 all-gather.28
  637.8 9.6 all-gather.26
  650.6 67.0 all-gather.30
  719.2 9.6 all-gather.48
  732.0 67.0 all-gather.32
  819.7 11.0 reduce-scatter.31
  836.6 11.8 all-gather.40
  849.9 11.7 all-gather.52
  863.6 11.7 all-gather.36
  876.8 11.7 all-gather.50
  890.9 13.1 reduce-scatter.39
  918.1 13.1 reduce-scatter.35
  933.6 10.8 reduce-scatter.29
  946.8 10.7 reduce-scatter.25
  966.7 11.7 all-gather.44
  979.9 11.7 all-gather.46
  993.2 11.7 all-gather.42
  1007.2 84.2 reduce-scatter.55
  1093.6 80.7 reduce-scatter.53
  1177.2 80.4 reduce-scatter.51
  1906.9 77.3 reduce-scatter.45
  1986.4 72.4 reduce-scatter.43
  2061.2 74.1 reduce-scatter.49
  2137.7 74.0 reduce-scatter.47
  2213.8 6.0 reduce-scatter.37
  2222.2 10.7 reduce-scatter.41
  2235.9 10.7 reduce-scatter.33
  2248.9 10.7 reduce-scatter.21
where the time goes:
time: 2340 us; the launch traced here: 2320 us
  matrix products  675 us (29%)
  waiting for transfers between devices  545 us (23%)
  other arithmetic  505 us (22%)
  local copies, waits for them, and re-layouts  356 us (15%)
  blocking collectives  165 us (7%)
  loops' own time  52.9 us (2%)
    scatter-add x12, other arithmetic, taylor(): second = jnp.take(outer, flat_index, axis=-1) * factors  213 us
    dot_general x24, matrix products, attend_block(): jnp.einsum('hrc,chv->rhv', weights, values_in, precision=EXACT)  208 us
    unnamed x2, blocking collectives  86.3 us
    dot_general x21, matrix products, back_product(): lax.dot_general(left, right, (((1,), (1,)), ((), ())), preferred_element_...  83.2 us
    gather x24, local copies, waits for them, and re-layouts, taylor(): second = jnp.take(outer, flat_index, axis=-1) * factors  78.3 us
    reduce_sum x12, other arithmetic, taylor(): halved[..., :, None] * halved[..., None, :]  75.6 us
    reduce_scatter x1, waiting for transfers between devices, body(): lax.psum_scatter(grad_out_sum.astype(jnp.bfloat16), 'dp', scatter_dimensi...  75.1 us
    reduce_scatter x1, waiting for transfers between devices, body(): lax.psum_scatter(grad_value_sum.astype(jnp.bfloat16), 'dp', scatter_dimen...  74.9 us
  transfers between devices with their start and end apart: 36, of which 17 were waited for; matrix products, arithmetic and copies ran while one was open for 63% of the time, Pallas kernels for 0%

commit v1 on v0

--- a/solution.py
+++ b/solution.py
@@ -1,9 +1,12 @@
+import functools
 import math
 
 import jax
 import jax.numpy as jnp
 import numpy as np
 from jax import lax
+from jax.experimental import pallas as pl
+from jax.experimental.pallas import tpu as pltpu
 from jax.sharding import PartitionSpec as P
 
 FEAT = 16
@@ -122,7 +125,7 @@
     return tuple(row_parts) + tuple(col_parts)
 
 
-def body(
+def plain_body(
     inputs,
     gain_attn,
     gain_mlp,
@@ -329,6 +332,748 @@
     )
 
 
+F32 = jnp.float32
+BF16 = jnp.bfloat16
+NN = (((1,), (0,)), ((), ()))
+NT = (((1,), (1,)), ((), ()))
+TN = (((0,), (0,)), ((), ()))
+TILE = 256
+SPAN = 2
+CHUNK = 512
+VMEM_BYTES = 60 << 20
+
+
+def mm(left, right, dims=NN):
+    return lax.dot_general(left, right, dims, preferred_element_type=F32)
+
+
+def params():
+    return pltpu.CompilerParams(vmem_limit_bytes=VMEM_BYTES)
+
+
+def anywhere():
+    return pl.BlockSpec(memory_space=pl.ANY)
+
+
+def exchange(value, bit):
+    count = lax.axis_size("dp")
+    return lax.ppermute(value, "dp", [(i, i ^ bit) for i in range(count)])
+
+
+def swap(value):
+    return lax.ppermute(value, "tensor", [(0, 1), (1, 0)])
+
+
+def gather_slab(slab):
+    half = slab.shape[0] // 2
+    far = lax.axis_size("dp") // 4
+    line = [slab] + [exchange(slab, 4 * k) for k in range(1, far)]
+    upper = jnp.stack([s[:half] for s in line])
+    lower = jnp.stack([s[half:] for s in line])
+    upper_y = exchange(upper, 2)
+    lower_x = exchange(lower, 1)
+    upper_x = exchange(upper, 1)
+    lower_y = exchange(lower, 2)
+    return (upper, lower, upper_x, lower_x, upper_y, lower_y, exchange(upper_y, 1), exchange(lower_x, 2))
+
+
+def place_slab(pieces, dest, sems):
+    me = lax.axis_index("dp")
+    far, half = pieces[0].shape[0], pieces[0].shape[1]
+    copies = []
+    for index, piece in enumerate(pieces):
+        for k in range(far):
+            row = (me ^ (4 * k + index // 2)) * (2 * half) + (index % 2) * half
+            copies.append(
+                pltpu.make_async_copy(
+                    piece.at[k], dest.at[pl.ds(pl.multiple_of(row, half), half)], sems.at[index, k]
+                )
+            )
+    for copy in copies:
+        copy.start()
+    for copy in copies:
+        copy.wait()
+
+
+def grad_shapes(rows, columns):
+    far = lax.axis_size("dp") // 4
+    half = rows // lax.axis_size("dp") // 2
+    return [jax.ShapeDtypeStruct((far, 2 * half, columns), BF16)] + [
+        jax.ShapeDtypeStruct((far, half, columns), BF16)
+    ] * 6
+
+
+def grad_specs(shapes):
+    return [pl.BlockSpec(s.shape, lambda *_: (0, 0, 0)) for s in shapes]
+
+
+def split_grads(total, outs):
+    me = lax.axis_index("dp")
+    far, rows = outs[0].shape[0], outs[0].shape[1]
+    half = rows // 2
+    for k in range(far):
+        for xy in range(4):
+            row = pl.multiple_of((me ^ (4 * k + xy)) * rows, rows)
+            if xy == 0:
+                outs[0][k] = total[pl.ds(row, rows)].astype(BF16)
+            else:
+                outs[2 * xy - 1][k] = total[pl.ds(row, half)].astype(BF16)
+                outs[2 * xy][k] = total[pl.ds(pl.multiple_of(row + half, half), half)].astype(BF16)
+
+
+def add(*terms):
+    total = terms[0].astype(F32)
+    for term in terms[1:]:
+        total = total + term.astype(F32)
+    return total
+
+
+def scatter_grads(pieces):
+    own, x_up, x_low, y_up, y_low, d_up, d_low = pieces
+    half = x_up.shape[1]
+    got_y_up = exchange(d_up, 1)
+    got_x_low = exchange(d_low, 2)
+    got_x_up = exchange(x_up, 1)
+    got_y_low = exchange(y_low, 2)
+    from_y_up = exchange(add(y_up, got_y_up).astype(BF16), 2)
+    from_x_low = exchange(add(x_low, got_x_low).astype(BF16), 1)
+    sums = []
+    for k in range(own.shape[0]):
+        top = add(own[k, :half], got_x_up[k], from_y_up[k])
+        low = add(own[k, half:], from_x_low[k], got_y_low[k])
+        sums.append(jnp.concatenate([top, low], 0))
+    arrived = [exchange(sums[k].astype(BF16), 4 * k) for k in range(1, own.shape[0])]
+    return add(sums[0], *arrived)
+
+
+def dma_sems(far):
+    return pltpu.SemaphoreType.DMA((8, far))
+
+
+def own_block(width, micro, rows):
+    return pl.BlockSpec((1, rows, width), lambda i, c: (jnp.maximum(i - micro, 0), 0, 0))
+
+
+def other_block(width, micro, rows):
+    return pl.BlockSpec((1, rows, width), lambda i, c: (jnp.minimum(i, micro - 1), 0, 0))
+
+
+def group_block(width, micro, rows, column=0):
+    def place(i, c):
+        return (lax.rem(i, micro), jnp.where(i < micro, 1 - c[0], c[0]), column)
+
+    return pl.BlockSpec((1, rows, width), place)
+
+
+def rows_kernel(kernel, name, core, micro, in_specs, out_specs, out_shape, scratch, operands):
+    return pl.pallas_call(
+        kernel,
+        grid_spec=pltpu.PrefetchScalarGridSpec(
+            num_scalar_prefetch=1,
+            grid=(2 * micro,),
+            in_specs=in_specs,
+            out_specs=out_specs,
+            scratch_shapes=scratch,
+        ),
+        out_shape=out_shape,
+        compiler_params=params(),
+        name=name,
+    )(core, *operands)
+
+
+def pick(is_other, other_ref, own_ref):
+    return jnp.where(is_other, other_ref[0], own_ref[0])
+
+
+def put(is_other, other_ref, own_ref, value):
+    @pl.when(is_other)
+    def _():
+        other_ref[0] = value
+
+    @pl.when(jnp.logical_not(is_other))
+    def _():
+        own_ref[0] = value
+
+
+def spread_gains(slab, column):
+    dim = slab.shape[0]
+    blocks = lax.axis_size("dp")
+    each = dim // blocks
+    lane_block = lax.broadcasted_iota(jnp.int32, (blocks, dim), 1) // each
+    block = lax.broadcasted_iota(jnp.int32, (blocks, dim), 0)
+    rows = []
+    for which in range(2):
+        picked = jnp.concatenate(
+            [slab[each * b : each * b + 16, column : column + 128].astype(F32)[which : which + 1] for b in range(blocks)], 0
+        )
+        tiled = jnp.concatenate([picked] * (dim // 128), 1)
+        rows.append(jnp.sum(jnp.where(lane_block == block, tiled, 0.0), axis=0, keepdims=True))
+    return jnp.concatenate(rows + [jnp.zeros((6, dim), F32)], 0)
+
+
+def project_kernel(micro, core, own, other, *refs):
+    pieces, (h_out, qkv_out, gain_out, slab, sems) = refs[:8], refs[8:]
+    i = pl.program_id(0)
+    columns = qkv_out.shape[2]
+
+    @pl.when(i == 0)
+    def _():
+        place_slab(pieces, slab, sems)
+        gain_out[...] = spread_gains(slab, columns)
+
+    x = pick(i < micro, other, own).astype(F32)
+    inverse = lax.rsqrt(jnp.mean(x * x, axis=-1, keepdims=True) + 1e-05)
+    h = (x * inverse * gain_out[0:1]).astype(BF16)
+    h_out[0] = h
+    qkv_out[0] = mm(h, slab[:, :columns]).astype(BF16)
+
+
+def project(core, x_own, x_other, pieces, columns):
+    micro, rows, dim = x_own.shape
+    return rows_kernel(
+        functools.partial(project_kernel, micro),
+        "project",
+        core,
+        micro,
+        [own_block(dim, micro, rows), other_block(dim, micro, rows)] + [anywhere()] * 8,
+        [
+            group_block(dim, micro, rows),
+            group_block(columns, micro, rows),
+            pl.BlockSpec((8, dim), lambda i, c: (0, 0)),
+        ],
+        [
+            jax.ShapeDtypeStruct((micro, 2 * rows, dim), BF16),
+            jax.ShapeDtypeStruct((micro, 2 * rows, columns), BF16),
+            jax.ShapeDtypeStruct((8, dim), F32),
+        ],
+        [pltpu.VMEM((dim, pieces[0].shape[2]), BF16), dma_sems(pieces[0].shape[0])],
+        (x_own, x_other, *pieces),
+    )
+
+
+def first_lane(lane):
+    return (lane == 0).astype(F32).astype(BF16)
+
+
+def attend_kernel(q_ref, k_ref, v_ref, start_ref, mix_ref, inv_ref, keys, mask, queries, values):
+    pair = pl.program_id(1)
+    group = q_ref.shape[1]
+    tiles = group // TILE
+    lane = lax.broadcasted_iota(jnp.int32, (group, 128), 1)
+
+    @pl.when(pair == 0)
+    def _():
+        keys[:, :128] = k_ref[0]
+        keys[:, 128:] = first_lane(lane)
+        for i in range(tiles):
+            j = max(0, i - SPAN)
+            wide = (i - j + 1) * TILE
+            column = lax.broadcasted_iota(jnp.int32, (TILE, wide), 1) + j * TILE
+            row = lax.broadcasted_iota(jnp.int32, (TILE, wide), 0) + i * TILE
+            allowed = (column <= row) & (column >= start_ref[0, i * TILE : (i + 1) * TILE, :])
+            mask[i * TILE : (i + 1) * TILE, :wide] = jnp.where(allowed, 1.0, 0.0)
+
+    query = q_ref[0].astype(F32)
+    value = v_ref[0].astype(F32)
+    for side in range(2):
+        queries[side, :, :128] = jnp.where(lane // FEAT == 2 * pair + side, query * 0.25, 0.0).astype(BF16)
+        queries[side, :, 128:] = first_lane(lane)
+        mine = lane // VD == side
+        values[side, :, :128] = jnp.where(mine, value, 0.0).astype(BF16)
+        values[side, :, 128:] = mine.astype(F32).astype(BF16)
+    for i in range(tiles):
+        j = max(0, i - SPAN)
+        wide = (i - j + 1) * TILE
+        here = slice(i * TILE, (i + 1) * TILE)
+        total = None
+        for side in range(2):
+            t = mm(queries[side, here], keys[j * TILE : (i + 1) * TILE], NT)
+            weights = ((t * t + 1.0) * mask[here, :wide]).astype(BF16)
+            part = mm(weights, values[side, j * TILE : (i + 1) * TILE])
+            total = part if total is None else total + part
+        inverse = 1.0 / total[:, 128:]
+        mix_ref[0, here, :] = (total[:, :128] * inverse).astype(BF16)
+        inv_ref[0, here, :] = inverse
+
+
+def lanes_at(group, column):
+    return pl.BlockSpec((1, group, 128), lambda m, p: (m, 0, column))
+
+
+def lanes_of_pair(group, first):
+    return pl.BlockSpec((1, group, 128), lambda m, p: (m, 0, first + p))
+
+
+def attend_all(qkv, starts):
+    micro, group, columns = qkv.shape
+    wide = columns - 256
+    pair = lanes_of_pair(group, 0)
+    return pl.pallas_call(
+        attend_kernel,
+        grid=(micro, wide // 128),
+        in_specs=[
+            lanes_at(group, 0),
+            lanes_at(group, 1),
+            lanes_of_pair(group, 2),
+            pl.BlockSpec((1, group, 1), lambda m, p: (m, 0, 0)),
+        ],
+        out_specs=[pair, pair],
+        out_shape=[
+            jax.ShapeDtypeStruct((micro, group, wide), BF16),
+            jax.ShapeDtypeStruct((micro, group, wide), F32),
+        ],
+        scratch_shapes=[
+            pltpu.VMEM((group, 256), BF16),
+            pltpu.VMEM((group, TILE * (SPAN + 1)), F32),
+            pltpu.VMEM((2, group, 256), BF16),
+            pltpu.VMEM((2, group, 256), BF16),
+        ],
+        compiler_params=params(),
+        name="attend",
+    )(qkv, qkv, qkv, starts)
+
+
+def attend_back_kernel(
+    q_ref, k_ref, v_ref, mix_ref, inv_ref, dmix_ref, start_ref, dq_ref, dk_ref, dv_ref,
+    keys, keys_t, mask, queries, values, douts, scaled_q, scaled_d, dk_sum, dq_t, scale,
+):
+    pair = pl.program_id(1)
+    group = q_ref.shape[1]
+    tiles = group // TILE
+    lane = lax.broadcasted_iota(jnp.int32, (group, 128), 1)
+
+    @pl.when(pair == 0)
+    def _():
+        keys[:, :128] = k_ref[0]
+        keys[:, 128:] = first_lane(lane)
+        keys_t[...] = k_ref[0].astype(F32).T.astype(BF16)
+        for j in range(tiles):
+            i = min(tiles, j + SPAN + 1)
+            wide = (i - j) * TILE
+            column = lax.broadcasted_iota(jnp.int32, (TILE, wide), 0) + j * TILE
+            row = lax.broadcasted_iota(jnp.int32, (TILE, wide), 1) + j * TILE
+            allowed = (column <= row) & (column >= start_ref[0, :, j * TILE : i * TILE])
+            mask[j * TILE : (j + 1) * TILE, :wide] = jnp.where(allowed, 1.0, 0.0)
+        dk_sum[...] = jnp.zeros_like(dk_sum)
+        scale[...] = jnp.zeros_like(scale)
+
+    query = q_ref[0].astype(F32)
+    dmix = dmix_ref[0].astype(F32)
+    inverse = inv_ref[0]
+    values[:, :128] = v_ref[0]
+    values[:, 128:] = (lane < 2).astype(F32).astype(BF16)
+    product = dmix * mix_ref[0].astype(F32)
+    for side in range(2):
+        mine = lane // VD == side
+        head = lane // FEAT == 2 * pair + side
+        masked = jnp.where(head, query, 0.0)
+        queries[side, :, :128] = (masked * 0.25).astype(BF16)
+        queries[side, :, 128:] = first_lane(lane)
+        delta = jnp.sum(jnp.where(mine, product, 0.0), axis=1, keepdims=True)
+        coarse = delta.astype(BF16).astype(F32)
+        douts[side, :, :128] = jnp.where(mine, dmix, 0.0).astype(BF16)
+        douts[side, :, 128:] = jnp.where(lane == 0, -coarse, jnp.where(lane == 1, coarse - delta, 0.0)).astype(BF16)
+        half_inverse = inverse[:, VD * side : VD * side + 1] * 0.5
+        scaled_q[side] = (masked * half_inverse).astype(BF16)
+        scaled_d[side] = jnp.where(mine, dmix * inverse, 0.0).astype(BF16)
+        scale[...] += jnp.where(head, half_inverse, 0.0)
+    for j in range(tiles):
+        i = min(tiles, j + SPAN + 1)
+        here = slice(j * TILE, (j + 1) * TILE)
+        below = slice(j * TILE, i * TILE)
+        allowed = mask[here, : (i - j) * TILE]
+        dv = None
+        dk = None
+        for side in range(2):
+            t = mm(keys[here], queries[side, below], NT)
+            slope = mm(values[here], douts[side, below], NT)
+            masked_t = t * allowed
+            d_t = (slope * masked_t).astype(BF16)
+            weights = (t * masked_t + allowed).astype(BF16)
+            dv_part = mm(weights, scaled_d[side, below])
+            dk_part = mm(d_t, scaled_q[side, below])
+            dv = dv_part if dv is None else dv + dv_part
+            dk = dk_part if dk is None else dk + dk_part
+            rows = pl.ds(pl.multiple_of((2 * pair + side) * FEAT, FEAT), FEAT)
+            dq_part = mm(keys_t[rows, here], d_t)
+            for r in range(j, i):
+                piece = dq_part[:, (r - j) * TILE : (r - j + 1) * TILE]
+                if j == max(0, r - SPAN):
+                    dq_t[rows, r * TILE : (r + 1) * TILE] = piece
+                else:
+                    dq_t[rows, r * TILE : (r + 1) * TILE] += piece
+        dv_ref[0, here, :] = dv.astype(BF16)
+        dk_sum[here] += dk
+
+    @pl.when(pair == pl.num_programs(1) - 1)
+    def _():
+        dk_ref[0] = dk_sum[...].astype(BF16)
+        dq_ref[0] = (dq_t[...].T * scale[...]).astype(BF16)
+
+
+def attend_back(qkv, mix, inverse, dmix, starts):
+    micro, group, columns = qkv.shape
+    wide = columns - 256
+    pair = lanes_of_pair(group, 0)
+    narrow = jax.ShapeDtypeStruct((micro, group, 128), BF16)
+    return pl.pallas_call(
+        attend_back_kernel,
+        grid=(micro, wide // 128),
+        in_specs=[
+            lanes_at(group, 0),
+            lanes_at(group, 1),
+            lanes_of_pair(group, 2),
+            pair,
+            pair,
+            pair,
+            pl.BlockSpec((1, 1, group), lambda m, p: (m, 0, 0)),
+        ],
+        out_specs=[lanes_at(group, 0), lanes_at(group, 0), pair],
+        out_shape=[narrow, narrow, jax.ShapeDtypeStruct((micro, group, wide), BF16)],
+        scratch_shapes=[
+            pltpu.VMEM((group, 256), BF16),
+            pltpu.VMEM((128, group), BF16),
+            pltpu.VMEM((group, TILE * (SPAN + 1)), F32),
+            pltpu.VMEM((2, group, 256), BF16),
+            pltpu.VMEM((group, 256), BF16),
+            pltpu.VMEM((2, group, 256), BF16),
+            pltpu.VMEM((2, group, 128), BF16),
+            pltpu.VMEM((2, group, 128), BF16),
+            pltpu.VMEM((group, 128), F32),
+            pltpu.VMEM((128, group), F32),
+            pltpu.VMEM((group, 128), F32),
+        ],
+        compiler_params=params(),
+        name="attend_back",
+    )(qkv, qkv, qkv, mix, inverse, dmix, starts)
+
+
+def out_kernel(micro, core, mix, *refs):
+    pieces, (own, other, slab, sems) = refs[:8], refs[8:]
+    i = pl.program_id(0)
+
+    @pl.when(i == 0)
+    def _():
+        place_slab(pieces, slab, sems)
+
+    put(i < micro, other, own, mm(mix[0], slab[...], NT).astype(BF16))
+
+
+def out_project(core, mix, pieces):
+    micro, group, wide = mix.shape
+    rows = group // 2
+    far, half, columns = pieces[0].shape
+    dim = far * half * 8
+    shape = jax.ShapeDtypeStruct((micro, rows, dim), BF16)
+    return rows_kernel(
+        functools.partial(out_kernel, micro),
+        "out_project",
+        core,
+        micro,
+        [group_block(wide, micro, rows)] + [anywhere()] * 8,
+        [own_block(dim, micro, rows), other_block(dim, micro, rows)],
+        [shape, shape],
+        [pltpu.VMEM((dim, columns), BF16), dma_sems(far)],
+        (mix, *pieces),
+    )
+
+
+def mid_kernel(x, own, got, gains, resid_out, h_out):
+    resid = x[0].astype(F32) + own[0].astype(F32) + got[0].astype(F32)
+    inverse = lax.rsqrt(jnp.mean(resid * resid, axis=-1, keepdims=True) + 1e-05)
+    resid_out[0] = resid.astype(BF16)
+    h_out[0] = (resid * inverse * gains[1:2]).astype(BF16)
+
+
+def local_call(kernel, name, arrays, gains, out_types):
+    micro, rows, dim = arrays[0].shape
+    tile = min(rows, 256)
+    block = pl.BlockSpec((1, tile, dim), lambda m, t: (m, t, 0))
+    return pl.pallas_call(
+        kernel,
+        grid=(micro, rows // tile),
+        in_specs=[block] * len(arrays) + [pl.BlockSpec((8, dim), lambda m, t: (0, 0))],
+        out_specs=[block] * len(out_types),
+        out_shape=[jax.ShapeDtypeStruct((micro, rows, dim), t) for t in out_types],
+        compiler_params=params(),
+        name=name,
+    )(*arrays, gains)
+
+
+def feed_kernel(micro, width, first, core, h_own, h_other, g_own, g_other, *refs):
+    if first:
+        before = None
+    else:
+        before, refs = refs[:4], refs[4:]
+    pieces, refs = refs[:8], refs[8:]
+    out_own, out_other, dm_own, dm_other = refs[:4]
+    grads, (slab, total, hidden_s, dgu_s, sems) = refs[4:11], refs[11:]
+    i = pl.program_id(0)
+    is_other = i < micro
+
+    @pl.when(i == 0)
+    def _():
+        place_slab(pieces, slab, sems)
+        total[...] = jnp.zeros_like(total)
+
+    w_gu = slab[:, : 2 * width]
+    w_down = slab[:, 2 * width :]
+    h = pick(is_other, h_other, h_own)
+    g = pick(is_other, g_other, g_own)
+    gate_up = mm(h, w_gu)
+    d_hidden = mm(g, w_down)
+    gate = gate_up[:, :width]
+    up = gate_up[:, width:]
+    sigmoid = 0.5 * jnp.tanh(0.5 * gate) + 0.5
+    silu = gate * sigmoid
+    hidden_s[...] = (silu * up).astype(BF16)
+    dgu_s[:, :width] = (d_hidden * up * (sigmoid + silu * (1.0 - sigmoid))).astype(BF16)
+    dgu_s[:, width:] = (d_hidden * silu).astype(BF16)
+    out = mm(hidden_s[...], w_down, NT)
+    dm = mm(dgu_s[...], w_gu, NT)
+    if not first:
+        out = out + pick(is_other, before[1], before[0]).astype(F32)
+        dm = dm + pick(is_other, before[3], before[2]).astype(F32)
+    put(is_other, out_other, out_own, out.astype(BF16))
+    put(is_other, dm_other, dm_own, dm.astype(BF16))
+    total[:, : 2 * width] += mm(h, dgu_s[...], TN)
+    total[:, 2 * width :] += mm(g, hidden_s[...], TN)
+
+    @pl.when(i == 2 * micro - 1)
+    def _():
+        split_grads(total, grads)
+
+
+def feed(core, h_own, h_other, g_own, g_other, before, pieces):
+    micro, rows, dim = h_own.shape
+    far, half, columns = pieces[0].shape
+    own = own_block(dim, micro, rows)
+    other = other_block(dim, micro, rows)
+    shape = jax.ShapeDtypeStruct((micro, rows, dim), BF16)
+    grads = grad_shapes(dim, columns)
+    first = before is None
+    results = rows_kernel(
+        functools.partial(feed_kernel, micro, columns // 3, first),
+        "feed",
+        core,
+        micro,
+        [own, other, own, other] + ([] if first else [own, other, own, other]) + [anywhere()] * 8,
+        [own, other, own, other] + grad_specs(grads),
+        [shape] * 4 + grads,
+        [
+            pltpu.VMEM((dim, columns), BF16),
+            pltpu.VMEM((dim, columns), F32),
+            pltpu.VMEM((rows, columns // 3), BF16),
+            pltpu.VMEM((rows, 2 * (columns // 3)), BF16),
+            dma_sems(far),
+        ],
+        (h_own, h_other, g_own, g_other) + (() if first else tuple(before)) + tuple(pieces),
+    )
+    return results[:4], results[4:]
+
+
+def back_mid_kernel(resid, own, got, g, gains, d_out):
+    res = resid[0].astype(F32)
+    inverse = lax.rsqrt(jnp.mean(res * res, axis=-1, keepdims=True) + 1e-05)
+    normed = res * inverse
+    scaled = (own[0].astype(F32) + got[0].astype(F32)) * gains[1:2]
+    slope = inverse * (scaled - normed * jnp.mean(scaled * normed, axis=-1, keepdims=True))
+    d_out[0] = (g[0].astype(F32) + slope).astype(BF16)
+
+
+def back_in_kernel(x, own, got, d, gains, grad_out):
+    values = x[0].astype(F32)
+    inverse = lax.rsqrt(jnp.mean(values * values, axis=-1, keepdims=True) + 1e-05)
+    normed = values * inverse
+    scaled = (own[0].astype(F32) + got[0].astype(F32)) * gains[0:1]
+    slope = inverse * (scaled - normed * jnp.mean(scaled * normed, axis=-1, keepdims=True))
+    grad_out[0] = d[0].astype(F32) + slope
+
+
+def back_out_kernel(micro, core, d_own, d_other, mix, *refs):
+    pieces, dmix, grads, (slab, total, sems) = refs[:8], refs[8], refs[9:16], refs[16:]
+    i = pl.program_id(0)
+
+    @pl.when(i == 0)
+    def _():
+        place_slab(pieces, slab, sems)
+        total[...] = jnp.zeros_like(total)
+
+    d = pick(i < micro, d_other, d_own)
+    dmix[0] = mm(d, slab[...]).astype(BF16)
+    total[...] += mm(d, mix[0], TN)
+
+    @pl.when(i == 2 * micro - 1)
+    def _():
+        split_grads(total, grads)
+
+
+def back_out(core, d_own, d_other, mix, pieces):
+    micro, rows, dim = d_own.shape
+    far, half, columns = pieces[0].shape
+    grads = grad_shapes(dim, columns)
+    results = rows_kernel(
+        functools.partial(back_out_kernel, micro),
+        "back_out",
+        core,
+        micro,
+        [own_block(dim, micro, rows), other_block(dim, micro, rows), group_block(columns, micro, rows)]
+        + [anywhere()] * 8,
+        [group_block(columns, micro, rows)] + grad_specs(grads),
+        [jax.ShapeDtypeStruct((micro, 2 * rows, columns), BF16)] + grads,
+        [pltpu.VMEM((dim, columns), BF16), pltpu.VMEM((dim, columns), F32), dma_sems(far)],
+        (d_own, d_other, mix, *pieces),
+    )
+    return results[0], results[1:]
+
+
+def grad_qkv_kernel(micro, core, h, dq, dk, dv, *refs):
+    grads, total = refs[:7], refs[7]
+    i = pl.program_id(0)
+
+    @pl.when(i == 0)
+    def _():
+        total[...] = jnp.zeros_like(total)
+
+    total[...] += mm(h[0], jnp.concatenate([dq[0], dk[0], dv[0]], 1), TN)
+
+    @pl.when(i == 2 * micro - 1)
+    def _():
+        split_grads(total, grads)
+
+
+def grad_qkv(core, h, dq, dk, dv):
+    micro, group, dim = h.shape
+    rows = group // 2
+    widths = [dq.shape[2], dk.shape[2], dv.shape[2]]
+    grads = grad_shapes(dim, sum(widths))
+    return rows_kernel(
+        functools.partial(grad_qkv_kernel, micro),
+        "grad_qkv",
+        core,
+        micro,
+        [group_block(w, micro, rows) for w in [dim] + widths],
+        grad_specs(grads),
+        grads,
+        [pltpu.VMEM((dim, sum(widths)), F32)],
+        (h, dq, dk, dv),
+    )
+
+
+def back_in_project_kernel(micro, core, dq, dk, dv, *refs):
+    pieces, (own, other, slab, sems) = refs[:8], refs[8:]
+    i = pl.program_id(0)
+
+    @pl.when(i == 0)
+    def _():
+        place_slab(pieces, slab, sems)
+
+    d = jnp.concatenate([dq[0], dk[0], dv[0]], 1)
+    put(i < micro, other, own, mm(d, slab[:, : d.shape[1]], NT).astype(BF16))
+
+
+def back_in_project(core, dq, dk, dv, pieces):
+    micro, group, _ = dq.shape
+    rows = group // 2
+    far, half, columns = pieces[0].shape
+    dim = far * half * 8
+    shape = jax.ShapeDtypeStruct((micro, rows, dim), BF16)
+    return rows_kernel(
+        functools.partial(back_in_project_kernel, micro),
+        "back_in_project",
+        core,
+        micro,
+        [group_block(a.shape[2], micro, rows) for a in (dq, dk, dv)] + [anywhere()] * 8,
+        [own_block(dim, micro, rows), other_block(dim, micro, rows)],
+        [shape, shape],
+        [pltpu.VMEM((dim, columns), BF16), dma_sems(far)],
+        (dq, dk, dv, *pieces),
+    )
+
+
+def fused_body(
+    inputs, gain_attn, gain_mlp, w_query, w_key, w_value, w_out, w_gate, w_up, w_down, out_grad, lengths
+):
+    micro, rows, dim = inputs.shape
+    group = rows * lax.axis_size("tensor")
+    core = lax.axis_index("tensor").astype(jnp.int32).reshape(1)
+    each = w_query.shape[0]
+    units = w_gate.shape[1]
+
+    gain_rows = jnp.stack([gain_attn, gain_mlp])
+    gain_part = jnp.pad(jnp.concatenate([gain_rows, gain_rows], 1), ((0, each - 2), (0, 0)))
+    slab_in = jnp.concatenate([w_query, w_key, w_value, gain_part], 1)
+    widths_in = (w_query.shape[1], w_key.shape[1], w_value.shape[1])
+    slab_out = w_out.T
+    down_t = w_down.T
+    padded = -(-units // 128) * 128
+    edges = [(at, min(at + CHUNK, padded)) for at in range(0, padded, CHUNK)]
+    slabs = []
+    for low, high in edges:
+        parts = [a[:, low : min(high, units)] for a in (w_gate, w_up, down_t)]
+        slabs.append(jnp.concatenate([jnp.pad(a, ((0, 0), (0, high - low - a.shape[1]))) for a in parts], 1))
+
+    ends = jnp.cumsum(lengths[:, 0], axis=-1)
+    places = jnp.arange(group, dtype=jnp.int32)
+    starts = jnp.max(jnp.where(places[None, :, None] >= ends[:, None, :], ends[:, None, :], 0), axis=-1)
+
+    x_other = swap(inputs)
+    pieces_in = gather_slab(slab_in)
+    g_other = swap(out_grad)
+    pieces_out = gather_slab(slab_out)
+    pieces_feed = [gather_slab(s) for s in slabs]
+
+    h_in, qkv, gains = project(core, inputs, x_other, pieces_in, sum(widths_in))
+    mix, inverse = attend_all(qkv, starts.reshape(micro, group, 1))
+    part_own, part_other = out_project(core, mix, pieces_out)
+    resid, h_own = local_call(mid_kernel, "mid", [inputs, part_own, swap(part_other)], gains, [BF16, BF16])
+    h_other = swap(h_own)
+
+    sums = None
+    feed_grads = []
+    for pieces in pieces_feed:
+        sums, grads = feed(core, h_own, h_other, out_grad, g_other, sums, pieces)
+        feed_grads.append(scatter_grads(grads))
+    out_own, out_other, dm_own, dm_other = sums
+    (d_own,) = local_call(back_mid_kernel, "back_mid", [resid, dm_own, swap(dm_other), out_grad], gains, [BF16])
+    mixed_out = add(resid, out_own, swap(out_other)).astype(BF16)
+    dmix, grads = back_out(core, d_own, swap(d_own), mix, pieces_out)
+    grad_out_t = scatter_grads(grads)
+    dq, dk, dv = attend_back(qkv, mix, inverse, dmix, starts.reshape(micro, 1, group))
+    grad_in = scatter_grads(grad_qkv(core, h_in, dq, dk, dv))
+    din_own, din_other = back_in_project(core, dq, dk, dv, pieces_in)
+    (input_grad,) = local_call(
+        back_in_kernel, "back_in", [inputs, din_own, swap(din_other), d_own], gains, [F32]
+    )
+
+    def columns_of(at):
+        kept = []
+        for (low, high), grad in zip(edges, feed_grads):
+            kept.append(grad[:, at * (high - low) : at * (high - low) + min(high, units) - low])
+        return jnp.concatenate(kept, 1)
+
+    grad_gate, grad_up, grad_down_t = columns_of(0), columns_of(1), columns_of(2)
+    from_in = jnp.sum(slab_in[:, : sum(widths_in)].astype(F32) * grad_in, axis=1)
+    from_mid = jnp.sum(w_gate.astype(F32) * grad_gate + w_up.astype(F32) * grad_up, axis=1)
+    both = jnp.stack([from_in / gain_attn.astype(F32), from_mid / gain_mlp.astype(F32)])
+    both = both + swap(both)
+    at_key = widths_in[0]
+    at_value = widths_in[0] + widths_in[1]
+    return (
+        mixed_out,
+        input_grad,
+        both[0],
+        both[1],
+        grad_in[:, :at_key],
+        grad_in[:, at_key:at_value],
+        grad_in[:, at_value:],
+        grad_out_t.T,
+        grad_gate,
+        grad_up,
+        grad_down_t.T,
+    )
+
+
 def solution(mesh):
     in_specs = (
         P(None, ("dp", "tensor"), None),
@@ -357,4 +1102,6 @@
         P("dp", "tensor"),
         P("tensor", "dp"),
     )
-    return jax.shard_map(body, mesh=mesh, in_specs=in_specs, out_specs=out_specs, check_vma=False)
+    fits = mesh.shape["tensor"] == 2 and mesh.shape["dp"] % 4 == 0
+    chosen = fused_body if fits else plain_body
+    return jax.shard_map(chosen, mesh=mesh, in_specs=in_specs, out_specs=out_specs, check_vma=False)

time: 2340 us -> 639 us (0.27)
  matrix products: 675 us -> 0 us
  other arithmetic: 505 us -> 32.1 us
  waiting for transfers between devices: 545 us -> 161 us
  local copies, waits for them, and re-layouts: 356 us -> 26.9 us
  Pallas kernels: 0 us -> 293 us
  blocking collectives: 165 us -> 0 us
  starting transfers between devices: 3.61 us -> 114 us
  loops' own time: 52.9 us -> 0 us
    dot_general x171 -> x0, matrix products: 675 us -> none  [the longest x24 208 us: attend_block(): jnp.einsum('hrc,chv->rhv', weights, values_in, precision=EXACT)]
    reduce_scatter x19 -> x0, waiting for transfers between devices: 321 us -> none  [the longest x1 75.1 us: body(): lax.psum_scatter(grad_out_sum.astype(jnp.bfloat16), 'dp', scatter_dimensi...]
    pallas_call x0 -> x13, Pallas kernels: none -> 293 us  [the longest x8 183 us: rows_kernel(): pl.pallas_call(kernel, grid_spec=pltpu.PrefetchScalarGridSpec(num_scalar_...]
    all_gather x17 -> x0, waiting for transfers between devices: 217 us -> none  [the longest x1 70.2 us: fetch_weights(): lax.all_gather(w_down, 'dp', axis=1, tiled=True)]
    scatter-add x12 -> x0, other arithmetic: 213 us -> none  [taylor(): second = jnp.take(outer, flat_index, axis=-1) * factors]
    ppermute x0 -> x99, waiting for transfers between devices: none -> 161 us  [the longest x90 161 us: exchange(): return lax.ppermute(value, 'dp', [(i, i ^ bit) for i in range(count)])]
    ppermute x0 -> x99, starting transfers between devices: none -> 114 us  [the longest x90 113 us: exchange(): return lax.ppermute(value, 'dp', [(i, i ^ bit) for i in range(count)])]
    reduce_sum x26 -> x2, other arithmetic: 112 us -> 1.19 us  [the longest x1 1.03 us: fused_body(): jnp.sum(w_gate.astype(F32) * grad_gate + w_up.astype(F32) * grad_up, axis=1)]
  transfers between devices with their start and end apart: 36 -> 99, of which waited for: 17 -> 37; matrix products, arithmetic and copies ran while one was open for 63% -> 8% of each run, Pallas kernels for 0% -> 39%
where the time goes in v1:
time: 639 us; the launch traced here: 629 us
  Pallas kernels  293 us (46%)
  waiting for transfers between devices  161 us (25%)
  starting transfers between devices  114 us (18%)
  other arithmetic  32.1 us (5%)
  local copies, waits for them, and re-layouts  26.9 us (4%)
    pallas_call x8, Pallas kernels, rows_kernel(): pl.pallas_call(kernel, grid_spec=pltpu.PrefetchScalarGridSpec(num_scalar_...  183 us
    ppermute x90, waiting for transfers between devices, exchange(): return lax.ppermute(value, 'dp', [(i, i ^ bit) for i in range(count)])  161 us
    ppermute x90, starting transfers between devices, exchange(): return lax.ppermute(value, 'dp', [(i, i ^ bit) for i in range(count)])  113 us
    pallas_call x1, Pallas kernels, attend_back(): pl.pallas_call(attend_back_kernel, grid=(micro, wide // 128), in_specs=[l...  57.3 us
    pallas_call x1, Pallas kernels, attend_all(): pl.pallas_call(attend_kernel, grid=(micro, wide // 128), in_specs=[lanes_...  26.6 us
    pallas_call x3, Pallas kernels, local_call(): pl.pallas_call(kernel, grid=(micro, rows // tile), in_specs=[block] * len...  26.5 us
    another operation x20, local copies, waits for them, and re-layouts, gather_slab(): lower = jnp.stack([s[half:] for s in line])  13.3 us
  transfers between devices with their start and end apart: 99, of which 37 were waited for; matrix products, arithmetic and copies ran while one was open for 8% of the time, Pallas kernels for 39%

profile of v1, /device:TPU:0, one launch (start us, length us, event | category | flops | bytes accessed | tf_op | source)
XLA Modules:
  0.0 629.1 jit_solution(636797576022287563)
XLA Ops:
  2.3 3.1 collective-permute-start.1
  15.4 3.5 collective-permute-start.11
  19.0 3.8 collective-permute-done.11
  22.8 3.1 collective-permute-start.12
  25.9 3.2 collective-permute-done.12
  44.7 3.3 collective-permute-done.4.refs_2_
  59.3 12.3 %project.1 = (bf16[3,1024,1024]{2,1,0:T(8,128)(2,1)}, bf16[3,1024,768]{2,1,0:T(8,128)(2,1)}, f32[8,1024]{1,0:T(8,128)}) custom-call(s32[1]{0:T(128)} %bitcast.core, bf16[3,512,1024]{2,1,0:T(8,128)(2,1)} %x.11, bf16[3,512,1024]{2,1,0:T(8,128)(2,1)} %copy-done.3, bf16[4,32,896]{2,1,0:T(8,128)(2,1)} %copy-done.5, bf16[4,32,896]{2,1,0:T(8,128)(2,1)} %copy-done.6, ...), custom_call_target="tpu_custom_call" | custom-call | tf_op jit(solution)/shard_map/project/pallas_call | solution.py:469
  71.7 26.6 %attend.1 = (bf16[3,1024,512]{2,1,0:T(8,128)(2,1)}, f32[3,1024,512]{2,1,0:T(8,128)}) custom-call(bf16[3,1024,768]{2,1,0:T(8,128)(2,1)} %get-tuple-element.73.q_ref.k_ref.v_ref, bf16[3,1024,768]{2,1,0:T(8,128)(2,1)} %get-tuple-element.73.q_ref.k_ref.v_ref, bf16[3,1024,768]{2,1,0:T(8,128)(2,1)} %get-tuple-element.73.q_ref.k_ref.v_ref, ...), custom_call_target="tpu_custom_call" | custom-call | tf_op jit(solution)/shard_map/attend/pallas_call | solution.py:611
  102.8 10.4 %out_project.1 = (bf16[3,512,1024]{2,1,0:T(8,128)(2,1)}, bf16[3,512,1024]{2,1,0:T(8,128)(2,1)}) custom-call(s32[1]{0:T(128)} %bitcast.core, bf16[3,1024,512]{2,1,0:T(8,128)(2,1)} %get-tuple-element.74.mix.mix_ref, bf16[4,32,512]{2,1,0:T(8,128)(2,1)} %copy-done.11, bf16[4,32,512]{2,1,0:T(8,128)(2,1)} %pad_maximum_fusion.22.refs_1_, ...), custom_call_target="tpu_custom_call" | custom-call | tf_op jit(solution)/shard_map/out_project/pallas_call | solution.py:469
  114.2 7.6 %collective-permute-done.41 = bf16[64,1152]{1,0:T(8,128)(2,1)} collective-permute-done((bf16[64,1152]{1,0:T(8,128)(2,1)}, bf16[64,1152]{1,0:T(8,128)(2,1)}, u32[]{:S(2)}, u32[]{:S(2)}) %collective-permute-start.41) | collective-permute-done | bytes 147488 | tf_op jit(solution)/shard_map/ppermute | solution.py:360
  123.1 7.4 %collective-permute-done.42 = bf16[64,1152]{1,0:T(8,128)(2,1)S(1)} collective-permute-done((bf16[64,1152]{1,0:T(8,128)(2,1)}, bf16[64,1152]{1,0:T(8,128)(2,1)S(1)}, u32[]{:S(2)}, u32[]{:S(2)}) %collective-permute-start.42) | collective-permute-done | bytes 147488 | tf_op jit(solution)/shard_map/ppermute | solution.py:360
  135.2 4.3 collective-permute-start.33
  142.6 8.1 %mid.1 = (bf16[3,512,1024]{2,1,0:T(8,128)(2,1)}, bf16[3,512,1024]{2,1,0:T(8,128)(2,1)}) custom-call(bf16[3,512,1024]{2,1,0:T(8,128)(2,1)} %x.11, bf16[3,512,1024]{2,1,0:T(8,128)(2,1)} %get-tuple-element.75.own, bf16[3,512,1024]{2,1,0:T(8,128)(2,1)} %collective-permute-done.19.got, f32[8,1024]{1,0:T(8,128)} %get-tuple-element.77.gains), custom_call_target="tpu_custom_call" | custom-call | tf_op jit(solution)/shard_map/mid/pallas_call | solution.py:792
  158.5 3.7 collective-permute-done.44.refs_7_
  163.0 3.1 collective-permute-done.27.refs_4_
  167.3 3.2 collective-permute-done.26.refs_3_
  171.7 6.6 %collective-permute-done.25.refs_2_ = bf16[4,32,1536]{2,1,0:T(8,128)(2,1)S(1)} collective-permute-done((bf16[4,32,1536]{2,1,0:T(8,128)(2,1)S(1)}, bf16[4,32,1536]{2,1,0:T(8,128)(2,1)S(1)}, u32[]{:S(2)}, u32[]{:S(2)}) %collective-permute-start.25) | collective-permute-done | bytes 393248 | tf_op jit(solution)/shard_map/ppermute | solution.py:360
  180.3 4.4 collective-permute-done.36.refs_8_
  185.9 4.6 collective-permute-done.35.refs_7_
  191.2 7.7 %collective-permute-done.34.refs_6_ = bf16[4,32,1536]{2,1,0:T(8,128)(2,1)} collective-permute-done((bf16[4,32,1536]{2,1,0:T(8,128)(2,1)S(1)}, bf16[4,32,1536]{2,1,0:T(8,128)(2,1)}, u32[]{:S(2)}, u32[]{:S(2)}) %collective-permute-start.34) | collective-permute-done | bytes 393248 | tf_op jit(solution)/shard_map/ppermute | solution.py:360
  200.8 6.4 %collective-permute-done.29.refs_6_ = bf16[4,32,1536]{2,1,0:T(8,128)(2,1)S(1)} collective-permute-done((bf16[4,32,1536]{2,1,0:T(8,128)(2,1)S(1)}, bf16[4,32,1536]{2,1,0:T(8,128)(2,1)S(1)}, u32[]{:S(2)}, u32[]{:S(2)}) %collective-permute-start.29) | collective-permute-done | bytes 393248 | tf_op jit(solution)/shard_map/ppermute | solution.py:360
  209.1 6.5 %collective-permute-done.38.refs_10_ = bf16[4,32,1536]{2,1,0:T(8,128)(2,1)S(1)} collective-permute-done((bf16[4,32,1536]{2,1,0:T(8,128)(2,1)S(1)}, bf16[4,32,1536]{2,1,0:T(8,128)(2,1)S(1)}, u32[]{:S(2)}, u32[]{:S(2)}) %collective-permute-start.38) | collective-permute-done | bytes 393248 | tf_op jit(solution)/shard_map/ppermute | solution.py:360
  218.6 42.2 %feed.3 = (bf16[3,512,1024]{2,1,0:T(8,128)(2,1)}, bf16[3,512,1024]{2,1,0:T(8,128)(2,1)}, bf16[3,512,1024]{2,1,0:T(8,128)(2,1)}, bf16[3,512,1024]{2,1,0:T(8,128)(...) custom-call(s32[1]{0:T(128)} %bitcast.core, ...), custom_call_target="tpu_custom_call" | custom-call | tf_op jit(solution)/shard_map/feed/pallas_call | solution.py:469
  260.8 43.7 %feed.4 = (bf16[3,512,1024]{2,1,0:T(8,128)(2,1)}, bf16[3,512,1024]{2,1,0:T(8,128)(2,1)}, bf16[3,512,1024]{2,1,0:T(8,128)(2,1)}, bf16[3,512,1024]{2,1,0:T(8,128)(...) custom-call(s32[1]{0:T(128)} %bitcast.core, ...), custom_call_target="tpu_custom_call" | custom-call | tf_op jit(solution)/shard_map/feed/pallas_call | solution.py:469
  305.4 38.2 %feed.5 = (bf16[3,512,1024]{2,1,0:T(8,128)(2,1)}, bf16[3,512,1024]{2,1,0:T(8,128)(2,1)}, bf16[3,512,1024]{2,1,0:T(8,128)(2,1)}, bf16[3,512,1024]{2,1,0:T(8,128)(...) custom-call(s32[1]{0:T(128)} %bitcast.core, ...), custom_call_target="tpu_custom_call" | custom-call | tf_op jit(solution)/shard_map/feed/pallas_call | solution.py:469
  349.5 4.3 collective-permute-done.81
  356.0 7.9 %collective-permute-done.83 = bf16[4,32,1152]{2,1,0:T(8,128)(2,1)S(1)} collective-permute-done((bf16[4,32,1152]{2,1,0:T(8,128)(2,1)}, bf16[4,32,1152]{2,1,0:T(8,128)(2,1)S(1)}, u32[]{:S(2)}, u32[]{:S(2)}) %collective-permute-start.83) | collective-permute-done | bytes 294944 | tf_op jit(solution)/shard_map/ppermute | solution.py:360
  368.6 9.0 %collective-permute-done.72 = bf16[4,32,1536]{2,1,0:T(8,128)(2,1)S(1)} collective-permute-done((bf16[4,32,1536]{2,1,0:T(8,128)(2,1)S(1)}, bf16[4,32,1536]{2,1,0:T(8,128)(2,1)S(1)}, u32[]{:S(2)}, u32[]{:S(2)}) %collective-permute-start.72) | collective-permute-done | bytes 393248 | tf_op jit(solution)/shard_map/ppermute | solution.py:360
  380.7 3.6 collective-permute-done.82
  385.6 5.3 collective-permute-done.84
  391.8 3.9 collective-permute-start.88
  398.9 2.8 collective-permute-done.87
  405.8 10.1 %collective-permute-done.64 = bf16[4,32,1536]{2,1,0:T(8,128)(2,1)S(1)} collective-permute-done((bf16[4,32,1536]{2,1,0:T(8,128)(2,1)S(1)}, bf16[4,32,1536]{2,1,0:T(8,128)(2,1)S(1)}, u32[]{:S(2)}, u32[]{:S(2)}) %collective-permute-start.64) | collective-permute-done | bytes 393248 | tf_op jit(solution)/shard_map/ppermute | solution.py:360
  417.3 6.3 %collective-permute-done.66 = bf16[4,32,1536]{2,1,0:T(8,128)(2,1)S(1)} collective-permute-done((bf16[4,32,1536]{2,1,0:T(8,128)(2,1)S(1)}, bf16[4,32,1536]{2,1,0:T(8,128)(2,1)S(1)}, u32[]{:S(2)}, u32[]{:S(2)}) %collective-permute-start.66) | collective-permute-done | bytes 393248 | tf_op jit(solution)/shard_map/ppermute | solution.py:360
  434.0 8.8 %back_mid.1.d_own.d = bf16[3,512,1024]{2,1,0:T(8,128)(2,1)} custom-call(bf16[3,512,1024]{2,1,0:T(8,128)(2,1)} %get-tuple-element.78.resid, bf16[3,512,1024]{2,1,0:T(8,128)(2,1)} %get-tuple-element.91.own, bf16[3,512,1024]{2,1,0:T(8,128)(2,1)} %copy-done.4, bf16[3,512,1024]{2,1,0:T(8,128)(2,1)} %g.1, f32[8,1024]{1,0:T(8,128)} %get-tuple-element.77.gains), custom_call_target="tpu_custom_call" | custom-call | tf_op jit(solution)/shard_map/back_mid/pallas_call | solution.py:792
  455.5 5.2 collective-permute-done.77
  460.7 6.3 %collective-permute-done.78 = bf16[64,1536]{1,0:T(8,128)(2,1)S(1)} collective-permute-done((bf16[64,1536]{1,0:T(8,128)(2,1)S(1)}, bf16[64,1536]{1,0:T(8,128)(2,1)S(1)}, u32[]{:S(2)}, u32[]{:S(2)}) %collective-permute-start.78) | collective-permute-done | bytes 196640 | tf_op jit(solution)/shard_map/ppermute | solution.py:360
  469.5 13.6 %back_out.1 = (bf16[3,1024,512]{2,1,0:T(8,128)(2,1)}, bf16[4,64,512]{2,1,0:T(8,128)(2,1)}, bf16[4,32,512]{2,1,0:T(8,128)(2,1)}, bf16[4,32,512]{2,1,0:T(8,128)(2,...) custom-call(s32[1]{0:T(128)} %bitcast.core, ...), custom_call_target="tpu_custom_call" | custom-call | tf_op jit(solution)/shard_map/back_out/pallas_call | solution.py:469
  484.4 6.8 %add_convert_fusion = bf16[3,512,1024]{2,1,0:T(8,128)(2,1)} fusion(bf16[3,512,1024]{2,1,0:T(8,128)(2,1)} %collective-permute-done.49, bf16[3,512,1024]{2,1,0:T(8,128)(2,1)} %get-tuple-element.88, bf16[3,512,1024]{2,1,0:T(8,128)(2,1)S(1)} %copy-done.1), kind=kLoop, calls=%fused_computation | loop fusion | flops 9437184 | bytes 12582912 | tf_op jit(solution)/shard_map/convert_element_type | solution.py:1039
  494.1 57.3 %attend_back.1 = (bf16[3,1024,128]{2,1,0:T(8,128)(2,1)}, bf16[3,1024,128]{2,1,0:T(8,128)(2,1)}, bf16[3,1024,512]{2,1,0:T(8,128)(2,1)}) custom-call(bf16[3,1024,768]{2,1,0:T(8,128)(2,1)} %get-tuple-element.73.q_ref.k_ref.v_ref, bf16[3,1024,768]{2,1,0:T(8,128)(2,1)} %get-tuple-element.73.q_ref.k_ref.v_ref, ...), custom_call_target="tpu_custom_call" | custom-call | tf_op jit(solution)/shard_map/attend_back/pallas_call | solution.py:719
  551.4 10.5 %grad_qkv.1 = (bf16[4,64,768]{2,1,0:T(8,128)(2,1)}, bf16[4,32,768]{2,1,0:T(8,128)(2,1)}, bf16[4,32,768]{2,1,0:T(8,128)(2,1)}, bf16[4,32,768]{2,1,0:T(8,128)(2,1)...) custom-call(s32[1]{0:T(128)} %bitcast.core, ...), custom_call_target="tpu_custom_call" | custom-call | tf_op jit(solution)/shard_map/grad_qkv/pallas_call | solution.py:469
  563.3 12.0 %back_in_project.1 = (bf16[3,512,1024]{2,1,0:T(8,128)(2,1)}, bf16[3,512,1024]{2,1,0:T(8,128)(2,1)}) custom-call(s32[1]{0:T(128)} %bitcast.core, bf16[3,1024,128]{2,1,0:T(8,128)(2,1)} %get-tuple-element.94.dq, bf16[3,1024,128]{2,1,0:T(8,128)(2,1)} %get-tuple-element.95.dk, bf16[3,1024,512]{2,1,0:T(8,128)(2,1)} %get-tuple-element.96.dv, ...), custom_call_target="tpu_custom_call" | custom-call | tf_op jit(solution)/shard_map/back_in_project/pallas_call | solution.py:469
  578.5 5.1 collective-permute-done.56
  585.8 2.8 collective-permute-done.92
  595.9 4.4 collective-permute-start.96
  606.2 2.9 collective-permute-done.97
  612.0 3.5 collective-permute-done.61
  619.3 9.6 %back_in.1 = f32[3,512,1024]{2,1,0:T(8,128)} custom-call(bf16[3,512,1024]{2,1,0:T(8,128)(2,1)} %x.11, bf16[3,512,1024]{2,1,0:T(8,128)(2,1)} %get-tuple-element.97.own, bf16[3,512,1024]{2,1,0:T(8,128)(2,1)} %copy-done.2, bf16[3,512,1024]{2,1,0:T(8,128)(2,1)} %back_mid.1.d_own.d, f32[8,1024]{1,0:T(8,128)} %get-tuple-element.77.gains), custom_call_target="tpu_custom_call" | custom-call | tf_op jit(solution)/shard_map/back_in/pallas_call | solution.py:792
  (409 shorter events, 157.8 us)
Async XLA Ops:
  2.3 29.2 %collective-permute-start.1 = (bf16[64,896]{1,0:T(8,128)(2,1)S(1)}, bf16[64,896]{1,0:T(8,128)(2,1)S(1)}, u32[]{:S(2)}, u32[]{:S(2)}) collective-permute-start(bf16[64,896]{1,0:T(8,128)(2,1)S(1)} %pad_maximum_fusion.23), channel_id=1, source_target_pairs={{0,8},{2,10},{4,12},{6,14},{8,0},{10,2},{12,4},{14,6},{16,24},{18,... | collective-permute-start | bytes 344072 | tf_op jit(solution)/shard_map/ppermute | solution.py:360
  5.4 27.6 %collective-permute-start.2 = (bf16[64,896]{1,0:T(8,128)(2,1)S(1)}, bf16[64,896]{1,0:T(8,128)(2,1)S(1)}, u32[]{:S(2)}, u32[]{:S(2)}) collective-permute-start(bf16[64,896]{1,0:T(8,128)(2,1)S(1)} %pad_maximum_fusion.23), channel_id=1, source_target_pairs={{0,16},{2,18},{4,20},{6,22},{8,24},{10,26},{12,28},{14,30},{16,0},... | collective-permute-start | bytes 344072 | tf_op jit(solution)/shard_map/ppermute | solution.py:360
  8.0 25.1 %collective-permute-start.3 = (bf16[64,896]{1,0:T(8,128)(2,1)S(1)}, bf16[64,896]{1,0:T(8,128)(2,1)S(1)}, u32[]{:S(2)}, u32[]{:S(2)}) collective-permute-start(bf16[64,896]{1,0:T(8,128)(2,1)S(1)} %pad_maximum_fusion.23), channel_id=1, source_target_pairs={{0,24},{2,26},{4,28},{6,30},{8,16},{10,18},{12,20},{14,22},{16,8},... | collective-permute-start | bytes 344072 | tf_op jit(solution)/shard_map/ppermute | solution.py:360
  8.0 46.2 %collective-permute-start = (bf16[3,512,1024]{2,1,0:T(8,128)(2,1)}, bf16[3,512,1024]{2,1,0:T(8,128)(2,1)S(1)}, u32[]{:S(2)}, u32[]{:S(2)}) collective-permute-start(bf16[3,512,1024]{2,1,0:T(8,128)(2,1)} %x.11), channel_id=1, source_target_pairs={{0,1},{1,0},{2,3},{3,2},{4,5},{5,4},{6,7},{7,6},{8,9},{9,8},{10,11... | collective-permute-start | bytes 9437192 | tf_op jit(solution)/shard_map/ppermute | solution.py:364
  48.0 65.2 %collective-permute-start.40 = (bf16[64,1152]{1,0:T(8,128)(2,1)}, bf16[64,1152]{1,0:T(8,128)(2,1)}, u32[]{:S(2)}, u32[]{:S(2)}) collective-permute-start(bf16[64,1152]{1,0:T(8,128)(2,1)} %fusion.13), channel_id=1, source_target_pairs={{0,8},{2,10},{4,12},{6,14},{8,0},{10,2},{12,4},{14,6},{16,24},{18,... | collective-permute-start | bytes 442376 | tf_op jit(solution)/shard_map/ppermute | solution.py:360
  48.0 50.3 %collective-permute-start.13 = (bf16[4,32,512]{2,1,0:T(8,128)(2,1)S(1)}, bf16[4,32,512]{2,1,0:T(8,128)(2,1)}, u32[]{:S(2)}, u32[]{:S(2)}) collective-permute-start(bf16[4,32,512]{2,1,0:T(8,128)(2,1)S(1)} %pad_maximum_fusion.21.refs_0_), channel_id=1, source_target_pairs={{0,2},{2,0},{4,6},{6,4},{8,10},{10,8},{12,14},{14,12},{16,18},{18,... | collective-permute-start | bytes 393224 | tf_op jit(solution)/shard_map/ppermute | solution.py:360
  52.1 46.3 %collective-permute-start.16 = (bf16[4,32,512]{2,1,0:T(8,128)(2,1)}, bf16[4,32,512]{2,1,0:T(8,128)(2,1)}, u32[]{:S(2)}, u32[]{:S(2)}) collective-permute-start(bf16[4,32,512]{2,1,0:T(8,128)(2,1)} %pad_maximum_fusion.22.refs_1_), channel_id=1, source_target_pairs={{0,4},{2,6},{4,0},{6,2},{8,12},{10,14},{12,8},{14,10},{16,20},{18,... | collective-permute-start | bytes 393224 | tf_op jit(solution)/shard_map/ppermute | solution.py:360
  53.2 47.4 %collective-permute-start.17 = (bf16[4,32,512]{2,1,0:T(8,128)(2,1)}, bf16[4,32,512]{2,1,0:T(8,128)(2,1)}, u32[]{:S(2)}, u32[]{:S(2)}) collective-permute-start(bf16[4,32,512]{2,1,0:T(8,128)(2,1)} %collective-permute-done.15.refs_4_), channel_id=1, source_target_pairs={{0,2},{2,0},{4,6},{6,4},{8,10},{10,8},{12,14},{14,12},{16,18},{18,... | collective-permute-start | bytes 393224 | tf_op jit(solution)/shard_map/ppermute | solution.py:360
  54.2 48.6 %collective-permute-start.18 = (bf16[4,32,512]{2,1,0:T(8,128)(2,1)}, bf16[4,32,512]{2,1,0:T(8,128)(2,1)}, u32[]{:S(2)}, u32[]{:S(2)}) collective-permute-start(bf16[4,32,512]{2,1,0:T(8,128)(2,1)} %collective-permute-done.14.refs_3_), channel_id=1, source_target_pairs={{0,4},{2,6},{4,0},{6,2},{8,12},{10,14},{12,8},{14,10},{16,20},{18,... | collective-permute-start | bytes 393224 | tf_op jit(solution)/shard_map/ppermute | solution.py:360
  98.3 33.8 %collective-permute-start.22 = (bf16[64,1536]{1,0:T(8,128)(2,1)S(1)}, bf16[64,1536]{1,0:T(8,128)(2,1)S(1)}, u32[]{:S(2)}, u32[]{:S(2)}) collective-permute-start(bf16[64,1536]{1,0:T(8,128)(2,1)S(1)} %copy-done.19), channel_id=1, source_target_pairs={{0,8},{2,10},{4,12},{6,14},{8,0},{10,2},{12,4},{14,6},{16,24},{18,... | collective-permute-start | bytes 589832 | tf_op jit(solution)/shard_map/ppermute | solution.py:360
  98.4 36.1 %collective-permute-start.23 = (bf16[64,1536]{1,0:T(8,128)(2,1)S(1)}, bf16[64,1536]{1,0:T(8,128)(2,1)S(1)}, u32[]{:S(2)}, u32[]{:S(2)}) collective-permute-start(bf16[64,1536]{1,0:T(8,128)(2,1)S(1)} %copy-done.19), channel_id=1, source_target_pairs={{0,16},{2,18},{4,20},{6,22},{8,24},{10,26},{12,28},{14,30},{16,0},... | collective-permute-start | bytes 589832 | tf_op jit(solution)/shard_map/ppermute | solution.py:360
  100.6 40.4 %collective-permute-start.24 = (bf16[64,1536]{1,0:T(8,128)(2,1)S(1)}, bf16[64,1536]{1,0:T(8,128)(2,1)S(1)}, u32[]{:S(2)}, u32[]{:S(2)}) collective-permute-start(bf16[64,1536]{1,0:T(8,128)(2,1)S(1)} %copy-done.19), channel_id=1, source_target_pairs={{0,24},{2,26},{4,28},{6,30},{8,16},{10,18},{12,20},{14,22},{16,8},... | collective-permute-start | bytes 589832 | tf_op jit(solution)/shard_map/ppermute | solution.py:360
  102.8 19.0 %collective-permute-start.41 = (bf16[64,1152]{1,0:T(8,128)(2,1)}, bf16[64,1152]{1,0:T(8,128)(2,1)}, u32[]{:S(2)}, u32[]{:S(2)}) collective-permute-start(bf16[64,1152]{1,0:T(8,128)(2,1)} %fusion.13), channel_id=1, source_target_pairs={{0,16},{2,18},{4,20},{6,22},{8,24},{10,26},{12,28},{14,30},{16,0},... | collective-permute-start | bytes 442376 | tf_op jit(solution)/shard_map/ppermute | solution.py:360
  113.2 28.5 %collective-permute-start.19 = (bf16[3,512,1024]{2,1,0:T(8,128)(2,1)}, bf16[3,512,1024]{2,1,0:T(8,128)(2,1)}, u32[]{:S(2)}, u32[]{:S(2)}) collective-permute-start(bf16[3,512,1024]{2,1,0:T(8,128)(2,1)} %get-tuple-element.76), channel_id=1, source_target_pairs={{0,1},{1,0},{2,3},{3,2},{4,5},{5,4},{6,7},{7,6},{8,9},{9,8},{10,11... | collective-permute-start | bytes 9437192 | tf_op jit(solution)/shard_map/ppermute | solution.py:364
  130.5 20.2 %collective-permute-start.31 = (bf16[64,1536]{1,0:T(8,128)(2,1)}, bf16[64,1536]{1,0:T(8,128)(2,1)}, u32[]{:S(2)}, u32[]{:S(2)}) collective-permute-start(bf16[64,1536]{1,0:T(8,128)(2,1)} %pad_maximum_fusion.11), channel_id=1, source_target_pairs={{0,8},{2,10},{4,12},{6,14},{8,0},{10,2},{12,4},{14,6},{16,24},{18,... | collective-permute-start | bytes 589832 | tf_op jit(solution)/shard_map/ppermute | solution.py:360
  132.8 19.2 %collective-permute-start.32 = (bf16[64,1536]{1,0:T(8,128)(2,1)}, bf16[64,1536]{1,0:T(8,128)(2,1)}, u32[]{:S(2)}, u32[]{:S(2)}) collective-permute-start(bf16[64,1536]{1,0:T(8,128)(2,1)} %pad_maximum_fusion.11), channel_id=1, source_target_pairs={{0,16},{2,18},{4,20},{6,22},{8,24},{10,26},{12,28},{14,30},{16,0},... | collective-permute-start | bytes 589832 | tf_op jit(solution)/shard_map/ppermute | solution.py:360
  135.2 19.9 %collective-permute-start.33 = (bf16[64,1536]{1,0:T(8,128)(2,1)}, bf16[64,1536]{1,0:T(8,128)(2,1)}, u32[]{:S(2)}, u32[]{:S(2)}) collective-permute-start(bf16[64,1536]{1,0:T(8,128)(2,1)} %pad_maximum_fusion.11), channel_id=1, source_target_pairs={{0,24},{2,26},{4,28},{6,30},{8,16},{10,18},{12,20},{14,22},{16,8},... | collective-permute-start | bytes 589832 | tf_op jit(solution)/shard_map/ppermute | solution.py:360
  141.0 75.7 %collective-permute-start.21 = (bf16[3,512,1024]{2,1,0:T(8,128)(2,1)S(1)}, bf16[3,512,1024]{2,1,0:T(8,128)(2,1)}, u32[]{:S(2)}, u32[]{:S(2)}) collective-permute-start(bf16[3,512,1024]{2,1,0:T(8,128)(2,1)S(1)} %copy-done), channel_id=1, source_target_pairs={{0,1},{1,0},{2,3},{3,2},{4,5},{5,4},{6,7},{7,6},{8,9},{9,8},{10,11... | collective-permute-start | bytes 9437192 | tf_op jit(solution)/shard_map/ppermute | solution.py:364
  150.7 66.8 %collective-permute-start.20 = (bf16[3,512,1024]{2,1,0:T(8,128)(2,1)}, bf16[3,512,1024]{2,1,0:T(8,128)(2,1)}, u32[]{:S(2)}, u32[]{:S(2)}) collective-permute-start(bf16[3,512,1024]{2,1,0:T(8,128)(2,1)} %get-tuple-element.79.h_own), channel_id=1, source_target_pairs={{0,1},{1,0},{2,3},{3,2},{4,5},{5,4},{6,7},{7,6},{8,9},{9,8},{10,11... | collective-permute-start | bytes 9437192 | tf_op jit(solution)/shard_map/ppermute | solution.py:364
  179.1 19.8 %collective-permute-start.34 = (bf16[4,32,1536]{2,1,0:T(8,128)(2,1)S(1)}, bf16[4,32,1536]{2,1,0:T(8,128)(2,1)}, u32[]{:S(2)}, u32[]{:S(2)}) collective-permute-start(bf16[4,32,1536]{2,1,0:T(8,128)(2,1)S(1)} %pad_maximum_fusion.2.refs_4_), channel_id=1, source_target_pairs={{0,2},{2,0},{4,6},{6,4},{8,10},{10,8},{12,14},{14,12},{16,18},{18,... | collective-permute-start | bytes 1179656 | tf_op jit(solution)/shard_map/ppermute | solution.py:360
  190.5 16.7 %collective-permute-start.29 = (bf16[4,32,1536]{2,1,0:T(8,128)(2,1)S(1)}, bf16[4,32,1536]{2,1,0:T(8,128)(2,1)S(1)}, u32[]{:S(2)}, u32[]{:S(2)}) collective-permute-start(bf16[4,32,1536]{2,1,0:T(8,128)(2,1)S(1)} %collective-permute-done.27.refs_4_), channel_id=1, source_target_pairs={{0,2},{2,0},{4,6},{6,4},{8,10},{10,8},{12,14},{14,12},{16,18},{18,... | collective-permute-start | bytes 1179656 | tf_op jit(solution)/shard_map/ppermute | solution.py:360
  207.2 53.6 %collective-permute-start.39 = (bf16[4,32,1536]{2,1,0:T(8,128)(2,1)}, bf16[4,32,1536]{2,1,0:T(8,128)(2,1)}, u32[]{:S(2)}, u32[]{:S(2)}) collective-permute-start(bf16[4,32,1536]{2,1,0:T(8,128)(2,1)} %collective-permute-done.35.refs_7_), channel_id=1, source_target_pairs={{0,4},{2,6},{4,0},{6,2},{8,12},{10,14},{12,8},{14,10},{16,20},{18,... | collective-permute-start | bytes 1179656 | tf_op jit(solution)/shard_map/ppermute | solution.py:360
  208.4 96.2 %collective-permute-start.43 = (bf16[4,32,1152]{2,1,0:T(8,128)(2,1)}, bf16[4,32,1152]{2,1,0:T(8,128)(2,1)}, u32[]{:S(2)}, u32[]{:S(2)}) collective-permute-start(bf16[4,32,1152]{2,1,0:T(8,128)(2,1)} %pad_maximum_fusion.6.refs_4_), channel_id=1, source_target_pairs={{0,2},{2,0},{4,6},{6,4},{8,10},{10,8},{12,14},{14,12},{16,18},{18,... | collective-permute-start | bytes 884744 | tf_op jit(solution)/shard_map/ppermute | solution.py:360
  215.7 88.9 %collective-permute-start.46 = (bf16[4,32,1152]{2,1,0:T(8,128)(2,1)}, bf16[4,32,1152]{2,1,0:T(8,128)(2,1)}, u32[]{:S(2)}, u32[]{:S(2)}) collective-permute-start(bf16[4,32,1152]{2,1,0:T(8,128)(2,1)} %pad_maximum_fusion.7.refs_5_), channel_id=1, source_target_pairs={{0,4},{2,6},{4,0},{6,2},{8,12},{10,14},{12,8},{14,10},{16,20},{18,... | collective-permute-start | bytes 884744 | tf_op jit(solution)/shard_map/ppermute | solution.py:360
  216.8 87.8 %collective-permute-start.47 = (bf16[4,32,1152]{2,1,0:T(8,128)(2,1)}, bf16[4,32,1152]{2,1,0:T(8,128)(2,1)S(1)}, u32[]{:S(2)}, u32[]{:S(2)}) collective-permute-start(bf16[4,32,1152]{2,1,0:T(8,128)(2,1)} %collective-permute-done.45.refs_8_), channel_id=1, source_target_pairs={{0,2},{2,0},{4,6},{6,4},{8,10},{10,8},{12,14},{14,12},{16,18},{18,... | collective-permute-start | bytes 884744 | tf_op jit(solution)/shard_map/ppermute | solution.py:360
  217.7 86.9 %collective-permute-start.48 = (bf16[4,32,1152]{2,1,0:T(8,128)(2,1)}, bf16[4,32,1152]{2,1,0:T(8,128)(2,1)S(1)}, u32[]{:S(2)}, u32[]{:S(2)}) collective-permute-start(bf16[4,32,1152]{2,1,0:T(8,128)(2,1)} %collective-permute-done.44.refs_7_), channel_id=1, source_target_pairs={{0,4},{2,6},{4,0},{6,2},{8,12},{10,14},{12,8},{14,10},{16,20},{18,... | collective-permute-start | bytes 884744 | tf_op jit(solution)/shard_map/ppermute | solution.py:360
  345.5 20.6 %collective-permute-start.63 = (bf16[4,32,1536]{2,1,0:T(8,128)(2,1)S(1)}, bf16[4,32,1536]{2,1,0:T(8,128)(2,1)S(1)}, u32[]{:S(2)}, u32[]{:S(2)}) collective-permute-start(bf16[4,32,1536]{2,1,0:T(8,128)(2,1)S(1)} %copy-done.72), channel_id=1, source_target_pairs={{0,2},{2,0},{4,6},{6,4},{8,10},{10,8},{12,14},{14,12},{16,18},{18,... | collective-permute-start | bytes 1179656 | tf_op jit(solution)/shard_map/ppermute | solution.py:360
  346.3 58.5 %collective-permute-start.62 = (bf16[4,32,1536]{2,1,0:T(8,128)(2,1)}, bf16[4,32,1536]{2,1,0:T(8,128)(2,1)S(1)}, u32[]{:S(2)}, u32[]{:S(2)}) collective-permute-start(bf16[4,32,1536]{2,1,0:T(8,128)(2,1)} %get-tuple-element.108), channel_id=1, source_target_pairs={{0,2},{2,0},{4,6},{6,4},{8,10},{10,8},{12,14},{14,12},{16,18},{18,... | collective-permute-start | bytes 1179656 | tf_op jit(solution)/shard_map/ppermute | solution.py:360
  347.6 19.9 %collective-permute-start.65 = (bf16[4,32,1536]{2,1,0:T(8,128)(2,1)S(1)}, bf16[4,32,1536]{2,1,0:T(8,128)(2,1)S(1)}, u32[]{:S(2)}, u32[]{:S(2)}) collective-permute-start(bf16[4,32,1536]{2,1,0:T(8,128)(2,1)S(1)} %copy-done.71), channel_id=1, source_target_pairs={{0,4},{2,6},{4,0},{6,2},{8,12},{10,14},{12,8},{14,10},{16,20},{18,... | collective-permute-start | bytes 1179656 | tf_op jit(solution)/shard_map/ppermute | solution.py:360
  348.7 28.8 %collective-permute-start.72 = (bf16[4,32,1536]{2,1,0:T(8,128)(2,1)S(1)}, bf16[4,32,1536]{2,1,0:T(8,128)(2,1)S(1)}, u32[]{:S(2)}, u32[]{:S(2)}) collective-permute-start(bf16[4,32,1536]{2,1,0:T(8,128)(2,1)S(1)} %copy-done.73), channel_id=1, source_target_pairs={{0,2},{2,0},{4,6},{6,4},{8,10},{10,8},{12,14},{14,12},{16,18},{18,... | collective-permute-start | bytes 1179656 | tf_op jit(solution)/shard_map/ppermute | solution.py:360
  363.9 27.9 %collective-permute-start.74 = (bf16[4,32,1536]{2,1,0:T(8,128)(2,1)S(1)}, bf16[4,32,1536]{2,1,0:T(8,128)(2,1)S(1)}, u32[]{:S(2)}, u32[]{:S(2)}) collective-permute-start(bf16[4,32,1536]{2,1,0:T(8,128)(2,1)S(1)} %copy-done.70), channel_id=1, source_target_pairs={{0,4},{2,6},{4,0},{6,2},{8,12},{10,14},{12,8},{14,10},{16,20},{18,... | collective-permute-start | bytes 1179656 | tf_op jit(solution)/shard_map/ppermute | solution.py:360
  367.5 18.1 %collective-permute-start.85 = (bf16[4,32,1152]{2,1,0:T(8,128)(2,1)}, bf16[4,32,1152]{2,1,0:T(8,128)(2,1)S(1)}, u32[]{:S(2)}, u32[]{:S(2)}) collective-permute-start(bf16[4,32,1152]{2,1,0:T(8,128)(2,1)} %get-tuple-element.127), channel_id=1, source_target_pairs={{0,4},{2,6},{4,0},{6,2},{8,12},{10,14},{12,8},{14,10},{16,20},{18,... | collective-permute-start | bytes 884744 | tf_op jit(solution)/shard_map/ppermute | solution.py:360
  380.7 51.6 %collective-permute-start.50 = (bf16[3,512,1024]{2,1,0:T(8,128)(2,1)S(1)}, bf16[3,512,1024]{2,1,0:T(8,128)(2,1)S(1)}, u32[]{:S(2)}, u32[]{:S(2)}) collective-permute-start(bf16[3,512,1024]{2,1,0:T(8,128)(2,1)S(1)} %copy-done.67), channel_id=1, source_target_pairs={{0,1},{1,0},{2,3},{3,2},{4,5},{5,4},{6,7},{7,6},{8,9},{9,8},{10,11... | collective-permute-start | bytes 9437192 | tf_op jit(solution)/shard_map/ppermute | solution.py:364
  397.8 19.5 %collective-permute-start.67 = (bf16[4,32,1536]{2,1,0:T(8,128)(2,1)S(1)}, bf16[4,32,1536]{2,1,0:T(8,128)(2,1)S(1)}, u32[]{:S(2)}, u32[]{:S(2)}) collective-permute-start(bf16[4,32,1536]{2,1,0:T(8,128)(2,1)S(1)} %copy-done.69), channel_id=1, source_target_pairs={{0,4},{2,6},{4,0},{6,2},{8,12},{10,14},{12,8},{14,10},{16,20},{18,... | collective-permute-start | bytes 1179656 | tf_op jit(solution)/shard_map/ppermute | solution.py:360
  401.7 26.0 %collective-permute-start.71 = (bf16[4,32,1536]{2,1,0:T(8,128)(2,1)S(1)}, bf16[4,32,1536]{2,1,0:T(8,128)(2,1)S(1)}, u32[]{:S(2)}, u32[]{:S(2)}) collective-permute-start(bf16[4,32,1536]{2,1,0:T(8,128)(2,1)S(1)} %copy-done.68), channel_id=1, source_target_pairs={{0,2},{2,0},{4,6},{6,4},{8,10},{10,8},{12,14},{14,12},{16,18},{18,... | collective-permute-start | bytes 1179656 | tf_op jit(solution)/shard_map/ppermute | solution.py:360
  404.9 38.0 %collective-permute-start.76 = (bf16[4,32,1536]{2,1,0:T(8,128)(2,1)}, bf16[4,32,1536]{2,1,0:T(8,128)(2,1)}, u32[]{:S(2)}, u32[]{:S(2)}) collective-permute-start(bf16[4,32,1536]{2,1,0:T(8,128)(2,1)} %get-tuple-element.120), channel_id=1, source_target_pairs={{0,4},{2,6},{4,0},{6,2},{8,12},{10,14},{12,8},{14,10},{16,20},{18,... | collective-permute-start | bytes 1179656 | tf_op jit(solution)/shard_map/ppermute | solution.py:360
  417.3 67.2 %collective-permute-start.49 = (bf16[3,512,1024]{2,1,0:T(8,128)(2,1)}, bf16[3,512,1024]{2,1,0:T(8,128)(2,1)}, u32[]{:S(2)}, u32[]{:S(2)}) collective-permute-start(bf16[3,512,1024]{2,1,0:T(8,128)(2,1)} %get-tuple-element.89), channel_id=1, source_target_pairs={{0,1},{1,0},{2,3},{3,2},{4,5},{5,4},{6,7},{7,6},{8,9},{9,8},{10,11... | collective-permute-start | bytes 9437192 | tf_op jit(solution)/shard_map/ppermute | solution.py:364
  427.7 17.9 %collective-permute-start.75 = (bf16[4,32,1536]{2,1,0:T(8,128)(2,1)}, bf16[4,32,1536]{2,1,0:T(8,128)(2,1)}, u32[]{:S(2)}, u32[]{:S(2)}) collective-permute-start(bf16[4,32,1536]{2,1,0:T(8,128)(2,1)} %add_convert_fusion.1), channel_id=1, source_target_pairs={{0,2},{2,0},{4,6},{6,4},{8,10},{10,8},{12,14},{14,12},{16,18},{18,... | collective-permute-start | bytes 1179656 | tf_op jit(solution)/shard_map/ppermute | solution.py:360
  431.4 18.4 %collective-permute-start.68 = (bf16[64,1536]{1,0:T(8,128)(2,1)}, bf16[64,1536]{1,0:T(8,128)(2,1)}, u32[]{:S(2)}, u32[]{:S(2)}) collective-permute-start(bf16[64,1536]{1,0:T(8,128)(2,1)} %pad_maximum_fusion.12), channel_id=1, source_target_pairs={{0,8},{2,10},{4,12},{6,14},{8,0},{10,2},{12,4},{14,6},{16,24},{18,... | collective-permute-start | bytes 589832 | tf_op jit(solution)/shard_map/ppermute | solution.py:360
  432.3 17.5 %collective-permute-start.69 = (bf16[64,1536]{1,0:T(8,128)(2,1)}, bf16[64,1536]{1,0:T(8,128)(2,1)}, u32[]{:S(2)}, u32[]{:S(2)}) collective-permute-start(bf16[64,1536]{1,0:T(8,128)(2,1)} %pad_maximum_fusion.13), channel_id=1, source_target_pairs={{0,16},{2,18},{4,20},{6,22},{8,24},{10,26},{12,28},{14,30},{16,0},... | collective-permute-start | bytes 589832 | tf_op jit(solution)/shard_map/ppermute | solution.py:360
  445.6 24.0 %collective-permute-start.51 = (bf16[3,512,1024]{2,1,0:T(8,128)(2,1)}, bf16[3,512,1024]{2,1,0:T(8,128)(2,1)}, u32[]{:S(2)}, u32[]{:S(2)}) collective-permute-start(bf16[3,512,1024]{2,1,0:T(8,128)(2,1)} %back_mid.1.d_own.d), channel_id=1, source_target_pairs={{0,1},{1,0},{2,3},{3,2},{4,5},{5,4},{6,7},{7,6},{8,9},{9,8},{10,11... | collective-permute-start | bytes 9437192 | tf_op jit(solution)/shard_map/ppermute | solution.py:364
  449.9 17.1 %collective-permute-start.78 = (bf16[64,1536]{1,0:T(8,128)(2,1)S(1)}, bf16[64,1536]{1,0:T(8,128)(2,1)S(1)}, u32[]{:S(2)}, u32[]{:S(2)}) collective-permute-start(bf16[64,1536]{1,0:T(8,128)(2,1)S(1)} %pad_maximum_fusion.16), channel_id=1, source_target_pairs={{0,16},{2,18},{4,20},{6,22},{8,24},{10,26},{12,28},{14,30},{16,0},... | collective-permute-start | bytes 589832 | tf_op jit(solution)/shard_map/ppermute | solution.py:360
  483.1 92.2 %collective-permute-start.91 = (bf16[4,32,512]{2,1,0:T(8,128)(2,1)}, bf16[4,32,512]{2,1,0:T(8,128)(2,1)}, u32[]{:S(2)}, u32[]{:S(2)}) collective-permute-start(bf16[4,32,512]{2,1,0:T(8,128)(2,1)} %get-tuple-element.131), channel_id=1, source_target_pairs={{0,2},{2,0},{4,6},{6,4},{8,10},{10,8},{12,14},{14,12},{16,18},{18,... | collective-permute-start | bytes 393224 | tf_op jit(solution)/shard_map/ppermute | solution.py:360
  491.3 93.6 %collective-permute-start.90 = (bf16[4,32,512]{2,1,0:T(8,128)(2,1)}, bf16[4,32,512]{2,1,0:T(8,128)(2,1)}, u32[]{:S(2)}, u32[]{:S(2)}) collective-permute-start(bf16[4,32,512]{2,1,0:T(8,128)(2,1)} %get-tuple-element.129), channel_id=1, source_target_pairs={{0,2},{2,0},{4,6},{6,4},{8,10},{10,8},{12,14},{14,12},{16,18},{18,... | collective-permute-start | bytes 393224 | tf_op jit(solution)/shard_map/ppermute | solution.py:360
  492.1 85.0 %collective-permute-start.93 = (bf16[4,32,512]{2,1,0:T(8,128)(2,1)}, bf16[4,32,512]{2,1,0:T(8,128)(2,1)S(1)}, u32[]{:S(2)}, u32[]{:S(2)}) collective-permute-start(bf16[4,32,512]{2,1,0:T(8,128)(2,1)} %get-tuple-element.133), channel_id=1, source_target_pairs={{0,4},{2,6},{4,0},{6,2},{8,12},{10,14},{12,8},{14,10},{16,20},{18,... | collective-permute-start | bytes 393224 | tf_op jit(solution)/shard_map/ppermute | solution.py:360
  493.2 97.8 %collective-permute-start.95 = (bf16[4,32,512]{2,1,0:T(8,128)(2,1)}, bf16[4,32,512]{2,1,0:T(8,128)(2,1)S(1)}, u32[]{:S(2)}, u32[]{:S(2)}) collective-permute-start(bf16[4,32,512]{2,1,0:T(8,128)(2,1)} %get-tuple-element.134), channel_id=1, source_target_pairs={{0,4},{2,6},{4,0},{6,2},{8,12},{10,14},{12,8},{14,10},{16,20},{18,... | collective-permute-start | bytes 393224 | tf_op jit(solution)/shard_map/ppermute | solution.py:360
  575.3 20.5 %collective-permute-start.53 = (bf16[4,32,768]{2,1,0:T(8,128)(2,1)}, bf16[4,32,768]{2,1,0:T(8,128)(2,1)S(1)}, u32[]{:S(2)}, u32[]{:S(2)}) collective-permute-start(bf16[4,32,768]{2,1,0:T(8,128)(2,1)} %get-tuple-element.101), channel_id=1, source_target_pairs={{0,2},{2,0},{4,6},{6,4},{8,10},{10,8},{12,14},{14,12},{16,18},{18,... | collective-permute-start | bytes 589832 | tf_op jit(solution)/shard_map/ppermute | solution.py:360
  578.4 39.3 %collective-permute-start.52 = (bf16[3,512,1024]{2,1,0:T(8,128)(2,1)}, bf16[3,512,1024]{2,1,0:T(8,128)(2,1)S(1)}, u32[]{:S(2)}, u32[]{:S(2)}) collective-permute-start(bf16[3,512,1024]{2,1,0:T(8,128)(2,1)} %get-tuple-element.98), channel_id=1, source_target_pairs={{0,1},{1,0},{2,3},{3,2},{4,5},{5,4},{6,7},{7,6},{8,9},{9,8},{10,11... | collective-permute-start | bytes 9437192 | tf_op jit(solution)/shard_map/ppermute | solution.py:364
  (125 other events, 2492.0 us)

commit v2 on v0

--- a/solution.py
+++ b/solution.py
@@ -1,9 +1,12 @@
+import functools
 import math
 
 import jax
 import jax.numpy as jnp
 import numpy as np
 from jax import lax
+from jax.experimental import pallas as pl
+from jax.experimental.pallas import tpu as pltpu
 from jax.sharding import PartitionSpec as P
 
 FEAT = 16
@@ -122,7 +125,7 @@
     return tuple(row_parts) + tuple(col_parts)
 
 
-def body(
+def plain_body(
     inputs,
     gain_attn,
     gain_mlp,
@@ -329,6 +332,1435 @@
     )
 
 
+F32 = jnp.float32
+BF16 = jnp.bfloat16
+NN = (((1,), (0,)), ((), ()))
+NT = (((1,), (1,)), ((), ()))
+TN = (((0,), (0,)), ((), ()))
+TILE = 256
+SPAN = 2
+CHUNK = 512
+UNIT = 1536
+EARLY = 640
+JOBS = ((), ((0, 768), (0, 384), (1, 768)), ((1, 384),), ((1, 384), (2, 768), (2, 768)))
+RATE = 0.019
+VMEM_BYTES = 62 << 20
+MESH = pl.DeviceIdType.MESH
+
+
+def mm(left, right, dims=NN):
+    return lax.dot_general(left, right, dims, preferred_element_type=F32)
+
+
+def params(number=None):
+    if number is None:
+        return pltpu.CompilerParams(vmem_limit_bytes=VMEM_BYTES)
+    return pltpu.CompilerParams(vmem_limit_bytes=VMEM_BYTES, collective_id=number, has_side_effects=True)
+
+
+def anywhere():
+    return pl.BlockSpec(memory_space=pl.ANY)
+
+
+def once(shape):
+    return pl.BlockSpec(shape, lambda *_: (0,) * len(shape), pipeline_mode=pl.Buffered(1))
+
+
+def far_count():
+    return lax.axis_size("dp") // 4
+
+
+def dp_peer(bits):
+    return {"dp": lax.axis_index("dp") ^ bits}
+
+
+def sibling():
+    return {"tensor": 1 - lax.axis_index("tensor")}
+
+
+def dp_peers():
+    return [dp_peer(1), dp_peer(2)] + [dp_peer(4 * k) for k in range(1, far_count())]
+
+
+def greet(peers):
+    barrier = pltpu.get_barrier_semaphore()
+    for peer in peers:
+        pl.semaphore_signal(barrier, inc=1, device_id=peer, device_id_type=MESH)
+    pl.semaphore_wait(barrier, len(peers))
+
+
+def remote(source, target, send, recv, peer):
+    return pltpu.make_async_remote_copy(
+        src_ref=source, dst_ref=target, send_sem=send, recv_sem=recv, device_id=peer, device_id_type=MESH
+    )
+
+
+def gather_sems():
+    count = 7 * far_count() - 1
+    return [pltpu.SemaphoreType.DMA((count,)), pltpu.SemaphoreType.DMA((count,)), pltpu.SemaphoreType.DMA]
+
+
+class Gather:
+    def __init__(self, source, whole, send, recv, local=None):
+        self.source, self.whole, self.send, self.recv, self.local = source, whole, send, recv, local
+        self.me = lax.axis_index("dp")
+        self.far = far_count()
+        self.each = whole.shape[0] // lax.axis_size("dp")
+        self.half = self.each // 2
+
+    def block(self, bits):
+        start = pl.multiple_of((self.me ^ bits) * self.each, self.each)
+        return self.whole.at[pl.ds(start, self.each)]
+
+    def piece(self, bits, part):
+        start = pl.multiple_of((self.me ^ bits) * self.each + part * self.half, self.half)
+        return self.whole.at[pl.ds(start, self.half)]
+
+
+    def along(self, k):
+        return k - 1, self.source, self.block(0), 4 * k, self.block(4 * k)
+
+    def first(self, k, part, bit):
+        index = self.far - 1 + 4 * k + 2 * part + bit - 1
+        if k == 0:
+            source = self.source.at[pl.ds(part * self.half, self.half)]
+        else:
+            source = self.piece(4 * k, part)
+        return index, source, self.piece(4 * k, part), bit, self.piece(4 * k + bit, part)
+
+    def second(self, k, part):
+        index = 5 * self.far - 1 + 2 * k + part
+        source = self.piece(4 * k + 2 - part, part)
+        return index, source, source, 1 + part, self.piece(4 * k + 3, part)
+
+    def outgoing(self, transfer):
+        index, source, target, bits, _ = transfer
+        return remote(source, target, self.send.at[index], self.recv.at[index], dp_peer(bits))
+
+    def start(self, transfer):
+        self.outgoing(transfer).start()
+
+    def sent(self, transfer):
+        self.outgoing(transfer).wait_send()
+
+    def arrived(self, transfer):
+        index, _, _, bits, landing = transfer
+        remote(landing, landing, self.send.at[index], self.recv.at[index], dp_peer(bits)).wait_recv()
+
+    def kept(self):
+        return pltpu.make_async_copy(self.source, self.block(0), self.local)
+
+    def pass_on(self, k):
+        for part, bit in ((0, 2), (1, 1), (0, 1), (1, 2)):
+            self.start(self.first(k, part, bit))
+
+    def begin(self):
+        if self.local is not None:
+            self.kept().start()
+        for k in range(1, self.far):
+            self.start(self.along(k))
+        self.pass_on(0)
+
+    def spread(self, k):
+        self.arrived(self.along(k))
+        self.pass_on(k)
+
+    def turn(self, k):
+        self.arrived(self.first(k, 0, 2))
+        self.start(self.second(k, 0))
+        self.arrived(self.first(k, 1, 1))
+        self.start(self.second(k, 1))
+
+    def finish(self):
+        for k in range(self.far):
+            self.arrived(self.first(k, 0, 1))
+            self.arrived(self.first(k, 1, 2))
+            for part in range(2):
+                self.arrived(self.second(k, part))
+        for k in range(1, self.far):
+            self.sent(self.along(k))
+        for k in range(self.far):
+            for part in range(2):
+                for bit in (1, 2):
+                    self.sent(self.first(k, part, bit))
+                self.sent(self.second(k, part))
+        if self.local is not None:
+            self.kept().wait()
+
+    def plan(self, start):
+        along = RATE * self.whole.shape[1]
+        far = 2 * along / 3
+        events = [(start, self.begin)]
+        for k in range(1, self.far):
+            at = start + 3.0 + far * (0.4 + 0.6 * k / (self.far - 1))
+            events.append((at, functools.partial(self.spread, k)))
+        for k in range(self.far):
+            at = start + 6.0 + far * (0.4 + 0.6 * k / (self.far - 1)) + along / 4
+            events.append((at, functools.partial(self.turn, k)))
+        return events
+
+
+class Plan:
+
+    def __init__(self, step, steps, places, step_us):
+        self.step, self.steps, self.places, self.step_us = step, steps, places, step_us
+        self.events = {}
+        self.ends = []
+
+    def add(self, events, end):
+        for time, action in events:
+            index = min(int(time * self.places / self.step_us), self.steps * self.places - 1)
+            self.events.setdefault(divmod(index, self.places), []).append((time, action))
+        self.ends.append(end)
+
+    def at(self, place):
+        for key in sorted(self.events):
+            if key[1] == place:
+
+                @pl.when(self.step == key[0])
+                def _(actions=sorted(self.events[key], key=lambda event: event[0])):
+                    for _, action in actions:
+                        action()
+
+    def finish(self):
+        for end in self.ends:
+            end()
+
+
+def add_gathers(plan, jobs, refs, start=0.0):
+    for at, (source, whole, first, target, width) in enumerate(jobs):
+        gather = Gather(
+            source.at[:, pl.ds(first, width)], whole.at[:, pl.ds(target, width)], *refs[3 * at : 3 * at + 3]
+        )
+        plan.add(gather.plan(start), gather.finish)
+        start += RATE * width
+
+
+def pieces_of(width, most):
+    return [(at, min(most, width - at)) for at in range(0, width, most)]
+
+
+def scatter_scratch(columns, dim):
+    far = far_count()
+    half = dim // lax.axis_size("dp") // 2
+    part = pltpu.VMEM((far, half, columns), BF16)
+    return [part] * 8 + [
+        pltpu.VMEM((far, 2, half, columns), BF16),
+        pltpu.VMEM((far - 1, 2, half, columns), BF16),
+        pltpu.SemaphoreType.DMA((5 + far,)),
+        pltpu.SemaphoreType.DMA((5 + far,)),
+        pltpu.SemaphoreType.DMA((3,)),
+    ]
+
+
+SCATTER_REFS = 13
+
+
+class Scatter:
+    def __init__(self, grads, first, out, refs):
+        (
+            self.mine_y, self.mine_x, self.got_dy, self.got_dx, self.got_x, self.got_y, self.got_y2, self.got_x2,
+            self.mine, self.got_far, self.send, self.recv, self.local,
+        ) = refs
+        self.grads, self.out = grads, out
+        self.columns = pl.ds(first, self.mine.shape[3])
+        me = lax.axis_index("dp")
+        self.far = far_count()
+        self.low, self.high = lax.rem(me, 4), lax.div(me, 4)
+
+    def copy(self, index, source, target, bits):
+        return remote(source, target, self.send.at[index], self.recv.at[index], dp_peer(bits))
+
+    def share(self, bits, part):
+        return self.grads.at[:, self.low ^ bits, part, :, self.columns]
+
+    def from_grads(self):
+        return [
+            self.copy(0, self.share(3, 0), self.got_dy, 1),
+            self.copy(1, self.share(3, 1), self.got_dx, 2),
+            self.copy(2, self.share(1, 0), self.got_x, 1),
+            self.copy(3, self.share(2, 1), self.got_y, 2),
+        ]
+
+    def added(self):
+        return [self.copy(4, self.mine_y, self.got_y2, 2), self.copy(5, self.mine_x, self.got_x2, 1)]
+
+    def along(self):
+        return [
+            self.copy(5 + k, self.mine.at[self.high ^ k], self.got_far.at[k - 1], 4 * k) for k in range(1, self.far)
+        ]
+
+    def loads(self):
+        own = self.grads.at[:, self.low, :, :, self.columns]
+        return [
+            pltpu.make_async_copy(self.share(2, 0), self.mine_y, self.local.at[0]),
+            pltpu.make_async_copy(self.share(1, 1), self.mine_x, self.local.at[1]),
+            pltpu.make_async_copy(own, self.mine, self.local.at[2]),
+        ]
+
+    def begin(self):
+        for copy in self.from_grads() + self.loads():
+            copy.start()
+
+    def second(self):
+        loads, got, added = self.loads(), self.from_grads(), self.added()
+        loads[0].wait()
+        got[0].wait_recv()
+        self.mine_y[...] = add(self.mine_y[...], self.got_dy[...]).astype(BF16)
+        added[0].start()
+        loads[1].wait()
+        got[1].wait_recv()
+        self.mine_x[...] = add(self.mine_x[...], self.got_dx[...]).astype(BF16)
+        added[1].start()
+
+    def third(self):
+        got, added = self.from_grads(), self.added()
+        self.loads()[2].wait()
+        got[2].wait_recv()
+        added[0].wait_recv()
+        self.mine[:, 0] = add(self.mine[:, 0], self.got_x[...], self.got_y2[...]).astype(BF16)
+        got[3].wait_recv()
+        added[1].wait_recv()
+        self.mine[:, 1] = add(self.mine[:, 1], self.got_y[...], self.got_x2[...]).astype(BF16)
+        for copy in self.along():
+            copy.start()
+
+    def finish(self):
+        for copy in self.along():
+            copy.wait_recv()
+        self.out[...] = add(self.mine[self.high], *[self.got_far[k] for k in range(self.far - 1)])
+        for copy in self.from_grads() + self.added() + self.along():
+            copy.wait_send()
+
+
+    def plan(self, start):
+        along = RATE * self.mine.shape[3]
+        times = (start, start + 4 + 2 * along / 3, start + 8 + along)
+        return list(zip(times, (self.begin, self.second, self.third)))
+
+
+def scatters_scratch(jobs, dim):
+    scratch = []
+    for _, width in jobs:
+        scratch += scatter_scratch(width, dim)
+    return scratch
+
+
+def scatter_outs(jobs, dim):
+    half = dim // lax.axis_size("dp") // 2
+    shapes = [jax.ShapeDtypeStruct((2, half, width), F32) for _, width in jobs]
+    return shapes, [once(shape.shape) for shape in shapes]
+
+
+def add_scatters(plan, jobs, sources, outs, refs, start=0.0):
+    for at, (first, width) in enumerate(jobs):
+        scatter = Scatter(sources[at], first, outs[at], refs[SCATTER_REFS * at : SCATTER_REFS * (at + 1)])
+        plan.add(scatter.plan(start), scatter.finish)
+        start += RATE * width
+
+
+def grad_shape(dim, columns):
+    return jax.ShapeDtypeStruct((far_count(), 4, 2, dim // lax.axis_size("dp") // 2, columns), BF16)
+
+
+def add(*terms):
+    total = terms[0].astype(F32)
+    for term in terms[1:]:
+        total = total + term.astype(F32)
+    return total
+
+
+def call(kernel, name, number, steps, in_specs, out_specs, out_shape, scratch, operands):
+    return pl.pallas_call(
+        kernel,
+        grid=steps if isinstance(steps, tuple) else (steps,),
+        in_specs=in_specs,
+        out_specs=out_specs,
+        out_shape=out_shape,
+        scratch_shapes=scratch,
+        compiler_params=params(number),
+        name=name,
+    )(*operands)
+
+
+def spread_gains(slab, column):
+    dim = slab.shape[0]
+    blocks = lax.axis_size("dp")
+    each = dim // blocks
+    lane_block = lax.broadcasted_iota(jnp.int32, (blocks, dim), 1) // each
+    block = lax.broadcasted_iota(jnp.int32, (blocks, dim), 0)
+    rows = []
+    for which in range(2):
+        picked = jnp.concatenate(
+            [slab[each * b : each * b + 16, column : column + 128].astype(F32)[which : which + 1] for b in range(blocks)], 0
+        )
+        tiled = jnp.concatenate([picked] * (dim // 128), 1)
+        rows.append(jnp.sum(jnp.where(lane_block == block, tiled, 0.0), axis=0, keepdims=True))
+    return jnp.concatenate(rows + [jnp.zeros((6, dim), F32)], 0)
+
+
+def part_block(width, per, rows, lag=0, last=None):
+    def place(i):
+        i = i - lag if last is None else jnp.clip(i - lag, 0, last)
+        return lax.div(i, per), lax.rem(i, per), 0
+
+    return pl.BlockSpec((1, rows, width), place)
+
+
+def core_block(width, per, rows, other, last=None):
+    def place(i):
+        if last is not None:
+            i = jnp.minimum(i, last)
+        core = lax.axis_index("tensor")
+        return lax.div(i, per), (1 - core if other else core) * per + lax.rem(i, per), 0
+
+    return pl.BlockSpec((1, rows, width), place)
+
+
+def root_mean(values):
+    return lax.rsqrt(jnp.mean(values * values, axis=-1, keepdims=True) + 1e-05)
+
+
+def norm_slope(values, scaled):
+    inverse = root_mean(values)
+    normed = values * inverse
+    return inverse * (scaled - normed * jnp.mean(scaled * normed, axis=-1, keepdims=True))
+
+
+def half_sems(count):
+    return [pltpu.SemaphoreType.DMA((count,)), pltpu.SemaphoreType.DMA((count,))]
+
+
+def chunk_slices(width):
+    return [(at, min(256, width - at)) for at in range(0, width, 256)]
+
+
+def build_slabs(edges, gate, up, down_t, out_t, slabs):
+    at = out_t.shape[1]
+    slabs[:, :at] = out_t[...]
+    units = gate.shape[1]
+
+    def place(ref, low, high):
+        nonlocal at
+        end = min(high, units)
+        slabs[:, at : at + end - low] = ref[:, low:end]
+        if end < high:
+            slabs[:, at + end - low : at + high - low] = jnp.zeros((slabs.shape[0], high - end), BF16)
+        at += high - low
+
+    for low, high in edges:
+        for start, width in chunk_slices(high - low):
+            place(gate, low + start, low + start + width)
+            place(up, low + start, low + start + width)
+        place(down_t, low, high)
+
+
+def project_kernel(
+    edges, inputs, w_query, w_key, w_value, gain_attn, gain_mlp, gate, up, down_t, out_t,
+    h_out, qkv_out, gain_out, whole_in, slabs, x_own, x_other, h_all, qkv_all, slab, gain_slab,
+    local, swap_send, swap_recv, *sems,
+):
+    micro, rows, _ = x_own.shape
+    each = w_query.shape[0]
+    core = lax.axis_index("tensor")
+    parts = 2 * micro
+
+    def load(m):
+        return pltpu.make_async_copy(inputs.at[m], x_own.at[m], local.at[m])
+
+    def swap(m):
+        return remote(inputs.at[m], x_other.at[m], swap_send.at[m], swap_recv.at[m], sibling())
+
+    def place(t):
+        first = pl.multiple_of((core if t < micro else 1 - core) * rows, rows)
+        return t % micro, pl.ds(first, rows)
+
+    def store_h(t):
+        return pltpu.make_async_copy(h_all.at[t], h_out.at[place(t)], local.at[micro + t])
+
+    def store_qkv(t):
+        return pltpu.make_async_copy(qkv_all.at[t], qkv_out.at[place(t)], local.at[micro + parts + t])
+
+    def keep():
+        return pltpu.make_async_copy(slab, whole_in, local.at[micro + 2 * parts])
+
+    def norm(t):
+        x = (x_own if t < micro else x_other)[t % micro].astype(F32)
+        h_all[t] = (x * root_mean(x) * gain_out[0:1]).astype(BF16)
+        store_h(t).start()
+
+    for m in range(micro):
+        load(m).start()
+    mine = pl.ds(pl.multiple_of(lax.axis_index("dp") * each, each), each)
+    at = 0
+    for ref in (w_query, w_key, w_value):
+        slab[mine, at : at + ref.shape[1]] = ref[...]
+        at += ref.shape[1]
+    both = jnp.concatenate([gain_attn[...], gain_mlp[...]], 0).astype(F32)
+    both = jnp.concatenate([both, both], 1)
+    gain_slab[mine] = jnp.concatenate([both, jnp.zeros((each - 2, both.shape[1]), F32)], 0).astype(BF16)
+    greet(dp_peers() + [sibling()])
+    gains = Gather(gain_slab.at[mine], gain_slab, *sems[:2])
+    weights = Gather(slab.at[mine], slab, *sems[2:])
+    gains.begin()
+    weights.begin()
+    for m in range(micro):
+        swap(m).start()
+    build_slabs(edges, gate, up, down_t, out_t, slabs)
+    for k in range(1, gains.far):
+        gains.spread(k)
+    for k in range(gains.far):
+        gains.turn(k)
+    gains.finish()
+    gain_out[...] = spread_gains(gain_slab, 0)
+    duties = [functools.partial(weights.spread, k) for k in range(1, weights.far)]
+    duties += [functools.partial(weights.turn, k) for k in range(weights.far)]
+    for t in range(parts):
+        if t < micro:
+            load(t).wait()
+        else:
+            swap(t - micro).wait()
+        norm(t)
+        if duties:
+            duties.pop(0)()
+    for duty in duties:
+        duty()
+    weights.finish()
+    keep().start()
+    for t in range(parts):
+        qkv_all[t] = mm(h_all[t], slab[...]).astype(BF16)
+        store_qkv(t).start()
+    for t in range(parts):
+        store_h(t).wait()
+        store_qkv(t).wait()
+    keep().wait()
+
+
+def project(edges, inputs, w_query, w_key, w_value, gain_attn, gain_mlp, w_gate, w_up, down_t, out_t):
+    micro, rows, dim = inputs.shape
+    each = w_query.shape[0]
+    columns = w_query.shape[1] + w_key.shape[1] + w_value.shape[1]
+    all_columns = out_t.shape[1] + 3 * edges[-1][1]
+    locals_ = (w_query, w_key, w_value, gain_attn, gain_mlp, w_gate, w_up, down_t, out_t)
+    return call(
+        functools.partial(project_kernel, edges),
+        "project",
+        1,
+        1,
+        [anywhere()] + [once(a.shape) for a in locals_],
+        [anywhere(), anywhere(), once((8, dim)), anywhere(), once((each, all_columns))],
+        [
+            jax.ShapeDtypeStruct((micro, 2 * rows, dim), BF16),
+            jax.ShapeDtypeStruct((micro, 2 * rows, columns), BF16),
+            jax.ShapeDtypeStruct((8, dim), F32),
+            jax.ShapeDtypeStruct((dim, columns), BF16),
+            jax.ShapeDtypeStruct((each, all_columns), BF16),
+        ],
+        [
+            pltpu.VMEM((micro, rows, dim), BF16),
+            pltpu.VMEM((micro, rows, dim), BF16),
+            pltpu.VMEM((2 * micro, rows, dim), BF16),
+            pltpu.VMEM((2 * micro, rows, columns), BF16),
+            pltpu.VMEM((dim, columns), BF16),
+            pltpu.VMEM((dim, 128), BF16),
+            pltpu.SemaphoreType.DMA((5 * micro + 1,)),
+        ]
+        + half_sems(micro)
+        + gather_sems()[:2]
+        + gather_sems()[:2],
+        (inputs, *locals_),
+    )
+
+
+def fill_mask(mask, lengths, micro_step):
+    tiles = mask.shape[0]
+    row = lax.broadcasted_iota(jnp.int32, (tiles * TILE, TILE), 0)
+    start = jnp.zeros_like(row)
+    end = 0
+    for d in range(lengths.shape[1]):
+        end = end + lengths[micro_step, d]
+        start = jnp.where(row >= end, end, start)
+    lane = lax.broadcasted_iota(jnp.int32, (tiles * TILE, TILE), 1)
+    for j in range(tiles):
+        i = min(tiles, j + SPAN + 1)
+        tall = (i - j) * TILE
+        below = slice(j * TILE, i * TILE)
+        column = lane[:tall] + j * TILE
+        allowed = (column <= row[below]) & (column >= start[below])
+        mask[j, :tall, :] = jnp.where(allowed, 1.0, 0.0)
+
+
+def add_rows(total, j, tiles, value):
+    end = min(tiles, j + SPAN + 1)
+    begun = min(tiles, j + SPAN) if j else 0
+    if begun > j:
+        total[j * TILE : begun * TILE] += value[: (begun - j) * TILE]
+    if end > max(begun, j):
+        start = max(begun, j)
+        total[start * TILE : end * TILE] = value[(start - j) * TILE :]
+
+
+def attend_kernel(
+    jobs, lengths, qkv, grad_own, slabs, mix_ref, inv_ref, grad_other, whole_out, unit, mask, queries, values, total, *sems
+):
+    m = pl.program_id(0)
+    group = qkv.shape[1]
+    tiles = group // TILE
+    pairs = mix_ref.shape[2] // 128
+    lane = lax.broadcasted_iota(jnp.int32, (group, 128), 1)
+    zero = jnp.zeros((), BF16)
+
+    def swap():
+        return remote(grad_own, grad_other, sems[0], sems[1], sibling())
+
+    plan = Plan(m, lengths.shape[0], pairs, 8.0)
+    plan.add([(0.0, lambda: swap().start())], lambda: swap().wait())
+    add_gathers(plan, [(slabs, (whole_out, unit)[w], *job) for w, *job in jobs], sems[2:])
+
+    @pl.when(m == 0)
+    def _():
+        greet(dp_peers() + [sibling()])
+
+    fill_mask(mask, lengths, m)
+    query = qkv[0, :, :128] * jnp.asarray(0.25, BF16)
+    for pair in range(pairs):
+        at = 256 + 128 * pair
+        now = pair % 2
+        for side in range(2):
+            mine = lane // VD == side
+            queries[now, side] = jnp.where(lane // FEAT == 2 * pair + side, query, zero)
+            values[now, side, :, :128] = jnp.where(mine, qkv[0, :, at : at + 128], zero)
+            values[now, side, :, 128:] = mine.astype(F32).astype(BF16)
+        for j in range(tiles):
+            if j == 0:
+                plan.at(pair)
+            i = min(tiles, j + SPAN + 1)
+            tall = (i - j) * TILE
+            here, below = slice(j * TILE, (j + 1) * TILE), slice(j * TILE, i * TILE)
+            scores = mm(queries[now, :, below].reshape(2 * tall, 128), qkv[0, here, 128:256], NT)
+            allowed = mask[j, :tall]
+            weights = []
+            for side in range(2):
+                t = scores[side * tall : (side + 1) * tall] + 1.0
+                weights.append(((t * t + 1.0) * allowed).astype(BF16))
+            part = mm(jnp.concatenate(weights, 1), values[now, :, here].reshape(2 * TILE, 256))
+            add_rows(total.at[now], j, tiles, part)
+        inverse = 1.0 / total[now, :, 128:]
+        mix_ref[0, :, 128 * pair : 128 * (pair + 1)] = (total[now, :, :128] * inverse).astype(BF16)
+        turned = inverse.T
+        inv_ref[0, pair, 0:1] = turned[0:1]
+        inv_ref[0, pair, 1:2] = turned[VD : VD + 1]
+
+    @pl.when(m == pl.num_programs(0) - 1)
+    def _():
+        plan.finish()
+
+
+def whole_group(width, group):
+    return pl.BlockSpec((1, group, width), lambda m: (m, 0, 0))
+
+
+def lengths_spec(lengths):
+    return pl.BlockSpec(lengths.shape, lambda *_: (0, 0), memory_space=pltpu.SMEM)
+
+
+def attend_all(qkv, lengths, out_grad, slabs, out_columns, jobs):
+    micro, group, columns = qkv.shape
+    dim = out_grad.shape[2]
+    wide = columns - 256
+    dma = pltpu.SemaphoreType.DMA
+    unit = sum(job[3] for job in jobs if job[0])
+    return call(
+        functools.partial(attend_kernel, jobs),
+        "attend",
+        2,
+        micro,
+        [lengths_spec(lengths), whole_group(columns, group), anywhere(), anywhere()],
+        [
+            whole_group(wide, group),
+            pl.BlockSpec((1, wide // 128, 8, group), lambda m: (m, 0, 0, 0)),
+            anywhere(),
+            anywhere(),
+            anywhere(),
+        ],
+        [
+            jax.ShapeDtypeStruct((micro, group, wide), BF16),
+            jax.ShapeDtypeStruct((micro, wide // 128, 8, group), F32),
+            jax.ShapeDtypeStruct(out_grad.shape, BF16),
+            jax.ShapeDtypeStruct((dim, out_columns), BF16),
+            jax.ShapeDtypeStruct((dim, unit), BF16),
+        ],
+        [
+            pltpu.VMEM((group // TILE, TILE * (SPAN + 1), TILE), F32),
+            pltpu.VMEM((2, 2, group, 128), BF16),
+            pltpu.VMEM((2, 2, group, 256), BF16),
+            pltpu.VMEM((2, group, 256), F32),
+            dma,
+            dma,
+        ]
+        + gather_sems() * len(jobs),
+        (lengths, qkv, out_grad, slabs),
+    )
+
+
+def attend_back_kernel(jobs, lengths, qkv, mix_ref, inv_ref, dmix_ref, *refs):
+    sources, refs = refs[: len(jobs)], refs[len(jobs) :]
+    dqkv, refs = refs[0], refs[1:]
+    outs, refs = refs[: len(jobs)], refs[len(jobs) :]
+    (mask, queries, queries_t, keys, douts, douts_t, deltas, dv_t, dk_t, dq), refs = refs[:10], refs[10:]
+    m = pl.program_id(0)
+    group = qkv.shape[1]
+    tiles = group // TILE
+    pairs = mix_ref.shape[2] // 128
+    lane = lax.broadcasted_iota(jnp.int32, (group, 128), 1)
+    zero = jnp.zeros((), BF16)
+    plan = Plan(m, lengths.shape[0], pairs, 15.2)
+    add_scatters(plan, jobs, sources, outs, refs)
+
+    @pl.when(m == 0)
+    def _():
+        greet(dp_peers())
+
+    fill_mask(mask, lengths, m)
+    queries_t[...] = (qkv[0, :, :128].astype(F32) * 0.5).T.astype(BF16)
+    query = qkv[0, :, :128] * jnp.asarray(0.25, BF16)
+    key = qkv[0, :, 128:256] * jnp.asarray(0.5, BF16)
+    for pair in range(pairs):
+        now = pair % 2
+        lanes = slice(128 * pair, 128 * (pair + 1))
+        value = slice(256 + 128 * pair, 384 + 128 * pair)
+        inverse = jnp.concatenate(
+            [jnp.broadcast_to(inv_ref[0, pair, s : s + 1, :], (VD, group)) for s in range(2)], 0
+        ).T
+        dout_low = (dmix_ref[0, :, lanes].astype(F32) * inverse).astype(BF16)
+        dout = dout_low.astype(F32)
+        douts_t[now] = dout.T.astype(BF16)
+        product = dout * mix_ref[0, :, lanes].astype(F32)
+        for side in range(2):
+            mine = lane // VD == side
+            head = lane // FEAT == 2 * pair + side
+            queries[now, side] = jnp.where(head, query, zero)
+            keys[now, side] = jnp.where(head, key, zero)
+            douts[now, side] = jnp.where(mine, dout_low, zero)
+            delta = jnp.sum(jnp.where(mine, product, 0.0), axis=1, keepdims=True)
+            deltas[now, side] = jnp.broadcast_to(delta, (group, 128))
+        for j in range(tiles):
+            if j == 0:
+                plan.at(pair)
+            i = min(tiles, j + SPAN + 1)
+            tall = (i - j) * TILE
+            here, below = slice(j * TILE, (j + 1) * TILE), slice(j * TILE, i * TILE)
+            scores = mm(queries[now, :, below].reshape(2 * tall, 128), qkv[0, here, 128:256], NT)
+            slopes = mm(douts[now, :, below].reshape(2 * tall, 128), qkv[0, here, value], NT)
+            allowed = mask[j, :tall]
+            d_scores = []
+            for side in range(2):
+                t = scores[side * tall : (side + 1) * tall] + 1.0
+                masked = t * allowed
+                delta = jnp.concatenate([deltas[now, side, below]] * (TILE // 128), 1)
+                d_score = ((slopes[side * tall : (side + 1) * tall] - delta) * masked).astype(BF16)
+                weights = (t * masked + allowed).astype(BF16)
+                mine = slice(VD * side, VD * (side + 1))
+                head = slice((2 * pair + side) * FEAT, (2 * pair + side + 1) * FEAT)
+                dv_t[now, mine, here] = mm(douts_t[now, mine, below], weights)
+                dk_t[head, here] = mm(queries_t[head, below], d_score)
+                d_scores.append(d_score)
+            part = mm(jnp.concatenate(d_scores, 1), keys[now, :, here].reshape(2 * TILE, 128))
+            if pair:
+                dq[below] += part
+            else:
+                add_rows(dq, j, tiles, part)
+        dqkv[0, :, value] = dv_t[now].T.astype(BF16)
+    dqkv[0, :, 128:256] = dk_t[...].T.astype(BF16)
+    dqkv[0, :, :128] = dq[...].astype(BF16)
+
+    @pl.when(m == pl.num_programs(0) - 1)
+    def _():
+        plan.finish()
+
+
+def attend_back(qkv, mix, inverse, dmix, lengths, sources, jobs):
+    micro, group, columns = qkv.shape
+    wide = columns - 256
+    dim = sources[0].shape[3] * 2 * lax.axis_size("dp")
+    shapes, specs = scatter_outs(jobs, dim)
+    pair_rows = pltpu.VMEM((2, 2, group, 128), BF16)
+    return call(
+        functools.partial(attend_back_kernel, jobs),
+        "attend_back",
+        8,
+        micro,
+        [
+            lengths_spec(lengths),
+            whole_group(columns, group),
+            whole_group(wide, group),
+            pl.BlockSpec((1, wide // 128, 8, group), lambda m: (m, 0, 0, 0)),
+            whole_group(wide, group),
+        ]
+        + [anywhere()] * len(jobs),
+        [whole_group(columns, group)] + specs,
+        [jax.ShapeDtypeStruct((micro, group, columns), BF16)] + shapes,
+        [
+            pltpu.VMEM((group // TILE, TILE * (SPAN + 1), TILE), F32),
+            pair_rows,
+            pltpu.VMEM((128, group), BF16),
+            pair_rows,
+            pair_rows,
+            pltpu.VMEM((2, 128, group), BF16),
+            pltpu.VMEM((2, 2, group, 128), F32),
+            pltpu.VMEM((2, 128, group), F32),
+            pltpu.VMEM((128, group), F32),
+            pltpu.VMEM((group, 128), F32),
+        ]
+        + scatters_scratch(jobs, dim),
+        (lengths, qkv, mix, inverse, dmix, *sources),
+    )
+
+
+def out_kernel(
+    jobs, mix_own, mix_other, x, weights, gains, slabs, resid_out, h_out, h_other, unit,
+    parts, sent, got, h_sent, send, recv, *sems,
+):
+    i = pl.program_id(0)
+    count, rows = got.shape[0], got.shape[1]
+    per = h_other.shape[1] // rows
+    plan = Plan(i, 2 * count, 1, 0.95)
+    add_gathers(plan, [(slabs, unit, *job) for job in jobs], sems)
+
+    def swap(k):
+        return remote(sent.at[k], got.at[k], send.at[k], recv.at[k], sibling())
+
+    def swap_h(k):
+        place = h_other.at[lax.div(k, per), pl.ds(pl.multiple_of(lax.rem(k, per) * rows, rows), rows)]
+        return remote(h_sent.at[k], place, send.at[count + k], recv.at[count + k], sibling())
+
+    @pl.when(i == 0)
+    def _():
+        greet(dp_peers() + [sibling()])
+
+    plan.at(0)
+
+    @pl.when(i < count)
+    def _():
+        both = jnp.concatenate([mix_other[0], mix_own[0]], 0)
+        part = mm(both, weights[...], NT)
+        sent[i] = part[:rows].astype(BF16)
+        parts[i] = part[rows:]
+        swap(i).start()
+
+    @pl.when(i >= count)
+    def _():
+        k = i - count
+        swap(k).wait_recv()
+        resid = x[0].astype(F32) + parts[k] + got[k].astype(F32)
+        resid_out[0] = resid.astype(BF16)
+        h = (resid * root_mean(resid) * gains[1:2]).astype(BF16)
+        h_out[0] = h
+        h_sent[k] = h
+        swap_h(k).start()
+
+    @pl.when(i == 2 * count - 1)
+    def _():
+        plan.finish()
+        for k in range(count):
+            swap(k).wait_send()
+            swap_h(k).wait()
+
+
+def out_project(mix, x, weights, gains, slabs, jobs, rows=256):
+    micro, own_rows, dim = x.shape
+    wide = mix.shape[2]
+    per = own_rows // rows
+    count = micro * per
+    late = part_block(dim, per, rows, count, count - 1)
+    shape = jax.ShapeDtypeStruct((micro, own_rows, dim), BF16)
+    buffer = pltpu.VMEM((count, rows, dim), BF16)
+    return call(
+        functools.partial(out_kernel, jobs),
+        "out_project",
+        3,
+        2 * count,
+        [
+            core_block(wide, per, rows, False, count - 1),
+            core_block(wide, per, rows, True, count - 1),
+            late,
+            once(weights.shape),
+            once((8, dim)),
+            anywhere(),
+        ],
+        [late, late, anywhere(), anywhere()],
+        [shape, shape, shape, jax.ShapeDtypeStruct((dim, sum(job[2] for job in jobs)), BF16)],
+        [pltpu.VMEM((count, rows, dim), F32), buffer, buffer, buffer]
+        + half_sems(2 * count)
+        + gather_sems() * len(jobs),
+        (mix, mix, x, weights, gains, slabs),
+    )
+
+
+FEED_US = 6.8
+
+
+def feed_kernel(steps, width, loads, first, last, gathers, scatters, h_own, h_other, g_own, g_other, *refs):
+    def take(number):
+        nonlocal refs
+        taken, refs = refs[:number], refs[number:]
+        return taken
+
+    weights = take(len(loads))
+    before = None if first else take(4)
+    slabs = take(1)[0] if gathers else None
+    sources = take(len(scatters))
+    if last:
+        resid, g_late, resid_end, g_end, gains, mixed_out, d_out, d_other = take(8)
+    else:
+        out_own, out_other, dm_own, dm_other = take(4)
+    grads = take(1)[0]
+    unit = take(1)[0] if gathers else None
+    outs = take(len(scatters))
+    slab, total, h, g, hidden_s, dgu_s, rounded, load_sems, out_sem = take(9)
+    i = pl.program_id(0)
+    rows = h_own.shape[1]
+    plan = Plan(i, steps, 1, FEED_US * width / 512)
+    add_gathers(plan, [(slabs, unit, *job) for job in gathers], take(3 * len(gathers)))
+    busy = sum(RATE * job[2] for job in gathers)
+    add_scatters(plan, scatters, sources, outs, take(SCATTER_REFS * len(scatters)), busy)
+    if last:
+        dm_sent, dm_got, out_sent, out_got, dm_kept, out_kept, d_sent, mixed_s, send, recv, local = take(11)
+        per = d_other.shape[1] // rows
+
+        def place(ref, k):
+            return ref.at[lax.div(k, per), pl.ds(pl.multiple_of(lax.rem(k, per) * rows, rows), rows)]
+
+        def swaps(k):
+            return [
+                remote(dm_sent.at[k], dm_got.at[k + 1], send.at[3 * k], recv.at[3 * k], sibling()),
+                remote(out_sent.at[k], out_got.at[k + 1], send.at[3 * k + 1], recv.at[3 * k + 1], sibling()),
+            ]
+
+        def results(k):
+            return [
+                remote(d_sent.at[k + 1], place(d_other, k), send.at[3 * k + 2], recv.at[3 * k + 2], sibling()),
+                pltpu.make_async_copy(d_sent.at[k + 1], place(d_out, k), local.at[2 * k]),
+                pltpu.make_async_copy(mixed_s.at[k + 1], place(mixed_out, k), local.at[2 * k + 1]),
+            ]
+
+        def finish_part(slot, resid, g_late):
+            values = resid[0].astype(F32)
+            mixed_s[slot] = add(values, out_kept[lax.rem(slot, 2)], out_got[slot]).astype(BF16)
+            scaled = add(dm_kept[lax.rem(slot, 2)], dm_got[slot]) * gains[1:2]
+            d_sent[slot] = (g_late[0].astype(F32) + norm_slope(values, scaled)).astype(BF16)
+
+    def copies():
+        made = []
+        for at, (ref, (source, target, columns)) in enumerate(zip(weights, loads)):
+            cut = ref.at[:, pl.ds(source, columns)]
+            made.append(pltpu.make_async_copy(cut, slab.at[:, pl.ds(target, columns)], load_sems.at[at]))
+        return made
+
+    @pl.when(i == 0)
+    def _():
+        for copy in copies():
+            copy.start()
+        if last:
+            zeros = jnp.zeros(dm_kept.shape[1:], BF16)
+            for ref in (dm_got, out_got, dm_kept, out_kept):
+                ref[0] = zeros
+        greet(dp_peers() + ([sibling()] if last else []))
+
+    plan.at(0)
+
+    @pl.when(i == 0)
+    def _():
+        total[...] = jnp.zeros_like(total)
+        for copy in copies():
+            copy.wait()
+
+    h[:rows], h[rows:] = h_other[0], h_own[0]
+    g[:rows], g[rows:] = g_other[0], g_own[0]
+    half = jnp.asarray(0.5, BF16)
+    one = jnp.asarray(1.0, BF16)
+    for at, wide in chunk_slices(width):
+        both = slice(2 * at, 2 * (at + wide))
+        gate_up = mm(h[...], slab[:, both]).astype(BF16)
+        d_hidden = mm(g[...], slab[:, 2 * width + at : 2 * width + at + wide]).astype(BF16)
+        gate, up = gate_up[:, :wide], gate_up[:, wide:]
+        sigmoid = half * jnp.tanh(half * gate) + half
+        silu = gate * sigmoid
+        hidden_s[:, at : at + wide] = silu * up
+        d_gate = d_hidden * up * (sigmoid + silu * (one - sigmoid))
+        dgu_s[:, both] = jnp.concatenate([d_gate, d_hidden * silu], 1)
+    dim = slab.shape[0]
+    for at in range(0, dim, 512):
+        cut = slice(at, at + 512)
+        out = mm(hidden_s[...], slab[cut, 2 * width :], NT)
+        dm = mm(dgu_s[...], slab[cut, : 2 * width], NT)
+        parts_now = []
+        for at_before, value in enumerate((out[rows:], out[:rows], dm[rows:], dm[:rows])):
+            if not first:
+                value = value + before[at_before][0, :, cut].astype(F32)
+            parts_now.append(value.astype(BF16))
+        if last:
+            out_sent[i, :, cut], dm_sent[i, :, cut] = parts_now[1], parts_now[3]
+            kept = lax.rem(i + 1, 2)
+            out_kept[kept, :, cut], dm_kept[kept, :, cut] = parts_now[0], parts_now[2]
+        else:
+            out_own[0, :, cut], out_other[0, :, cut] = parts_now[0], parts_now[1]
+            dm_own[0, :, cut], dm_other[0, :, cut] = parts_now[2], parts_now[3]
+    if last:
+        for swap in swaps(i):
+            swap.start()
+
+        @pl.when(i > 0)
+        def _():
+            for swap in swaps(i - 1):
+                swap.wait_recv()
+
+        finish_part(i, resid, g_late)
+    total[:, : 2 * width] += mm(h[...], dgu_s[...], TN)
+    total[:, 2 * width :] += mm(g[...], hidden_s[...], TN)
+    if last:
+
+        @pl.when(i > 0)
+        def _():
+            for copy in results(i - 1):
+                copy.start()
+
+    @pl.when(i == steps - 1)
+    def _():
+        rounded[...] = total[...].astype(BF16).reshape(rounded.shape)
+        write = pltpu.make_async_copy(rounded, grads, out_sem)
+        write.start()
+        if last:
+            for swap in swaps(steps - 1):
+                swap.wait_recv()
+            finish_part(steps, resid_end, g_end)
+            for copy in results(steps - 1):
+                copy.start()
+        plan.finish()
+        if last:
+            for k in range(steps):
+                for copy in swaps(k):
+                    copy.wait_send()
+                for copy in results(k):
+                    copy.wait()
+        write.wait()
+
+
+def feed(number, rows_in, loads, width, before, slabs, gathers, sources, scatters, last=None, rows=256):
+    micro, own_rows, dim = rows_in[0].shape
+    columns = 3 * width
+    per = own_rows // rows
+    steps = micro * per
+    part = part_block(dim, per, rows)
+    shape = jax.ShapeDtypeStruct((micro, own_rows, dim), BF16)
+    grads = grad_shape(dim, columns)
+    first = before is None
+    in_specs = [part] * 4 + [anywhere()] * len(loads)
+    operands = list(rows_in) + [load[0] for load in loads]
+    scratch = [
+        pltpu.VMEM((dim, columns), BF16),
+        pltpu.VMEM((dim, columns), F32),
+        pltpu.VMEM((2 * rows, dim), BF16),
+        pltpu.VMEM((2 * rows, dim), BF16),
+        pltpu.VMEM((2 * rows, width), BF16),
+        pltpu.VMEM((2 * rows, 2 * width), BF16),
+        pltpu.VMEM(grads.shape, BF16),
+        pltpu.SemaphoreType.DMA((len(loads),)),
+        pltpu.SemaphoreType.DMA,
+    ]
+    if not first:
+        in_specs += [part] * 4
+        operands += list(before)
+    if gathers:
+        in_specs.append(anywhere())
+        operands.append(slabs)
+    in_specs += [anywhere()] * len(scatters)
+    operands += sources
+    if last:
+        resid, gains = last
+        late = part_block(dim, per, rows, 1, steps - 1)
+        end = pl.BlockSpec((1, rows, dim), lambda i: (micro - 1, per - 1, 0), pipeline_mode=pl.Buffered(1))
+        in_specs += [late, late, end, end, once((8, dim))]
+        operands += [resid, rows_in[2], resid, rows_in[2], gains]
+        out_specs, out_shape = [anywhere()] * 4, [shape] * 3 + [grads]
+    else:
+        out_specs, out_shape = [part] * 4 + [anywhere()], [shape] * 4 + [grads]
+    plain = len(out_shape)
+    if gathers:
+        out_specs.append(anywhere())
+        out_shape.append(jax.ShapeDtypeStruct((dim, sum(job[2] for job in gathers)), BF16))
+        scratch += gather_sems() * len(gathers)
+    if scatters:
+        shapes, specs = scatter_outs(scatters, dim)
+        out_specs += specs
+        out_shape += shapes
+        scratch += scatters_scratch(scatters, dim)
+    if last:
+        plain_slots, late_slots = pltpu.VMEM((steps, rows, dim), BF16), pltpu.VMEM((steps + 1, rows, dim), BF16)
+        two_slots = pltpu.VMEM((2, rows, dim), BF16)
+        scratch += [plain_slots, late_slots] * 2 + [two_slots] * 2 + [late_slots] * 2 + half_sems(3 * steps)
+        scratch.append(pltpu.SemaphoreType.DMA((2 * steps,)))
+    results = call(
+        functools.partial(
+            feed_kernel, steps, width, [load[1:] for load in loads], first, last is not None, gathers, scatters
+        ),
+        "feed",
+        number,
+        steps,
+        in_specs,
+        out_specs,
+        out_shape,
+        scratch,
+        operands,
+    )
+    rest = list(results[plain:])
+    unit = rest.pop(0) if gathers else None
+    return results[: plain - 1], results[plain - 1], unit, rest
+
+
+def back_out_kernel(micro, jobs, d_own, d_other, mix, weights, *refs):
+    sources, refs = refs[: len(jobs)], refs[len(jobs) :]
+    (dmix, grads), refs = refs[:2], refs[2:]
+    outs, refs = refs[: len(jobs)], refs[len(jobs) :]
+    (d, total, rounded, out_sem), refs = refs[:4], refs[4:]
+    i = pl.program_id(0)
+    rows = d_own.shape[1]
+    plan = Plan(i, micro, 1, 4.5)
+    add_scatters(plan, jobs, sources, outs, refs)
+
+    @pl.when(i == 0)
+    def _():
+        greet(dp_peers())
+        total[...] = jnp.zeros_like(total)
+
+    plan.at(0)
+    core = lax.axis_index("tensor")
+    d[pl.ds(pl.multiple_of(core * rows, rows), rows)] = d_own[0]
+    d[pl.ds(pl.multiple_of((1 - core) * rows, rows), rows)] = d_other[0]
+    dmix[0] = mm(d[...], weights[...]).astype(BF16)
+    total[...] += mm(d[...], mix[0], TN)
+
+    @pl.when(i == pl.num_programs(0) - 1)
+    def _():
+        rounded[...] = total[...].astype(BF16).reshape(rounded.shape)
+        write = pltpu.make_async_copy(rounded, grads, out_sem)
+        write.start()
+        plan.finish()
+        write.wait()
+
+
+def back_out(d_own, d_other, mix, weights, sources, jobs):
+    micro, rows, dim = d_own.shape
+    columns = mix.shape[2]
+    part = pl.BlockSpec((1, rows, dim), lambda i: (i, 0, 0))
+    grads = grad_shape(dim, columns)
+    shapes, specs = scatter_outs(jobs, dim)
+    return call(
+        functools.partial(back_out_kernel, micro, jobs),
+        "back_out",
+        7,
+        micro,
+        [part, part, whole_group(columns, 2 * rows), once(weights.shape)] + [anywhere()] * len(jobs),
+        [whole_group(columns, 2 * rows), anywhere()] + specs,
+        [jax.ShapeDtypeStruct((micro, 2 * rows, columns), BF16), grads] + shapes,
+        [
+            pltpu.VMEM((2 * rows, dim), BF16),
+            pltpu.VMEM((dim, columns), F32),
+            pltpu.VMEM(grads.shape, BF16),
+            pltpu.SemaphoreType.DMA,
+        ]
+        + scatters_scratch(jobs, dim),
+        (d_own, d_other, mix, weights, *sources),
+    )
+
+
+def back_in_kernel(
+    micro, feed_jobs, out_jobs, in_jobs, h, dqkv_all, dqkv, x, d_own, weights, gains, grads_last,
+    w_query, w_key, w_value, slabs, *refs,
+):
+    jobs = out_jobs + in_jobs
+    feed_count = sum(len(chunk) for chunk in feed_jobs)
+    feed_grads, refs = refs[:feed_count], refs[feed_count:]
+    (input_grad, gain_sums, grads), refs = refs[:3], refs[3:]
+    outs, refs = refs[: len(jobs)], refs[len(jobs) :]
+    (total, sent, got, send, recv, out_sem, rounded, sums, sums_got, sums_sems), refs = refs[:10], refs[10:]
+    i = pl.program_id(0)
+    m = lax.rem(i, micro)
+    plan = Plan(i, 3 * micro, 1, 2.4)
+    split = SCATTER_REFS * len(out_jobs)
+    add_scatters(plan, out_jobs, [grads_last] * len(out_jobs), outs, refs[:split])
+    outs = outs[len(out_jobs) :]
+    add_scatters(plan, in_jobs, [grads] * len(in_jobs), outs, refs[split:], 2.4 * micro)
+
+    def swap(k):
+        return remote(sent.at[k], got.at[k], send.at[k], recv.at[k], sibling())
+
+    def swap_sums():
+        return remote(sums, sums_got, sums_sems.at[0], sums_sems.at[1], sibling())
+
+    @pl.when(i == 0)
+    def _():
+        greet(dp_peers() + [sibling()])
+        total[...] = jnp.zeros_like(total)
+
+    @pl.when(i < micro)
+    def _():
+        total[...] += mm(h[0], dqkv_all[0], TN)
+
+    @pl.when(i == micro - 1)
+    def _():
+        rounded[...] = total[...].astype(BF16).reshape(rounded.shape)
+        write = pltpu.make_async_copy(rounded, grads, out_sem)
+        write.start()
+        write.wait()
+
+    plan.at(0)
+
+    @pl.when(i >= micro)
+    def _():
+        part = mm(dqkv[0], weights[...], NT)
+
+        @pl.when(i < 2 * micro)
+        def _():
+            sent[m] = part.astype(BF16)
+            swap(m).start()
+
+        @pl.when(i >= 2 * micro)
+        def _():
+            swap(m).wait_recv()
+            scaled = (part + got[m].astype(F32)) * gains[0:1]
+            input_grad[0] = (d_own[0].astype(F32) + norm_slope(x[0].astype(F32), scaled)).astype(BF16)
+
+    @pl.when(i == 3 * micro - 1)
+    def _():
+        each = slabs.shape[0]
+        sizes = [sum(wide for _, wide in chunk) for chunk in feed_jobs]
+        at = slabs.shape[1] - sum(sizes)
+        index = 0
+        mid = jnp.zeros((each, 128), F32)
+        for size, chunk in zip(sizes, feed_jobs):
+            for first, wide in chunk:
+                value = feed_grads[index][...].reshape(each, wide)
+                for column in range(0, wide, 128):
+                    if first + column < 2 * (size // 3):
+                        lanes = slice(at + first + column, at + first + column + 128)
+                        mid = mid + value[:, column : column + 128] * slabs[:, lanes].astype(F32)
+                index += 1
+            at += size
+        sums[1] = mid
+        plan.finish()
+        near = jnp.zeros((each, 128), F32)
+        at = 0
+        columns = [out[...].reshape(each, out.shape[2]) for out in outs]
+        columns = jnp.concatenate(columns, 1) if len(columns) > 1 else columns[0]
+        for ref in (w_query, w_key, w_value):
+            for column in range(0, ref.shape[1], 128):
+                near = near + columns[:, at : at + 128] * ref[:, column : column + 128].astype(F32)
+                at += 128
+        sums[0] = near
+        swap_sums().start()
+        for k in range(micro):
+            swap(k).wait_send()
+        swap_sums().wait()
+        gain_sums[...] = sums[...] + sums_got[...]
+
+
+def back_in(h, dqkv, x, d_own, weights, gains, grads_last, w_in, slabs, feed_grads, feed_jobs, out_jobs, in_jobs):
+    jobs = out_jobs + in_jobs
+    micro, rows, dim = x.shape
+    columns = dqkv.shape[2]
+    each = slabs.shape[0]
+    own = pl.BlockSpec((1, rows, dim), lambda i: (jnp.maximum(i - 2 * micro, 0), 0, 0))
+    grads = grad_shape(dim, columns)
+    shapes, specs = scatter_outs(jobs, dim)
+    buffer = pltpu.VMEM((micro, rows, dim), BF16)
+    sums = jax.ShapeDtypeStruct((2, each, 128), F32)
+
+    def all_place(i):
+        return jnp.minimum(i, micro - 1), 0, 0
+
+    def place(i):
+        core = lax.axis_index("tensor")
+        k = jnp.maximum(i - micro, 0)
+        return lax.rem(k, micro), jnp.where(k < micro, 1 - core, core), 0
+
+    locals_ = list(w_in) + [slabs] + list(feed_grads)
+    return call(
+        functools.partial(back_in_kernel, micro, feed_jobs, out_jobs, in_jobs),
+        "back_in",
+        9,
+        3 * micro,
+        [
+            pl.BlockSpec((1, 2 * rows, dim), all_place),
+            pl.BlockSpec((1, 2 * rows, columns), all_place),
+            pl.BlockSpec((1, rows, columns), place),
+            own,
+            own,
+            once(weights.shape),
+            once((8, dim)),
+            anywhere(),
+        ]
+        + [once(a.shape) for a in locals_],
+        [own, once(sums.shape), anywhere()] + specs,
+        [jax.ShapeDtypeStruct((micro, rows, dim), BF16), sums, grads] + shapes,
+        [pltpu.VMEM((dim, columns), F32), buffer, buffer]
+        + half_sems(micro)
+        + [
+            pltpu.SemaphoreType.DMA,
+            pltpu.VMEM(grads.shape, BF16),
+            pltpu.VMEM(sums.shape, F32),
+            pltpu.VMEM(sums.shape, F32),
+            pltpu.SemaphoreType.DMA((2,)),
+        ]
+        + scatters_scratch(jobs, dim),
+        (h, dqkv, dqkv, x, d_own, weights, gains, grads_last, *locals_),
+    )
+
+
+def finish_kernel(edges, counts, grad_in, mixed, gain_attn, gain_mlp, gain_sums, *refs):
+    feed_grads, refs = refs[: counts[0]], refs[counts[0] :]
+    out_grads, refs = refs[: counts[1]], refs[counts[1] :]
+    in_grads, refs = refs[: counts[2]], refs[counts[2] :]
+    mixed_out, grad_out, attn_out, mlp_out, q_out, k_out, v_out, out_t, gate_out, up_out, down_t = refs
+    each, units = gate_out.shape
+    grad_out[...] = grad_in[...].astype(F32)
+    mixed_out[...] = mixed[...]
+
+    def blocks(pieces):
+        found = []
+        for piece in pieces:
+            for at in range(0, piece.shape[2], 128):
+                found.append((piece, at))
+        return found
+
+    def copy_to(ref, at, block):
+        piece, column = block
+        wide = min(128, ref.shape[1] - at)
+        ref[:, at : at + wide] = piece[:, :, column : column + wide].reshape(each, wide)
+
+    @pl.when(pl.program_id(0) == 0)
+    def _():
+        turned = [gain_sums[k].T for k in range(2)]
+        for value, gain, ref in zip(turned, (gain_attn, gain_mlp), (attn_out, mlp_out)):
+            ref[...] = jnp.sum(value, axis=0, keepdims=True) / gain[...].astype(F32)
+        queue = blocks(in_grads)
+        for ref in (q_out, k_out, v_out):
+            for at in range(0, ref.shape[1], 128):
+                copy_to(ref, at, queue.pop(0))
+        for at, block in zip(range(0, out_t.shape[1], 128), blocks(out_grads)):
+            copy_to(out_t, at, block)
+        queue = blocks(feed_grads)
+        for low, high in edges:
+            for start, width in chunk_slices(high - low):
+                for ref in (gate_out, up_out):
+                    for at in range(low + start, low + start + width, 128):
+                        copy_to(ref, at, queue.pop(0))
+            for at in range(low, high, 128):
+                copy_to(down_t, at, queue.pop(0))
+
+
+def finish(edges, grad_in, mixed, gain_attn, gain_mlp, gain_sums, feed_grads, out_grads, in_grads, widths, units):
+    micro, rows, dim = mixed.shape
+    each = gain_sums.shape[1]
+    tile = min(rows, 256)
+    block = pl.BlockSpec((1, tile, dim), lambda m, t: (m, t, 0))
+    small = [gain_attn, gain_mlp, gain_sums, *feed_grads, *out_grads, *in_grads]
+    shapes = [jax.ShapeDtypeStruct((1, each), F32)] * 2
+    shapes += [jax.ShapeDtypeStruct((each, w), F32) for w in widths + [units] * 3]
+    counts = (len(feed_grads), len(out_grads), len(in_grads))
+    return call(
+        functools.partial(finish_kernel, edges, counts),
+        "finish",
+        None,
+        (micro, rows // tile),
+        [block, block] + [once(a.shape) for a in small],
+        [block, block] + [once(s.shape) for s in shapes],
+        [jax.ShapeDtypeStruct(mixed.shape, BF16), jax.ShapeDtypeStruct(mixed.shape, F32)] + shapes,
+        [],
+        (grad_in, mixed, *small),
+    )
+
+
+def fused_body(
+    inputs, gain_attn, gain_mlp, w_query, w_key, w_value, w_out, w_gate, w_up, w_down, out_grad, lengths
+):
+    micro, rows, dim = inputs.shape
+    units = w_gate.shape[1]
+    out_columns = w_out.shape[0]
+    lengths = lengths[:, 0]
+    gains = gain_attn.reshape(1, -1), gain_mlp.reshape(1, -1)
+    w_in = (w_query, w_key, w_value)
+    padded = -(-units // 128) * 128
+    edges = [(max(at - CHUNK, 0), at) for at in range(padded, 0, -CHUNK)][::-1]
+    wide = [3 * (high - low) for low, high in edges]
+
+    h_in, qkv, gain_full, whole_in, slabs = project(edges, inputs, *w_in, *gains, w_gate, w_up, w_down.T, w_out.T)
+
+    begin = [out_columns, out_columns + wide[0], out_columns + wide[0] + wide[1]]
+    early = min(EARLY, wide[0])
+    mix, inverse, g_other, whole_out, unit_0 = attend_all(
+        qkv, lengths, out_grad, slabs, out_columns, [(0, 0, 0, out_columns), (1, begin[0], 0, early)]
+    )
+    resid, h_own, h_other, unit_1 = out_project(
+        mix, inputs, whole_out, gain_full, slabs, [(begin[0] + early, 0, wide[0] - early)]
+    )
+
+    def in_pieces(first, width):
+        return [(first + at, at, most) for at, most in pieces_of(width, UNIT)]
+
+    feed_jobs, at = [[], [], []], []
+    for kernel in JOBS:
+        at.append([])
+        for chunk, width in kernel:
+            first = sum(w for _, w in feed_jobs[chunk])
+            feed_jobs[chunk].append((first, width))
+            at[-1].append((chunk, (first, width)))
+
+    def parts(number):
+        return [grads_of[chunk] for chunk, _ in at[number]], [job for _, job in at[number]]
+
+    rows_in = (h_own, h_other, out_grad, g_other)
+    grads_of = [None] * 3
+    loads = [(unit_0, 0, 0, early), (unit_1, 0, early, wide[0] - early)]
+    sums, grads_of[0], unit, _ = feed(4, rows_in, loads, wide[0] // 3, None, slabs, in_pieces(begin[1], wide[1]), [], [])
+    loads = [(unit, 0, 0, wide[1])]
+    sums, grads_of[1], unit, done = feed(
+        5, rows_in, loads, wide[1] // 3, sums, slabs, in_pieces(begin[2], wide[2]), *parts(0)
+    )
+    feed_grads = list(done)
+    loads = [(unit, 0, 0, wide[2])]
+    (mixed_out, d_own, d_other), grads_of[2], _, done = feed(
+        6, rows_in, loads, wide[2] // 3, sums, None, [], *parts(1), (resid, gain_full)
+    )
+    feed_grads += done
+    dmix, grads_out, *done = back_out(d_own, d_other, mix, whole_out, *parts(2))
+    feed_grads += done
+    dqkv, *done = attend_back(qkv, mix, inverse, dmix, lengths, *parts(3))
+    feed_grads += done
+    out_jobs, in_jobs = pieces_of(out_columns, 512), pieces_of(qkv.shape[2], 384)
+    input_grad, gain_sums, _, *done = back_in(
+        h_in, dqkv, inputs, d_own, whole_in, gain_full, grads_out, w_in, slabs, feed_grads, feed_jobs, out_jobs, in_jobs
+    )
+    out_grads, in_grads = done[: len(out_jobs)], done[len(out_jobs) :]
+    widths = [w.shape[1] for w in w_in] + [out_columns]
+    mixed_out, input_grad, attn_grad, mlp_grad, grad_query, grad_key, grad_value, out_t, gate, up, down_t = finish(
+        edges, input_grad, mixed_out, *gains, gain_sums, feed_grads, out_grads, in_grads, widths, units
+    )
+    return (
+        mixed_out,
+        input_grad,
+        attn_grad[0],
+        mlp_grad[0],
+        grad_query,
+        grad_key,
+        grad_value,
+        out_t.T,
+        gate,
+        up,
+        down_t.T,
+    )
+
+
 def solution(mesh):
     in_specs = (
         P(None, ("dp", "tensor"), None),
@@ -357,4 +1789,6 @@
         P("dp", "tensor"),
         P("tensor", "dp"),
     )
-    return jax.shard_map(body, mesh=mesh, in_specs=in_specs, out_specs=out_specs, check_vma=False)
+    fits = mesh.shape["tensor"] == 2 and mesh.shape["dp"] % 4 == 0
+    chosen = fused_body if fits else plain_body
+    return jax.shard_map(chosen, mesh=mesh, in_specs=in_specs, out_specs=out_specs, check_vma=False)

time: 2340 us -> 367 us (0.16)
  matrix products: 675 us -> 0 us
  waiting for transfers between devices: 545 us -> 0 us
  other arithmetic: 505 us -> 0 us
  Pallas kernels: 0 us -> 359 us
  local copies, waits for them, and re-layouts: 356 us -> 1.26 us
  blocking collectives: 165 us -> 0 us
  loops' own time: 52.9 us -> 0 us
    dot_general x171 -> x0, matrix products: 675 us -> none  [the longest x24 208 us: attend_block(): jnp.einsum('hrc,chv->rhv', weights, values_in, precision=EXACT)]
    pallas_call x0 -> x10, Pallas kernels: none -> 359 us  [call(): pl.pallas_call(kernel, grid=steps if isinstance(steps, tuple) else (steps...]
    reduce_scatter x19 -> x0, waiting for transfers between devices: 321 us -> none  [the longest x1 75.1 us: body(): lax.psum_scatter(grad_out_sum.astype(jnp.bfloat16), 'dp', scatter_dimensi...]
    all_gather x17 -> x0, waiting for transfers between devices: 217 us -> none  [the longest x1 70.2 us: fetch_weights(): lax.all_gather(w_down, 'dp', axis=1, tiled=True)]
    scatter-add x12 -> x0, other arithmetic: 213 us -> none  [taylor(): second = jnp.take(outer, flat_index, axis=-1) * factors]
    reduce_sum x26 -> x0, other arithmetic: 112 us -> none  [the longest x12 75.6 us: taylor(): halved[..., :, None] * halved[..., None, :]]
    mul x78 -> x0, other arithmetic: 103 us -> none  [the longest x30 73.1 us: taylor(): second = jnp.take(outer, flat_index, axis=-1) * factors]
    unnamed x2 -> x0, blocking collectives: 86.3 us -> none
  transfers between devices with their start and end apart: 36 -> 0, of which waited for: 17 -> 0; matrix products, arithmetic and copies ran while one was open for 63% -> 0% of each run, Pallas kernels for 0% -> 0%
where the time goes in v2:
time: 367 us; the launch traced here: 362 us
  Pallas kernels  359 us (98%)
    pallas_call x10, Pallas kernels, call(): pl.pallas_call(kernel, grid=steps if isinstance(steps, tuple) else (steps...  359 us

profile of v2, /device:TPU:0, one launch (start us, length us, event | category | flops | bytes accessed | tf_op | source)
XLA Modules:
  0.0 361.7 jit_solution(7379507752348549198)
XLA Ops:
  0.6 1.3 copy.25
  1.9 34.9 %project.1 = (bf16[3,1024,1024]{2,1,0:T(8,128)(2,1)}, bf16[3,1024,768]{2,1,0:T(8,128)(2,1)}, f32[8,1024]{1,0:T(8,128)}, bf16[1024,768]{1,0:T(8,128)(2,1)}, bf16[64,4736]{1,0:T(8,128)(2,1)}) custom-call(bf16[3,512,1024]{2,1,0:T(8,128)(2,1)} %x.3, bf16[64,128]{1,0:T(8,128)(2,1)} %w_query.3, bf16[64,128]{1,0:T(8,128)(2,1)} %w_key.3, bf16[64,512]{1,0:T(8,128)(2,1)} %w_value.3, ...), custom_call_target="tpu_custom_call" | custom-call | tf_op jit(solution)/shard_map/project/pallas_call | solution.py:674
  36.8 34.5 %attend.1 = (bf16[3,1024,512]{2,1,0:T(8,128)(2,1)}, f32[3,4,8,1024]{3,2,1,0:T(8,128)}, bf16[3,512,1024]{2,1,0:T(8,128)(2,1)}, bf16[1024,512]{1,0:T(8,128)(2,1)}, bf16[1024,640]{1,0:T(8,128)(2,1)}) custom-call(s32[3,8]{1,0:T(4,128)} %bitcast.13, bf16[3,1024,768]{2,1,0:T(8,128)(2,1)} %get-tuple-element.68.qkv, bf16[3,512,1024]{2,1,0:T(8,128)(2,1)} %refs_11_.1, ...), custom_call_target="tpu_custom_call" | custom-call | tf_op jit(solution)/shard_map/attend/pallas_call | solution.py:674
  71.2 20.6 %out_project.1 = (bf16[3,512,1024]{2,1,0:T(8,128)(2,1)}, bf16[3,512,1024]{2,1,0:T(8,128)(2,1)}, bf16[3,512,1024]{2,1,0:T(8,128)(2,1)}, bf16[1024,512]{1,0:T(8,128)(2,1)}) custom-call(bf16[3,1024,512]{2,1,0:T(8,128)(2,1)} %get-tuple-element.70.mix_own.mix_other.mix.mix_ref, bf16[3,1024,512]{2,1,0:T(8,128)(2,1)} %get-tuple-element.70.mix_own.mix_other.mix.mix_ref, ...), custom_call_target="tpu_custom_call" | custom-call | tf_op jit(solution)/shard_map/out_project/pallas_call | solution.py:674
  91.8 38.9 %feed.3 = (bf16[3,512,1024]{2,1,0:T(8,128)(2,1)}, bf16[3,512,1024]{2,1,0:T(8,128)(2,1)}, bf16[3,512,1024]{2,1,0:T(8,128)(2,1)}, bf16[3,512,1024]{2,1,0:T(8,128)(...) custom-call(bf16[3,512,1024]{2,1,0:T(8,128)(2,1)} %get-tuple-element.74.h_own, ...), custom_call_target="tpu_custom_call" | custom-call | tf_op jit(solution)/shard_map/feed/pallas_call | solution.py:674
  130.8 45.3 %feed.4 = (bf16[3,512,1024]{2,1,0:T(8,128)(2,1)}, bf16[3,512,1024]{2,1,0:T(8,128)(2,1)}, bf16[3,512,1024]{2,1,0:T(8,128)(2,1)}, bf16[3,512,1024]{2,1,0:T(8,128)(...) custom-call(bf16[3,512,1024]{2,1,0:T(8,128)(2,1)} %get-tuple-element.74.h_own, ...), custom_call_target="tpu_custom_call" | custom-call | tf_op jit(solution)/shard_map/feed/pallas_call | solution.py:674
  176.0 59.0 %feed.5 = (bf16[3,512,1024]{2,1,0:T(8,128)(2,1)}, bf16[3,512,1024]{2,1,0:T(8,128)(2,1)}, bf16[3,512,1024]{2,1,0:T(8,128)(2,1)}, bf16[4,4,2,32,1536]{4,3,2,1,0:T(...) custom-call(bf16[3,512,1024]{2,1,0:T(8,128)(2,1)} %get-tuple-element.74.h_own, ...), custom_call_target="tpu_custom_call" | custom-call | tf_op jit(solution)/shard_map/feed/pallas_call | solution.py:674
  235.1 19.8 %back_out.1 = (bf16[3,1024,512]{2,1,0:T(8,128)(2,1)}, bf16[4,4,2,32,512]{4,3,2,1,0:T(8,128)(2,1)}, f32[2,32,384]{2,1,0:T(8,128)}) custom-call(bf16[3,512,1024]{2,1,0:T(8,128)(2,1)} %get-tuple-element.92.d_own, bf16[3,512,1024]{2,1,0:T(8,128)(2,1)} %get-tuple-element.93.d_other, bf16[3,1024,512]{2,1,0:T(8,128)(2,1)} %get-tuple-element.70.mix_own.mix_other.mix.mix_ref, ...), custom_call_target="tpu_custom_call" | custom-call | tf_op jit(solution)/shard_map/back_out/pallas_call | solution.py:674
  254.8 57.6 %attend_back.1 = (bf16[3,1024,768]{2,1,0:T(8,128)(2,1)}, f32[2,32,384]{2,1,0:T(8,128)}, f32[2,32,768]{2,1,0:T(8,128)}, f32[2,32,768]{2,1,0:T(8,128)}) custom-call(s32[3,8]{1,0:T(4,128)} %bitcast.14, bf16[3,1024,768]{2,1,0:T(8,128)(2,1)} %get-tuple-element.68.qkv, bf16[3,1024,512]{2,1,0:T(8,128)(2,1)} %get-tuple-element.70.mix_own.mix_other.mix.mix_ref, ...), custom_call_target="tpu_custom_call" | custom-call | tf_op jit(solution)/shard_map/attend_back/pallas_call | solution.py:674
  312.5 40.2 %back_in.1 = (bf16[3,512,1024]{2,1,0:T(8,128)(2,1)}, f32[2,64,128]{2,1,0:T(8,128)}, bf16[4,4,2,32,768]{4,3,2,1,0:T(8,128)(2,1)}, f32[2,32,512]{2,1,0:T(8,128)}, ...) custom-call(bf16[3,1024,1024]{2,1,0:T(8,128)(2,1)} %get-tuple-element.67.h, ...), custom_call_target="tpu_custom_call" | custom-call | tf_op jit(solution)/shard_map/back_in/pallas_call | solution.py:674
  352.7 8.5 %finish.1 = (bf16[3,512,1024]{2,1,0:T(8,128)(2,1)}, f32[3,512,1024]{2,1,0:T(8,128)}, f32[1,64]{1,0:T(1,128)}, f32[1,64]{1,0:T(1,128)}, f32[64,128]{1,0:T(8,128)}...) custom-call(bf16[3,512,1024]{2,1,0:T(8,128)(2,1)} %get-tuple-element, ...), custom_call_target="tpu_custom_call" | custom-call | tf_op jit(solution)/shard_map/finish/pallas_call | solution.py:674

commit v3 on v2

--- a/solution.py
+++ b/solution.py
@@ -340,9 +340,8 @@
 TILE = 256
 SPAN = 2
 CHUNK = 512
-UNIT = 1536
 EARLY = 640
-JOBS = ((), ((0, 768), (0, 384), (1, 768)), ((1, 384),), ((1, 384), (2, 768), (2, 768)))
+JOBS = (((0, 768), (0, 384), (1, 768)), ((1, 768), (2, 768), (2, 384), (2, 384)))
 RATE = 0.019
 VMEM_BYTES = 62 << 20
 MESH = pl.DeviceIdType.MESH
@@ -401,8 +400,10 @@
 
 
 class Gather:
-    def __init__(self, source, whole, send, recv, local=None):
+
+    def __init__(self, source, whole, send, recv, local=None, near=None):
         self.source, self.whole, self.send, self.recv, self.local = source, whole, send, recv, local
+        self.near = near
         self.me = lax.axis_index("dp")
         self.far = far_count()
         self.each = whole.shape[0] // lax.axis_size("dp")
@@ -422,7 +423,9 @@
 
     def first(self, k, part, bit):
         index = self.far - 1 + 4 * k + 2 * part + bit - 1
-        if k == 0:
+        if self.near is not None:
+            source = near_block(self.near, k, part * self.half, self.half)
+        elif k == 0:
             source = self.source.at[pl.ds(part * self.half, self.half)]
         else:
             source = self.piece(4 * k, part)
@@ -448,21 +451,33 @@
         remote(landing, landing, self.send.at[index], self.recv.at[index], dp_peer(bits)).wait_recv()
 
     def kept(self):
-        return pltpu.make_async_copy(self.source, self.block(0), self.local)
+        if self.near is None:
+            return [pltpu.make_async_copy(self.source, self.block(0), self.local)]
+        sems = [self.local] + [self.recv.at[k - 1] for k in range(1, self.far)]
+        return [
+            pltpu.make_async_copy(near_block(self.near, k, 0, self.each), self.block(4 * k), sems[k])
+            for k in range(self.far)
+        ]
 
     def pass_on(self, k):
         for part, bit in ((0, 2), (1, 1), (0, 1), (1, 2)):
             self.start(self.first(k, part, bit))
 
+    def begin_far(self):
+        if self.local is not None:
+            for copy in self.kept():
+                copy.start()
+        if self.near is None:
+            for k in range(1, self.far):
+                self.start(self.along(k))
+
     def begin(self):
-        if self.local is not None:
-            self.kept().start()
-        for k in range(1, self.far):
-            self.start(self.along(k))
+        self.begin_far()
         self.pass_on(0)
 
     def spread(self, k):
-        self.arrived(self.along(k))
+        if self.near is None:
+            self.arrived(self.along(k))
         self.pass_on(k)
 
     def turn(self, k):
@@ -477,41 +492,96 @@
             self.arrived(self.first(k, 1, 2))
             for part in range(2):
                 self.arrived(self.second(k, part))
-        for k in range(1, self.far):
-            self.sent(self.along(k))
+        if self.near is None:
+            for k in range(1, self.far):
+                self.sent(self.along(k))
         for k in range(self.far):
             for part in range(2):
                 for bit in (1, 2):
                     self.sent(self.first(k, part, bit))
                 self.sent(self.second(k, part))
         if self.local is not None:
-            self.kept().wait()
+            for copy in self.kept():
+                copy.wait()
 
     def plan(self, start):
         along = RATE * self.whole.shape[1]
         far = 2 * along / 3
         events = [(start, self.begin)]
         for k in range(1, self.far):
-            at = start + 3.0 + far * (0.4 + 0.6 * k / (self.far - 1))
+            at = start + 1.0 + far * (0.4 + 0.6 * k / (self.far - 1))
             events.append((at, functools.partial(self.spread, k)))
         for k in range(self.far):
-            at = start + 6.0 + far * (0.4 + 0.6 * k / (self.far - 1)) + along / 4
+            at = start + 2.0 + far * (0.4 + 0.6 * k / (self.far - 1)) + along / 4
             events.append((at, functools.partial(self.turn, k)))
         return events
 
 
+    def plan_near(self, far_start, start):
+        along = RATE * self.whole.shape[1]
+        events = [(far_start, self.begin_far)]
+        events += [(start, functools.partial(self.pass_on, 0))]
+        events += [(start + 0.001 * k, functools.partial(self.spread, k)) for k in range(1, self.far)]
+        for k in range(self.far):
+            events.append((start + 2.0 + along * (k + 1) / 6, functools.partial(self.turn, k)))
+        return events
+
+
+def near_block(near, k, first, rows):
+    each = near.shape[0] // far_count()
+    start = (lax.div(lax.axis_index("dp"), 4) ^ k) * each + first
+    return near.at[pl.ds(pl.multiple_of(start, rows), rows)]
+
+
+class NearGather:
+
+    def __init__(self, source, near, send, recv, local):
+        self.source, self.near, self.send, self.recv, self.local = source, near, send, recv, local
+        self.each = source.shape[0]
+
+    def copies(self):
+        mine = near_block(self.near, 0, 0, self.each)
+        made = [pltpu.make_async_copy(self.source, mine, self.local)]
+        for k in range(1, far_count()):
+            made.append(remote(self.source, mine, self.send.at[k - 1], self.recv.at[k - 1], dp_peer(4 * k)))
+        return made
+
+    def begin(self):
+        for copy in self.copies():
+            copy.start()
+
+    def finish(self):
+        for k in range(1, far_count()):
+            landing = near_block(self.near, k, 0, self.each)
+            remote(landing, landing, self.send.at[k - 1], self.recv.at[k - 1], dp_peer(4 * k)).wait_recv()
+        for copy in self.copies()[1:]:
+            copy.wait_send()
+        self.copies()[0].wait()
+
+
 class Plan:
 
-    def __init__(self, step, steps, places, step_us):
-        self.step, self.steps, self.places, self.step_us = step, steps, places, step_us
+    def __init__(self, step, steps, places, step_us, clock=None):
+        self.step, self.steps, self.places = step, steps, places
+        self.clock = clock or [at * step_us / places for at in range(steps * places)]
         self.events = {}
+        self.tail = []
         self.ends = []
 
-    def add(self, events, end):
-        for time, action in events:
-            index = min(int(time * self.places / self.step_us), self.steps * self.places - 1)
-            self.events.setdefault(divmod(index, self.places), []).append((time, action))
+    def add(self, events, end, latest=None, earliest=0):
+        for at, (time, action) in enumerate(events):
+            index = sum(tick < time for tick in self.clock) if at else sum(tick <= time for tick in self.clock) - 1
+            index = max(index, earliest)
+            if latest is not None:
+                index = min(index, latest)
+            if index < self.steps * self.places:
+                self.events.setdefault(divmod(index, self.places), []).append((time, action))
+            else:
+                self.tail.append((time, action))
         self.ends.append(end)
+
+    def put(self, step, time, action):
+        self.events.setdefault((step, 0), []).append((time, action))
 
     def at(self, place):
         for key in sorted(self.events):
@@ -523,6 +593,8 @@
                         action()
 
     def finish(self):
+        for _, action in sorted(self.tail, key=lambda event: event[0]):
+            action()
         for end in self.ends:
             end()
 
@@ -635,7 +707,7 @@
 
     def plan(self, start):
         along = RATE * self.mine.shape[3]
-        times = (start, start + 4 + 2 * along / 3, start + 8 + along)
+        times = (start, start + 1.5 + 2 * along / 3, start + 3 + along)
         return list(zip(times, (self.begin, self.second, self.third)))
 
 
@@ -901,7 +973,7 @@
 
 
 def attend_kernel(
-    jobs, lengths, qkv, grad_own, slabs, mix_ref, inv_ref, grad_other, whole_out, unit, mask, queries, values, total, *sems
+    jobs, lengths, qkv, grad_own, slabs, mix_ref, inv_ref, grad_other, unit, mask, queries, values, total, *sems
 ):
     m = pl.program_id(0)
     group = qkv.shape[1]
@@ -913,9 +985,9 @@
     def swap():
         return remote(grad_own, grad_other, sems[0], sems[1], sibling())
 
-    plan = Plan(m, lengths.shape[0], pairs, 8.0)
+    plan = Plan(m, lengths.shape[0], pairs, 9.5)
     plan.add([(0.0, lambda: swap().start())], lambda: swap().wait())
-    add_gathers(plan, [(slabs, (whole_out, unit)[w], *job) for w, *job in jobs], sems[2:])
+    add_gathers(plan, [(slabs, unit, *job) for job in jobs], sems[2:])
 
     @pl.when(m == 0)
     def _():
@@ -964,12 +1036,12 @@
     return pl.BlockSpec(lengths.shape, lambda *_: (0, 0), memory_space=pltpu.SMEM)
 
 
-def attend_all(qkv, lengths, out_grad, slabs, out_columns, jobs):
+def attend_all(qkv, lengths, out_grad, slabs, jobs):
     micro, group, columns = qkv.shape
     dim = out_grad.shape[2]
     wide = columns - 256
     dma = pltpu.SemaphoreType.DMA
-    unit = sum(job[3] for job in jobs if job[0])
+    unit = sum(job[2] for job in jobs)
     return call(
         functools.partial(attend_kernel, jobs),
         "attend",
@@ -981,13 +1053,11 @@
             pl.BlockSpec((1, wide // 128, 8, group), lambda m: (m, 0, 0, 0)),
             anywhere(),
             anywhere(),
-            anywhere(),
         ],
         [
             jax.ShapeDtypeStruct((micro, group, wide), BF16),
             jax.ShapeDtypeStruct((micro, wide // 128, 8, group), F32),
             jax.ShapeDtypeStruct(out_grad.shape, BF16),
-            jax.ShapeDtypeStruct((dim, out_columns), BF16),
             jax.ShapeDtypeStruct((dim, unit), BF16),
         ],
         [
@@ -1003,24 +1073,33 @@
     )
 
 
-def attend_back_kernel(jobs, lengths, qkv, mix_ref, inv_ref, dmix_ref, *refs):
+def attend_back_kernel(jobs, lengths, qkv, mix_ref, inv_ref, d_own, d_other, weights, *refs):
     sources, refs = refs[: len(jobs)], refs[len(jobs) :]
-    dqkv, refs = refs[0], refs[1:]
+    (dqkv, grads), refs = refs[:2], refs[2:]
     outs, refs = refs[: len(jobs)], refs[len(jobs) :]
     (mask, queries, queries_t, keys, douts, douts_t, deltas, dv_t, dk_t, dq), refs = refs[:10], refs[10:]
+    (d, dmix, grad_total, rounded, out_sem), refs = refs[:5], refs[5:]
     m = pl.program_id(0)
     group = qkv.shape[1]
     tiles = group // TILE
     pairs = mix_ref.shape[2] // 128
     lane = lax.broadcasted_iota(jnp.int32, (group, 128), 1)
     zero = jnp.zeros((), BF16)
-    plan = Plan(m, lengths.shape[0], pairs, 15.2)
+    plan = Plan(m, lengths.shape[0], pairs, 18.0)
     add_scatters(plan, jobs, sources, outs, refs)
 
     @pl.when(m == 0)
     def _():
         greet(dp_peers())
-
+        grad_total[...] = jnp.zeros_like(grad_total)
+
+    plan.at(0)
+    rows = d_own.shape[1]
+    core = lax.axis_index("tensor")
+    d[pl.ds(pl.multiple_of(core * rows, rows), rows)] = d_own[0]
+    d[pl.ds(pl.multiple_of((1 - core) * rows, rows), rows)] = d_other[0]
+    dmix[...] = mm(d[...], weights[...]).astype(BF16)
+    grad_total[...] += mm(d[...], mix_ref[0], TN)
     fill_mask(mask, lengths, m)
     queries_t[...] = (qkv[0, :, :128].astype(F32) * 0.5).T.astype(BF16)
     query = qkv[0, :, :128] * jnp.asarray(0.25, BF16)
@@ -1032,7 +1111,7 @@
         inverse = jnp.concatenate(
             [jnp.broadcast_to(inv_ref[0, pair, s : s + 1, :], (VD, group)) for s in range(2)], 0
         ).T
-        dout_low = (dmix_ref[0, :, lanes].astype(F32) * inverse).astype(BF16)
+        dout_low = (dmix[:, lanes].astype(F32) * inverse).astype(BF16)
         dout = dout_low.astype(F32)
         douts_t[now] = dout.T.astype(BF16)
         product = dout * mix_ref[0, :, lanes].astype(F32)
@@ -1045,7 +1124,7 @@
             delta = jnp.sum(jnp.where(mine, product, 0.0), axis=1, keepdims=True)
             deltas[now, side] = jnp.broadcast_to(delta, (group, 128))
         for j in range(tiles):
-            if j == 0:
+            if j == 0 and pair:
                 plan.at(pair)
             i = min(tiles, j + SPAN + 1)
             tall = (i - j) * TILE
@@ -1076,14 +1155,19 @@
 
     @pl.when(m == pl.num_programs(0) - 1)
     def _():
+        rounded[...] = grad_total[...].astype(BF16).reshape(rounded.shape)
+        write = pltpu.make_async_copy(rounded, grads, out_sem)
+        write.start()
         plan.finish()
-
-
-def attend_back(qkv, mix, inverse, dmix, lengths, sources, jobs):
+        write.wait()
+
+
+def attend_back(qkv, mix, inverse, d_own, d_other, weights, lengths, sources, jobs):
     micro, group, columns = qkv.shape
     wide = columns - 256
-    dim = sources[0].shape[3] * 2 * lax.axis_size("dp")
+    rows, dim = d_own.shape[1:]
     shapes, specs = scatter_outs(jobs, dim)
+    grads = grad_shape(dim, wide)
     pair_rows = pltpu.VMEM((2, 2, group, 128), BF16)
     return call(
         functools.partial(attend_back_kernel, jobs),
@@ -1095,11 +1179,13 @@
             whole_group(columns, group),
             whole_group(wide, group),
             pl.BlockSpec((1, wide // 128, 8, group), lambda m: (m, 0, 0, 0)),
-            whole_group(wide, group),
+            whole_group(dim, rows),
+            whole_group(dim, rows),
+            once((dim, wide)),
         ]
         + [anywhere()] * len(jobs),
-        [whole_group(columns, group)] + specs,
-        [jax.ShapeDtypeStruct((micro, group, columns), BF16)] + shapes,
+        [whole_group(columns, group), anywhere()] + specs,
+        [jax.ShapeDtypeStruct((micro, group, columns), BF16), grads] + shapes,
         [
             pltpu.VMEM((group // TILE, TILE * (SPAN + 1), TILE), F32),
             pair_rows,
@@ -1111,21 +1197,28 @@
             pltpu.VMEM((2, 128, group), F32),
             pltpu.VMEM((128, group), F32),
             pltpu.VMEM((group, 128), F32),
+            pltpu.VMEM((group, dim), BF16),
+            pltpu.VMEM((group, wide), BF16),
+            pltpu.VMEM((dim, wide), F32),
+            pltpu.VMEM(grads.shape, BF16),
+            pltpu.SemaphoreType.DMA,
         ]
         + scatters_scratch(jobs, dim),
-        (lengths, qkv, mix, inverse, dmix, *sources),
+        (lengths, qkv, mix, inverse, d_own, d_other, weights, *sources),
     )
 
 
 def out_kernel(
-    jobs, mix_own, mix_other, x, weights, gains, slabs, resid_out, h_out, h_other, unit,
+    jobs, near_job, mix_own, mix_other, x, weights, gains, slabs, resid_out, h_out, h_other, unit, near,
     parts, sent, got, h_sent, send, recv, *sems,
 ):
     i = pl.program_id(0)
     count, rows = got.shape[0], got.shape[1]
     per = h_other.shape[1] // rows
     plan = Plan(i, 2 * count, 1, 0.95)
-    add_gathers(plan, [(slabs, unit, *job) for job in jobs], sems)
+    add_gathers(plan, [(slabs, unit, *job) for job in jobs], sems[3:])
+    ahead = NearGather(slabs.at[:, pl.ds(*near_job)], near, *sems[:3])
+    plan.add([(2.0, ahead.begin)], ahead.finish)
 
     def swap(k):
         return remote(sent.at[k], got.at[k], send.at[k], recv.at[k], sibling())
@@ -1167,7 +1260,7 @@
             swap_h(k).wait()
 
 
-def out_project(mix, x, weights, gains, slabs, jobs, rows=256):
+def out_project(mix, x, weights, gains, slabs, jobs, near_job, rows=256):
     micro, own_rows, dim = x.shape
     wide = mix.shape[2]
     per = own_rows // rows
@@ -1176,7 +1269,7 @@
     shape = jax.ShapeDtypeStruct((micro, own_rows, dim), BF16)
     buffer = pltpu.VMEM((count, rows, dim), BF16)
     return call(
-        functools.partial(out_kernel, jobs),
+        functools.partial(out_kernel, jobs, near_job),
         "out_project",
         3,
         2 * count,
@@ -1184,294 +1277,256 @@
             core_block(wide, per, rows, False, count - 1),
             core_block(wide, per, rows, True, count - 1),
             late,
-            once(weights.shape),
+            once((dim, wide)),
             once((8, dim)),
             anywhere(),
         ],
-        [late, late, anywhere(), anywhere()],
-        [shape, shape, shape, jax.ShapeDtypeStruct((dim, sum(job[2] for job in jobs)), BF16)],
+        [late, late, anywhere(), anywhere(), anywhere()],
+        [
+            shape,
+            shape,
+            shape,
+            jax.ShapeDtypeStruct((dim, sum(job[2] for job in jobs)), BF16),
+            jax.ShapeDtypeStruct((dim // 4, near_job[1]), BF16),
+        ],
         [pltpu.VMEM((count, rows, dim), F32), buffer, buffer, buffer]
         + half_sems(2 * count)
+        + half_sems(far_count() - 1)
+        + [pltpu.SemaphoreType.DMA]
         + gather_sems() * len(jobs),
         (mix, mix, x, weights, gains, slabs),
     )
 
 
-FEED_US = 6.8
-
-
-def feed_kernel(steps, width, loads, first, last, gathers, scatters, h_own, h_other, g_own, g_other, *refs):
+FEED_US = (5.2, 6.4, 7.2)
+GATHER_AT = ((0.0, 0.0), (0.5, 26.0))
+SCATTER_AT = (44.0, 59.0, 71.0, 86.0)
+BACK_US = 2.4
+OUT_PIECE = 512
+IN_PIECE = 384
+
+
+def feed_kernel(
+    steps, widths, loads, cuts, jobs, h_own, h_other, g_own, g_other, unit_0, unit_1, near, slabs,
+    resid, g_late, resid_end, g_end, gains, mixed_out, d_out, d_other, *refs,
+):
     def take(number):
         nonlocal refs
         taken, refs = refs[:number], refs[number:]
         return taken
 
-    weights = take(len(loads))
-    before = None if first else take(4)
-    slabs = take(1)[0] if gathers else None
-    sources = take(len(scatters))
-    if last:
-        resid, g_late, resid_end, g_end, gains, mixed_out, d_out, d_other = take(8)
-    else:
-        out_own, out_other, dm_own, dm_other = take(4)
-    grads = take(1)[0]
-    unit = take(1)[0] if gathers else None
-    outs = take(len(scatters))
-    slab, total, h, g, hidden_s, dgu_s, rounded, load_sems, out_sem = take(9)
+    chunks = len(widths)
+    grads = take(chunks)
+    units = take(chunks - 1)
+    outs = take(len(jobs))
+    slab_a, slab_b, total, h, g, hidden_s, dgu_s = take(7)
+    out_own, out_other, dm_own, dm_other, dm_got, out_got, d_sent, mixed_s = take(8)
+    load_sems, write_sems, send, recv, local = take(5)
     i = pl.program_id(0)
     rows = h_own.shape[1]
-    plan = Plan(i, steps, 1, FEED_US * width / 512)
-    add_gathers(plan, [(slabs, unit, *job) for job in gathers], take(3 * len(gathers)))
-    busy = sum(RATE * job[2] for job in gathers)
-    add_scatters(plan, scatters, sources, outs, take(SCATTER_REFS * len(scatters)), busy)
-    if last:
-        dm_sent, dm_got, out_sent, out_got, dm_kept, out_kept, d_sent, mixed_s, send, recv, local = take(11)
-        per = d_other.shape[1] // rows
-
-        def place(ref, k):
-            return ref.at[lax.div(k, per), pl.ds(pl.multiple_of(lax.rem(k, per) * rows, rows), rows)]
-
-        def swaps(k):
-            return [
-                remote(dm_sent.at[k], dm_got.at[k + 1], send.at[3 * k], recv.at[3 * k], sibling()),
-                remote(out_sent.at[k], out_got.at[k + 1], send.at[3 * k + 1], recv.at[3 * k + 1], sibling()),
-            ]
-
-        def results(k):
-            return [
-                remote(d_sent.at[k + 1], place(d_other, k), send.at[3 * k + 2], recv.at[3 * k + 2], sibling()),
-                pltpu.make_async_copy(d_sent.at[k + 1], place(d_out, k), local.at[2 * k]),
-                pltpu.make_async_copy(mixed_s.at[k + 1], place(mixed_out, k), local.at[2 * k + 1]),
-            ]
-
-        def finish_part(slot, resid, g_late):
-            values = resid[0].astype(F32)
-            mixed_s[slot] = add(values, out_kept[lax.rem(slot, 2)], out_got[slot]).astype(BF16)
-            scaled = add(dm_kept[lax.rem(slot, 2)], dm_got[slot]) * gains[1:2]
-            d_sent[slot] = (g_late[0].astype(F32) + norm_slope(values, scaled)).astype(BF16)
-
-    def copies():
+    per = d_other.shape[1] // rows
+    weights = [(slab_a, slab_b)[chunk % 2] for chunk in range(chunks)]
+
+    def place(ref, k):
+        return ref.at[lax.div(k, per), pl.ds(pl.multiple_of(lax.rem(k, per) * rows, rows), rows)]
+
+    def swaps(k):
+        return [
+            remote(dm_other.at[k], dm_got.at[k + 1], send.at[3 * k], recv.at[3 * k], sibling()),
+            remote(out_other.at[k], out_got.at[k + 1], send.at[3 * k + 1], recv.at[3 * k + 1], sibling()),
+        ]
+
+    def results(k):
+        return [
+            remote(d_sent.at[k + 1], place(d_other, k), send.at[3 * k + 2], recv.at[3 * k + 2], sibling()),
+            pltpu.make_async_copy(d_sent.at[k + 1], place(d_out, k), local.at[2 * k]),
+            pltpu.make_async_copy(mixed_s.at[k + 1], place(mixed_out, k), local.at[2 * k + 1]),
+        ]
+
+    def finish_part(slot, before, resid, g_late):
+        values = resid[0].astype(F32)
+        mixed_s[slot] = add(values, out_own[before], out_got[slot]).astype(BF16)
+        scaled = add(dm_own[before], dm_got[slot]) * gains[1:2]
+        d_sent[slot] = (g_late[0].astype(F32) + norm_slope(values, scaled)).astype(BF16)
+
+    def copies(chunk):
         made = []
-        for at, (ref, (source, target, columns)) in enumerate(zip(weights, loads)):
-            cut = ref.at[:, pl.ds(source, columns)]
-            made.append(pltpu.make_async_copy(cut, slab.at[:, pl.ds(target, columns)], load_sems.at[at]))
+        sources = loads if chunk == 0 else [(0, 0, 3 * widths[chunk])]
+        for at, (source, target, columns) in enumerate(sources):
+            ref = (unit_0, unit_1)[at] if chunk == 0 else units[chunk - 1]
+            tall = slab_a.shape[0] // 4
+            for part in range(4):
+                rows_at = pl.ds(part * tall, tall)
+                cut = ref.at[rows_at, pl.ds(source, columns)]
+                target_at = weights[chunk].at[rows_at, pl.ds(target, columns)]
+                made.append(pltpu.make_async_copy(cut, target_at, load_sems.at[chunk, at, part]))
         return made
+
+    def writes(chunk):
+        made = []
+        far, low, parts, half, columns = grads[chunk].shape
+        for at in range(far * low * parts):
+            source = weights[chunk].at[pl.ds(at * half, half), pl.ds(0, columns)]
+            target = grads[chunk].at[at // (low * parts), at // parts % low, at % parts]
+            made.append(pltpu.make_async_copy(source, target, write_sems.at[chunk, at]))
+        return made
+
+    def start_all(made):
+        for copy in made:
+            copy.start()
+
+    def wait_all(made):
+        for copy in made:
+            copy.wait()
+
+    clock = []
+    for chunk in range(chunks):
+        start = clock[-2] + FEED_US[chunk - 1] if clock else 0.0
+        clock += [start + FEED_US[chunk] * (step + part) for step in range(steps) for part in (0, 0.65)]
+    plan = Plan(i, chunks * steps, 2, None, clock)
+    for chunk in range(1, chunks):
+        first, width = cuts[chunk - 1]
+        gather = Gather(slabs.at[:, pl.ds(first, width)], units[chunk - 1], *take(3), near if chunk == 1 else None)
+        plan.add(gather.plan_near(*GATHER_AT[chunk - 1]), lambda: None, 2 * chunk * steps - 2)
+        plan.put(chunk * steps - 1, 1000.0, gather.finish)
+        plan.put(chunk * steps - 1, 1001.0, lambda chunk=chunk: start_all(copies(chunk)))
+    for at, (chunk, (first, width)) in enumerate(jobs):
+        scatter = Scatter(grads[chunk], first, outs[at], take(SCATTER_REFS))
+        plan.add(scatter.plan(SCATTER_AT[at]), scatter.finish, None, 2 * (chunk + 1) * steps + 2)
+    for chunk in range(chunks - 1):
+        plan.put((chunk + 1) * steps + 1, -1.0, lambda chunk=chunk: wait_all(writes(chunk)))
 
     @pl.when(i == 0)
     def _():
-        for copy in copies():
-            copy.start()
-        if last:
-            zeros = jnp.zeros(dm_kept.shape[1:], BF16)
-            for ref in (dm_got, out_got, dm_kept, out_kept):
-                ref[0] = zeros
-        greet(dp_peers() + ([sibling()] if last else []))
+        start_all(copies(0))
+        zeros = jnp.zeros(dm_got.shape[1:], BF16)
+        dm_got[0] = zeros
+        out_got[0] = zeros
+        greet(dp_peers() + [sibling()])
 
     plan.at(0)
-
-    @pl.when(i == 0)
-    def _():
-        total[...] = jnp.zeros_like(total)
-        for copy in copies():
-            copy.wait()
-
-    h[:rows], h[rows:] = h_other[0], h_own[0]
-    g[:rows], g[rows:] = g_other[0], g_own[0]
     half = jnp.asarray(0.5, BF16)
     one = jnp.asarray(1.0, BF16)
-    for at, wide in chunk_slices(width):
-        both = slice(2 * at, 2 * (at + wide))
-        gate_up = mm(h[...], slab[:, both]).astype(BF16)
-        d_hidden = mm(g[...], slab[:, 2 * width + at : 2 * width + at + wide]).astype(BF16)
-        gate, up = gate_up[:, :wide], gate_up[:, wide:]
-        sigmoid = half * jnp.tanh(half * gate) + half
-        silu = gate * sigmoid
-        hidden_s[:, at : at + wide] = silu * up
-        d_gate = d_hidden * up * (sigmoid + silu * (one - sigmoid))
-        dgu_s[:, both] = jnp.concatenate([d_gate, d_hidden * silu], 1)
-    dim = slab.shape[0]
-    for at in range(0, dim, 512):
-        cut = slice(at, at + 512)
-        out = mm(hidden_s[...], slab[cut, 2 * width :], NT)
-        dm = mm(dgu_s[...], slab[cut, : 2 * width], NT)
-        parts_now = []
-        for at_before, value in enumerate((out[rows:], out[:rows], dm[rows:], dm[:rows])):
-            if not first:
-                value = value + before[at_before][0, :, cut].astype(F32)
-            parts_now.append(value.astype(BF16))
+    dim = slab_a.shape[0]
+
+    def chunk_step(chunk):
+        slab, width, last = weights[chunk], widths[chunk], chunk == chunks - 1
+        j = i - chunk * steps
+
+        @pl.when(j == 0)
+        def _():
+            total[:, : 3 * width] = jnp.zeros((dim, 3 * width), F32)
+            wait_all(copies(chunk))
+
+        h[:rows], h[rows:] = h_other[0], h_own[0]
+        g[:rows], g[rows:] = g_other[0], g_own[0]
+        for at, wide in chunk_slices(width):
+            both = slice(2 * at, 2 * (at + wide))
+            gate_up = mm(h[...], slab[:, both]).astype(BF16)
+            d_hidden = mm(g[...], slab[:, 2 * width + at : 2 * width + at + wide]).astype(BF16)
+            gate, up = gate_up[:, :wide], gate_up[:, wide:]
+            sigmoid = half * jnp.tanh(half * gate) + half
+            silu = gate * sigmoid
+            hidden_s[:, at : at + wide] = silu * up
+            d_gate = d_hidden * up * (sigmoid + silu * (one - sigmoid))
+            dgu_s[:, both] = jnp.concatenate([d_gate, d_hidden * silu], 1)
+        for at in range(0, dim, 512):
+            cut = slice(at, at + 512)
+            out = mm(hidden_s[:, :width], slab[cut, 2 * width : 3 * width], NT)
+            dm = mm(dgu_s[:, : 2 * width], slab[cut, : 2 * width], NT)
+            for ref, value in ((out_own, out[rows:]), (out_other, out[:rows]), (dm_own, dm[rows:]), (dm_other, dm[:rows])):
+                if chunk:
+                    value = value + ref[j, :, cut].astype(F32)
+                ref[j, :, cut] = value.astype(BF16)
         if last:
-            out_sent[i, :, cut], dm_sent[i, :, cut] = parts_now[1], parts_now[3]
-            kept = lax.rem(i + 1, 2)
-            out_kept[kept, :, cut], dm_kept[kept, :, cut] = parts_now[0], parts_now[2]
-        else:
-            out_own[0, :, cut], out_other[0, :, cut] = parts_now[0], parts_now[1]
-            dm_own[0, :, cut], dm_other[0, :, cut] = parts_now[2], parts_now[3]
-    if last:
-        for swap in swaps(i):
-            swap.start()
-
-        @pl.when(i > 0)
+            start_all(swaps(j))
+
+            @pl.when(j > 0)
+            def _():
+                for swap in swaps(j - 1):
+                    swap.wait_recv()
+
+            finish_part(j, jnp.maximum(j - 1, 0), resid, g_late)
+        plan.at(1)
+        total[:, : 2 * width] += mm(h[...], dgu_s[:, : 2 * width], TN)
+        total[:, 2 * width : 3 * width] += mm(g[...], hidden_s[:, :width], TN)
+        if last:
+
+            @pl.when(j > 0)
+            def _():
+                start_all(results(j - 1))
+
+        @pl.when(j == steps - 1)
         def _():
-            for swap in swaps(i - 1):
-                swap.wait_recv()
-
-        finish_part(i, resid, g_late)
-    total[:, : 2 * width] += mm(h[...], dgu_s[...], TN)
-    total[:, 2 * width :] += mm(g[...], hidden_s[...], TN)
-    if last:
-
-        @pl.when(i > 0)
-        def _():
-            for copy in results(i - 1):
-                copy.start()
-
-    @pl.when(i == steps - 1)
-    def _():
-        rounded[...] = total[...].astype(BF16).reshape(rounded.shape)
-        write = pltpu.make_async_copy(rounded, grads, out_sem)
-        write.start()
-        if last:
-            for swap in swaps(steps - 1):
-                swap.wait_recv()
-            finish_part(steps, resid_end, g_end)
-            for copy in results(steps - 1):
-                copy.start()
-        plan.finish()
-        if last:
-            for k in range(steps):
-                for copy in swaps(k):
-                    copy.wait_send()
-                for copy in results(k):
-                    copy.wait()
-        write.wait()
-
-
-def feed(number, rows_in, loads, width, before, slabs, gathers, sources, scatters, last=None, rows=256):
+            slab[:, : 3 * width] = total[:, : 3 * width].astype(BF16)
+            start_all(writes(chunk))
+            if last:
+                for swap in swaps(steps - 1):
+                    swap.wait_recv()
+                finish_part(steps, steps - 1, resid_end, g_end)
+                start_all(results(steps - 1))
+                plan.finish()
+                for k in range(steps):
+                    for copy in swaps(k):
+                        copy.wait_send()
+                    wait_all(results(k))
+                wait_all(writes(chunk))
+
+    for chunk in range(chunks):
+
+        @pl.when((i >= chunk * steps) & (i < (chunk + 1) * steps))
+        def _(chunk=chunk):
+            chunk_step(chunk)
+
+
+def feed(rows_in, unit_0, unit_1, near, loads, widths, slabs, cuts, jobs, resid, gains, rows=256):
     micro, own_rows, dim = rows_in[0].shape
-    columns = 3 * width
     per = own_rows // rows
     steps = micro * per
-    part = part_block(dim, per, rows)
+    chunks = len(widths)
+
+    def part_at(lag):
+        def place(i):
+            k = lax.rem(i, steps) if lag == 0 else jnp.clip(i - (chunks - 1) * steps - lag, 0, steps - 1)
+            return lax.div(k, per), lax.rem(k, per), 0
+
+        return pl.BlockSpec((1, rows, dim), place)
+
+    part, late = part_at(0), part_at(1)
+    end = pl.BlockSpec((1, rows, dim), lambda i: (micro - 1, per - 1, 0), pipeline_mode=pl.Buffered(1))
     shape = jax.ShapeDtypeStruct((micro, own_rows, dim), BF16)
-    grads = grad_shape(dim, columns)
-    first = before is None
-    in_specs = [part] * 4 + [anywhere()] * len(loads)
-    operands = list(rows_in) + [load[0] for load in loads]
-    scratch = [
-        pltpu.VMEM((dim, columns), BF16),
-        pltpu.VMEM((dim, columns), F32),
-        pltpu.VMEM((2 * rows, dim), BF16),
-        pltpu.VMEM((2 * rows, dim), BF16),
-        pltpu.VMEM((2 * rows, width), BF16),
-        pltpu.VMEM((2 * rows, 2 * width), BF16),
-        pltpu.VMEM(grads.shape, BF16),
-        pltpu.SemaphoreType.DMA((len(loads),)),
-        pltpu.SemaphoreType.DMA,
-    ]
-    if not first:
-        in_specs += [part] * 4
-        operands += list(before)
-    if gathers:
-        in_specs.append(anywhere())
-        operands.append(slabs)
-    in_specs += [anywhere()] * len(scatters)
-    operands += sources
-    if last:
-        resid, gains = last
-        late = part_block(dim, per, rows, 1, steps - 1)
-        end = pl.BlockSpec((1, rows, dim), lambda i: (micro - 1, per - 1, 0), pipeline_mode=pl.Buffered(1))
-        in_specs += [late, late, end, end, once((8, dim))]
-        operands += [resid, rows_in[2], resid, rows_in[2], gains]
-        out_specs, out_shape = [anywhere()] * 4, [shape] * 3 + [grads]
-    else:
-        out_specs, out_shape = [part] * 4 + [anywhere()], [shape] * 4 + [grads]
-    plain = len(out_shape)
-    if gathers:
-        out_specs.append(anywhere())
-        out_shape.append(jax.ShapeDtypeStruct((dim, sum(job[2] for job in gathers)), BF16))
-        scratch += gather_sems() * len(gathers)
-    if scatters:
-        shapes, specs = scatter_outs(scatters, dim)
-        out_specs += specs
-        out_shape += shapes
-        scratch += scatters_scratch(scatters, dim)
-    if last:
-        plain_slots, late_slots = pltpu.VMEM((steps, rows, dim), BF16), pltpu.VMEM((steps + 1, rows, dim), BF16)
-        two_slots = pltpu.VMEM((2, rows, dim), BF16)
-        scratch += [plain_slots, late_slots] * 2 + [two_slots] * 2 + [late_slots] * 2 + half_sems(3 * steps)
-        scratch.append(pltpu.SemaphoreType.DMA((2 * steps,)))
+    grads = [grad_shape(dim, 3 * width) for width in widths]
+    units = [jax.ShapeDtypeStruct((dim, width), BF16) for _, width in cuts]
+    shapes, specs = scatter_outs([job for _, job in jobs], dim)
+    most = max(widths)
+    slots, late_slots = pltpu.VMEM((steps, rows, dim), BF16), pltpu.VMEM((steps + 1, rows, dim), BF16)
+    blocks = grads[0].shape[0] * grads[0].shape[1] * grads[0].shape[2]
     results = call(
-        functools.partial(
-            feed_kernel, steps, width, [load[1:] for load in loads], first, last is not None, gathers, scatters
-        ),
+        functools.partial(feed_kernel, steps, widths, loads, cuts, jobs),
         "feed",
-        number,
-        steps,
-        in_specs,
-        out_specs,
-        out_shape,
-        scratch,
-        operands,
-    )
-    rest = list(results[plain:])
-    unit = rest.pop(0) if gathers else None
-    return results[: plain - 1], results[plain - 1], unit, rest
-
-
-def back_out_kernel(micro, jobs, d_own, d_other, mix, weights, *refs):
-    sources, refs = refs[: len(jobs)], refs[len(jobs) :]
-    (dmix, grads), refs = refs[:2], refs[2:]
-    outs, refs = refs[: len(jobs)], refs[len(jobs) :]
-    (d, total, rounded, out_sem), refs = refs[:4], refs[4:]
-    i = pl.program_id(0)
-    rows = d_own.shape[1]
-    plan = Plan(i, micro, 1, 4.5)
-    add_scatters(plan, jobs, sources, outs, refs)
-
-    @pl.when(i == 0)
-    def _():
-        greet(dp_peers())
-        total[...] = jnp.zeros_like(total)
-
-    plan.at(0)
-    core = lax.axis_index("tensor")
-    d[pl.ds(pl.multiple_of(core * rows, rows), rows)] = d_own[0]
-    d[pl.ds(pl.multiple_of((1 - core) * rows, rows), rows)] = d_other[0]
-    dmix[0] = mm(d[...], weights[...]).astype(BF16)
-    total[...] += mm(d[...], mix[0], TN)
-
-    @pl.when(i == pl.num_programs(0) - 1)
-    def _():
-        rounded[...] = total[...].astype(BF16).reshape(rounded.shape)
-        write = pltpu.make_async_copy(rounded, grads, out_sem)
-        write.start()
-        plan.finish()
-        write.wait()
-
-
-def back_out(d_own, d_other, mix, weights, sources, jobs):
-    micro, rows, dim = d_own.shape
-    columns = mix.shape[2]
-    part = pl.BlockSpec((1, rows, dim), lambda i: (i, 0, 0))
-    grads = grad_shape(dim, columns)
-    shapes, specs = scatter_outs(jobs, dim)
-    return call(
-        functools.partial(back_out_kernel, micro, jobs),
-        "back_out",
-        7,
-        micro,
-        [part, part, whole_group(columns, 2 * rows), once(weights.shape)] + [anywhere()] * len(jobs),
-        [whole_group(columns, 2 * rows), anywhere()] + specs,
-        [jax.ShapeDtypeStruct((micro, 2 * rows, columns), BF16), grads] + shapes,
-        [
+        4,
+        chunks * steps,
+        [part] * 4 + [anywhere()] * 4 + [late, late, end, end, once((8, dim))],
+        [anywhere()] * (3 + chunks + chunks - 1) + specs,
+        [shape] * 3 + grads + units + shapes,
+        [pltpu.VMEM((dim, 3 * most), BF16)] * 2
+        + [
+            pltpu.VMEM((dim, 3 * most), F32),
             pltpu.VMEM((2 * rows, dim), BF16),
-            pltpu.VMEM((dim, columns), F32),
-            pltpu.VMEM(grads.shape, BF16),
-            pltpu.SemaphoreType.DMA,
+            pltpu.VMEM((2 * rows, dim), BF16),
+            pltpu.VMEM((2 * rows, most), BF16),
+            pltpu.VMEM((2 * rows, 2 * most), BF16),
         ]
-        + scatters_scratch(jobs, dim),
-        (d_own, d_other, mix, weights, *sources),
-    )
+        + [slots] * 4
+        + [late_slots] * 4
+        + [pltpu.SemaphoreType.DMA((chunks, 2, 4)), pltpu.SemaphoreType.DMA((chunks, blocks))]
+        + half_sems(3 * steps)
+        + [pltpu.SemaphoreType.DMA((2 * steps,))]
+        + gather_sems() * (chunks - 1)
+        + scatters_scratch([job for _, job in jobs], dim),
+        (*rows_in, unit_0, unit_1, near, slabs, resid, rows_in[2], resid, rows_in[2], gains),
+    )
+    return results[:3], results[3 : 3 + chunks], results[2 + 2 * chunks :]
 
 
 def back_in_kernel(
@@ -1486,11 +1541,11 @@
     (total, sent, got, send, recv, out_sem, rounded, sums, sums_got, sums_sems), refs = refs[:10], refs[10:]
     i = pl.program_id(0)
     m = lax.rem(i, micro)
-    plan = Plan(i, 3 * micro, 1, 2.4)
+    plan = Plan(i, 3 * micro, 1, BACK_US)
     split = SCATTER_REFS * len(out_jobs)
     add_scatters(plan, out_jobs, [grads_last] * len(out_jobs), outs, refs[:split])
     outs = outs[len(out_jobs) :]
-    add_scatters(plan, in_jobs, [grads] * len(in_jobs), outs, refs[split:], 2.4 * micro)
+    add_scatters(plan, in_jobs, [grads] * len(in_jobs), outs, refs[split:], BACK_US * micro)
 
     def swap(k):
         return remote(sent.at[k], got.at[k], send.at[k], recv.at[k], sibling())
@@ -1698,15 +1753,10 @@
 
     begin = [out_columns, out_columns + wide[0], out_columns + wide[0] + wide[1]]
     early = min(EARLY, wide[0])
-    mix, inverse, g_other, whole_out, unit_0 = attend_all(
-        qkv, lengths, out_grad, slabs, out_columns, [(0, 0, 0, out_columns), (1, begin[0], 0, early)]
-    )
-    resid, h_own, h_other, unit_1 = out_project(
-        mix, inputs, whole_out, gain_full, slabs, [(begin[0] + early, 0, wide[0] - early)]
-    )
-
-    def in_pieces(first, width):
-        return [(first + at, at, most) for at, most in pieces_of(width, UNIT)]
+    mix, inverse, g_other, unit_0 = attend_all(qkv, lengths, out_grad, slabs, [(0, 0, begin[0] + early)])
+    resid, h_own, h_other, unit_1, near = out_project(
+        mix, inputs, unit_0, gain_full, slabs, [(begin[0] + early, 0, wide[0] - early)], (begin[1], wide[1])
+    )
 
     feed_jobs, at = [[], [], []], []
     for kernel in JOBS:
@@ -1715,29 +1765,26 @@
             first = sum(w for _, w in feed_jobs[chunk])
             feed_jobs[chunk].append((first, width))
             at[-1].append((chunk, (first, width)))
-
-    def parts(number):
-        return [grads_of[chunk] for chunk, _ in at[number]], [job for _, job in at[number]]
-
-    rows_in = (h_own, h_other, out_grad, g_other)
-    grads_of = [None] * 3
-    loads = [(unit_0, 0, 0, early), (unit_1, 0, early, wide[0] - early)]
-    sums, grads_of[0], unit, _ = feed(4, rows_in, loads, wide[0] // 3, None, slabs, in_pieces(begin[1], wide[1]), [], [])
-    loads = [(unit, 0, 0, wide[1])]
-    sums, grads_of[1], unit, done = feed(
-        5, rows_in, loads, wide[1] // 3, sums, slabs, in_pieces(begin[2], wide[2]), *parts(0)
-    )
-    feed_grads = list(done)
-    loads = [(unit, 0, 0, wide[2])]
-    (mixed_out, d_own, d_other), grads_of[2], _, done = feed(
-        6, rows_in, loads, wide[2] // 3, sums, None, [], *parts(1), (resid, gain_full)
-    )
-    feed_grads += done
-    dmix, grads_out, *done = back_out(d_own, d_other, mix, whole_out, *parts(2))
-    feed_grads += done
-    dqkv, *done = attend_back(qkv, mix, inverse, dmix, lengths, *parts(3))
-    feed_grads += done
-    out_jobs, in_jobs = pieces_of(out_columns, 512), pieces_of(qkv.shape[2], 384)
+    loads = [(out_columns, 0, early), (0, early, wide[0] - early)]
+    (mixed_out, d_own, d_other), grads_of, done = feed(
+        (h_own, h_other, out_grad, g_other),
+        unit_0,
+        unit_1,
+        near,
+        loads,
+        [w // 3 for w in wide],
+        slabs,
+        list(zip(begin[1:], wide[1:])),
+        at[0],
+        resid,
+        gain_full,
+    )
+    found = dict(zip(at[0], done))
+    sources, jobs = [grads_of[chunk] for chunk, _ in at[1]], [job for _, job in at[1]]
+    dqkv, grads_out, *done = attend_back(qkv, mix, inverse, d_own, d_other, unit_0, lengths, sources, jobs)
+    found |= dict(zip(at[1], done))
+    feed_grads = [found[key] for key in sorted(found)]
+    out_jobs, in_jobs = pieces_of(out_columns, OUT_PIECE), pieces_of(qkv.shape[2], IN_PIECE)
     input_grad, gain_sums, _, *done = back_in(
         h_in, dqkv, inputs, d_own, whole_in, gain_full, grads_out, w_in, slabs, feed_grads, feed_jobs, out_jobs, in_jobs
     )

time: 367 us -> 342 us (0.932)
  Pallas kernels: 359 us -> 334 us
    pallas_call x10 -> x7, Pallas kernels: 359 us -> 334 us  [call(): pl.pallas_call(kernel, grid=steps if isinstance(steps, tuple) else (steps...]
where the time goes in v3:
time: 342 us; the launch traced here: 336 us
  Pallas kernels  334 us (98%)
    pallas_call x7, Pallas kernels, call(): pl.pallas_call(kernel, grid=steps if isinstance(steps, tuple) else (steps...  334 us

profile of v3, /device:TPU:0, one launch (start us, length us, event | category | flops | bytes accessed | tf_op | source)
XLA Modules:
  0.0 336.0 jit_solution(16639398175627912984)
XLA Ops:
  0.6 1.3 copy.25
  1.9 34.8 %project.1 = (bf16[3,1024,1024]{2,1,0:T(8,128)(2,1)}, bf16[3,1024,768]{2,1,0:T(8,128)(2,1)}, f32[8,1024]{1,0:T(8,128)}, bf16[1024,768]{1,0:T(8,128)(2,1)}, bf16[64,4736]{1,0:T(8,128)(2,1)}) custom-call(bf16[3,512,1024]{2,1,0:T(8,128)(2,1)} %x.3, bf16[64,128]{1,0:T(8,128)(2,1)} %w_query.3, bf16[64,128]{1,0:T(8,128)(2,1)} %w_key.3, bf16[64,512]{1,0:T(8,128)(2,1)} %w_value.3, ...), custom_call_target="tpu_custom_call" | custom-call | tf_op jit(solution)/shard_map/project/pallas_call | solution.py:746
  36.7 32.7 %attend.1 = (bf16[3,1024,512]{2,1,0:T(8,128)(2,1)}, f32[3,4,8,1024]{3,2,1,0:T(8,128)}, bf16[3,512,1024]{2,1,0:T(8,128)(2,1)}, bf16[1024,1152]{1,0:T(8,128)(2,1)}) custom-call(s32[3,8]{1,0:T(4,128)} %bitcast.13, bf16[3,1024,768]{2,1,0:T(8,128)(2,1)} %get-tuple-element.56.qkv, bf16[3,512,1024]{2,1,0:T(8,128)(2,1)} %g_end.1, ...), custom_call_target="tpu_custom_call" | custom-call | tf_op jit(solution)/shard_map/attend/pallas_call | solution.py:746
  69.4 26.3 %out_project.1 = (bf16[3,512,1024]{2,1,0:T(8,128)(2,1)}, bf16[3,512,1024]{2,1,0:T(8,128)(2,1)}, bf16[3,512,1024]{2,1,0:T(8,128)(2,1)}, bf16[1024,512]{1,0:T(8,128)(2,1)}, bf16[256,1536]{1,0:T(8,128)(2,1)}) custom-call(bf16[3,1024,512]{2,1,0:T(8,128)(2,1)} %get-tuple-element.58.mix_own.mix_other.mix_ref, ...), custom_call_target="tpu_custom_call" | custom-call | tf_op jit(solution)/shard_map/out_project/pallas_call | solution.py:746
  95.7 126.3 %feed.1 = (bf16[3,512,1024]{2,1,0:T(8,128)(2,1)}, bf16[3,512,1024]{2,1,0:T(8,128)(2,1)}, bf16[3,512,1024]{2,1,0:T(8,128)(2,1)}, bf16[4,4,2,32,1152]{4,3,2,1,0:T(...) custom-call(bf16[3,512,1024]{2,1,0:T(8,128)(2,1)} %get-tuple-element, ...), custom_call_target="tpu_custom_call" | custom-call | tf_op jit(solution)/shard_map/feed/pallas_call | solution.py:746
  222.0 64.9 %attend_back.1 = (bf16[3,1024,768]{2,1,0:T(8,128)(2,1)}, bf16[4,4,2,32,512]{4,3,2,1,0:T(8,128)(2,1)}, f32[2,32,768]{2,1,0:T(8,128)}, f32[2,32,768]{2,1,0:T(8,128...) custom-call(s32[3,8]{1,0:T(4,128)} %bitcast.14, bf16[3,1024,768]{2,1,0:T(8,128)(2,1)} %get-tuple-element.56.qkv, ...), custom_call_target="tpu_custom_call" | custom-call | tf_op jit(solution)/shard_map/attend_back/pallas_call | solution.py:746
  286.9 40.3 %back_in.1 = (bf16[3,512,1024]{2,1,0:T(8,128)(2,1)}, f32[2,64,128]{2,1,0:T(8,128)}, bf16[4,4,2,32,768]{4,3,2,1,0:T(8,128)(2,1)}, f32[2,32,512]{2,1,0:T(8,128)}, ...) custom-call(bf16[3,1024,1024]{2,1,0:T(8,128)(2,1)} %get-tuple-element.55.h, ...), custom_call_target="tpu_custom_call" | custom-call | tf_op jit(solution)/shard_map/back_in/pallas_call | solution.py:746
  327.3 8.5 %finish.1 = (bf16[3,512,1024]{2,1,0:T(8,128)(2,1)}, f32[3,512,1024]{2,1,0:T(8,128)}, f32[1,64]{1,0:T(1,128)}, f32[1,64]{1,0:T(1,128)}, f32[64,128]{1,0:T(8,128)}...) custom-call(bf16[3,512,1024]{2,1,0:T(8,128)(2,1)} %get-tuple-element, ...), custom_call_target="tpu_custom_call" | custom-call | tf_op jit(solution)/shard_map/finish/pallas_call | solution.py:746

commit v4 on v3

--- a/solution.py
+++ b/solution.py
@@ -341,6 +341,7 @@
 SPAN = 2
 CHUNK = 512
 EARLY = 640
+AHEAD = 768
 JOBS = (((0, 768), (0, 384), (1, 768)), ((1, 768), (2, 768), (2, 384), (2, 384)))
 RATE = 0.019
 VMEM_BYTES = 62 << 20
@@ -973,7 +974,8 @@
 
 
 def attend_kernel(
-    jobs, lengths, qkv, grad_own, slabs, mix_ref, inv_ref, grad_other, unit, mask, queries, values, total, *sems
+    jobs, near_job, lengths, qkv, grad_own, slabs, mix_ref, inv_ref, grad_other, unit, near,
+    mask, queries, values, total, *sems,
 ):
     m = pl.program_id(0)
     group = qkv.shape[1]
@@ -987,7 +989,9 @@
 
     plan = Plan(m, lengths.shape[0], pairs, 9.5)
     plan.add([(0.0, lambda: swap().start())], lambda: swap().wait())
-    add_gathers(plan, [(slabs, unit, *job) for job in jobs], sems[2:])
+    add_gathers(plan, [(slabs, unit, *job) for job in jobs], sems[5:])
+    ahead = NearGather(slabs.at[:, pl.ds(*near_job)], near, *sems[2:5])
+    plan.add([(12.0, ahead.begin)], ahead.finish)
 
     @pl.when(m == 0)
     def _():
@@ -1036,14 +1040,14 @@
     return pl.BlockSpec(lengths.shape, lambda *_: (0, 0), memory_space=pltpu.SMEM)
 
 
-def attend_all(qkv, lengths, out_grad, slabs, jobs):
+def attend_all(qkv, lengths, out_grad, slabs, jobs, near_job):
     micro, group, columns = qkv.shape
     dim = out_grad.shape[2]
     wide = columns - 256
     dma = pltpu.SemaphoreType.DMA
     unit = sum(job[2] for job in jobs)
     return call(
-        functools.partial(attend_kernel, jobs),
+        functools.partial(attend_kernel, jobs, near_job),
         "attend",
         2,
         micro,
@@ -1053,12 +1057,14 @@
             pl.BlockSpec((1, wide // 128, 8, group), lambda m: (m, 0, 0, 0)),
             anywhere(),
             anywhere(),
+            anywhere(),
         ],
         [
             jax.ShapeDtypeStruct((micro, group, wide), BF16),
             jax.ShapeDtypeStruct((micro, wide // 128, 8, group), F32),
             jax.ShapeDtypeStruct(out_grad.shape, BF16),
             jax.ShapeDtypeStruct((dim, unit), BF16),
+            jax.ShapeDtypeStruct((dim // 4, near_job[1]), BF16),
         ],
         [
             pltpu.VMEM((group // TILE, TILE * (SPAN + 1), TILE), F32),
@@ -1068,6 +1074,8 @@
             dma,
             dma,
         ]
+        + half_sems(far_count() - 1)
+        + [dma]
         + gather_sems() * len(jobs),
         (lengths, qkv, out_grad, slabs),
     )
@@ -1085,7 +1093,7 @@
     pairs = mix_ref.shape[2] // 128
     lane = lax.broadcasted_iota(jnp.int32, (group, 128), 1)
     zero = jnp.zeros((), BF16)
-    plan = Plan(m, lengths.shape[0], pairs, 18.0)
+    plan = Plan(m, lengths.shape[0], 2 * pairs, 18.0)
     add_scatters(plan, jobs, sources, outs, refs)
 
     @pl.when(m == 0)
@@ -1124,8 +1132,8 @@
             delta = jnp.sum(jnp.where(mine, product, 0.0), axis=1, keepdims=True)
             deltas[now, side] = jnp.broadcast_to(delta, (group, 128))
         for j in range(tiles):
-            if j == 0 and pair:
-                plan.at(pair)
+            if j % 2 == 0 and pair + j:
+                plan.at(2 * pair + j // 2)
             i = min(tiles, j + SPAN + 1)
             tall = (i - j) * TILE
             here, below = slice(j * TILE, (j + 1) * TILE), slice(j * TILE, i * TILE)
@@ -1299,7 +1307,7 @@
 
 
 FEED_US = (5.2, 6.4, 7.2)
-GATHER_AT = ((0.0, 0.0), (0.5, 26.0))
+GATHER_AT = ((0.0, 0.0), (0.0, 8.0), (0.5, 26.0))
 SCATTER_AT = (44.0, 59.0, 71.0, 86.0)
 BACK_US = 2.4
 OUT_PIECE = 512
@@ -1307,7 +1315,7 @@
 
 
 def feed_kernel(
-    steps, widths, loads, cuts, jobs, h_own, h_other, g_own, g_other, unit_0, unit_1, near, slabs,
+    steps, widths, loads, cuts, jobs, h_own, h_other, g_own, g_other, unit_0, unit_1, near_a, near_b, slabs,
     resid, g_late, resid_end, g_end, gains, mixed_out, d_out, d_other, *refs,
 ):
     def take(number):
@@ -1386,9 +1394,17 @@
     plan = Plan(i, chunks * steps, 2, None, clock)
     for chunk in range(1, chunks):
         first, width = cuts[chunk - 1]
-        gather = Gather(slabs.at[:, pl.ds(first, width)], units[chunk - 1], *take(3), near if chunk == 1 else None)
-        plan.add(gather.plan_near(*GATHER_AT[chunk - 1]), lambda: None, 2 * chunk * steps - 2)
-        plan.put(chunk * steps - 1, 1000.0, gather.finish)
+        whole = units[chunk - 1]
+        if chunk == 1:
+            part = near_a.shape[1]
+            parts = [(0, part, near_a, GATHER_AT[0]), (part, width - part, near_b, GATHER_AT[1])]
+        else:
+            parts = [(0, width, None, GATHER_AT[2])]
+        for at, wide, near, times in parts:
+            source = slabs.at[:, pl.ds(first + at, wide)]
+            gather = Gather(source, whole.at[:, pl.ds(at, wide)], *take(3), near)
+            plan.add(gather.plan_near(*times), lambda: None, 2 * chunk * steps - 2)
+            plan.put(chunk * steps - 1, 1000.0, gather.finish)
         plan.put(chunk * steps - 1, 1001.0, lambda chunk=chunk: start_all(copies(chunk)))
     for at, (chunk, (first, width)) in enumerate(jobs):
         scatter = Scatter(grads[chunk], first, outs[at], take(SCATTER_REFS))
@@ -1479,7 +1495,7 @@
             chunk_step(chunk)
 
 
-def feed(rows_in, unit_0, unit_1, near, loads, widths, slabs, cuts, jobs, resid, gains, rows=256):
+def feed(rows_in, unit_0, unit_1, near_a, near_b, loads, widths, slabs, cuts, jobs, resid, gains, rows=256):
     micro, own_rows, dim = rows_in[0].shape
     per = own_rows // rows
     steps = micro * per
@@ -1506,7 +1522,7 @@
         "feed",
         4,
         chunks * steps,
-        [part] * 4 + [anywhere()] * 4 + [late, late, end, end, once((8, dim))],
+        [part] * 4 + [anywhere()] * 5 + [late, late, end, end, once((8, dim))],
         [anywhere()] * (3 + chunks + chunks - 1) + specs,
         [shape] * 3 + grads + units + shapes,
         [pltpu.VMEM((dim, 3 * most), BF16)] * 2
@@ -1522,9 +1538,9 @@
         + [pltpu.SemaphoreType.DMA((chunks, 2, 4)), pltpu.SemaphoreType.DMA((chunks, blocks))]
         + half_sems(3 * steps)
         + [pltpu.SemaphoreType.DMA((2 * steps,))]
-        + gather_sems() * (chunks - 1)
+        + gather_sems() * chunks
         + scatters_scratch([job for _, job in jobs], dim),
-        (*rows_in, unit_0, unit_1, near, slabs, resid, rows_in[2], resid, rows_in[2], gains),
+        (*rows_in, unit_0, unit_1, near_a, near_b, slabs, resid, rows_in[2], resid, rows_in[2], gains),
     )
     return results[:3], results[3 : 3 + chunks], results[2 + 2 * chunks :]
 
@@ -1717,7 +1733,7 @@
 def finish(edges, grad_in, mixed, gain_attn, gain_mlp, gain_sums, feed_grads, out_grads, in_grads, widths, units):
     micro, rows, dim = mixed.shape
     each = gain_sums.shape[1]
-    tile = min(rows, 256)
+    tile = min(rows, 512)
     block = pl.BlockSpec((1, tile, dim), lambda m, t: (m, t, 0))
     small = [gain_attn, gain_mlp, gain_sums, *feed_grads, *out_grads, *in_grads]
     shapes = [jax.ShapeDtypeStruct((1, each), F32)] * 2
@@ -1753,9 +1769,12 @@
 
     begin = [out_columns, out_columns + wide[0], out_columns + wide[0] + wide[1]]
     early = min(EARLY, wide[0])
-    mix, inverse, g_other, unit_0 = attend_all(qkv, lengths, out_grad, slabs, [(0, 0, begin[0] + early)])
-    resid, h_own, h_other, unit_1, near = out_project(
-        mix, inputs, unit_0, gain_full, slabs, [(begin[0] + early, 0, wide[0] - early)], (begin[1], wide[1])
+    ahead = min(AHEAD, wide[1] - 128)
+    mix, inverse, g_other, unit_0, near_a = attend_all(
+        qkv, lengths, out_grad, slabs, [(0, 0, begin[0] + early)], (begin[1], ahead)
+    )
+    resid, h_own, h_other, unit_1, near_b = out_project(
+        mix, inputs, unit_0, gain_full, slabs, [(begin[0] + early, 0, wide[0] - early)], (begin[1] + ahead, wide[1] - ahead)
     )
 
     feed_jobs, at = [[], [], []], []
@@ -1770,7 +1789,8 @@
         (h_own, h_other, out_grad, g_other),
         unit_0,
         unit_1,
-        near,
+        near_a,
+        near_b,
         loads,
         [w // 3 for w in wide],
         slabs,

time: 342 us -> 339 us (level)
  no operation moved by 1% of the time
where the time goes in v4:
time: 339 us; the launch traced here: 333 us
  Pallas kernels  331 us (98%)
    pallas_call x7, Pallas kernels, call(): pl.pallas_call(kernel, grid=steps if isinstance(steps, tuple) else (steps...  331 us

profile of v4, /device:TPU:0, one launch (start us, length us, event | category | flops | bytes accessed | tf_op | source)
XLA Modules:
  0.0 333.3 jit_solution(17025751310509777491)
XLA Ops:
  0.6 1.3 copy.25
  1.9 34.9 %project.1 = (bf16[3,1024,1024]{2,1,0:T(8,128)(2,1)}, bf16[3,1024,768]{2,1,0:T(8,128)(2,1)}, f32[8,1024]{1,0:T(8,128)}, bf16[1024,768]{1,0:T(8,128)(2,1)}, bf16[64,4736]{1,0:T(8,128)(2,1)}) custom-call(bf16[3,512,1024]{2,1,0:T(8,128)(2,1)} %x.3, bf16[64,128]{1,0:T(8,128)(2,1)} %w_query.3, bf16[64,128]{1,0:T(8,128)(2,1)} %w_key.3, bf16[64,512]{1,0:T(8,128)(2,1)} %w_value.3, ...), custom_call_target="tpu_custom_call" | custom-call | tf_op jit(solution)/shard_map/project/pallas_call | solution.py:747
  36.8 32.8 %attend.1 = (bf16[3,1024,512]{2,1,0:T(8,128)(2,1)}, f32[3,4,8,1024]{3,2,1,0:T(8,128)}, bf16[3,512,1024]{2,1,0:T(8,128)(2,1)}, bf16[1024,1152]{1,0:T(8,128)(2,1)}, bf16[256,768]{1,0:T(8,128)(2,1)}) custom-call(s32[3,8]{1,0:T(4,128)} %bitcast.13, bf16[3,1024,768]{2,1,0:T(8,128)(2,1)} %get-tuple-element.57.qkv, bf16[3,512,1024]{2,1,0:T(8,128)(2,1)} %g_end.1, ...), custom_call_target="tpu_custom_call" | custom-call | tf_op jit(solution)/shard_map/attend/pallas_call | solution.py:747
  69.6 23.8 %out_project.1 = (bf16[3,512,1024]{2,1,0:T(8,128)(2,1)}, bf16[3,512,1024]{2,1,0:T(8,128)(2,1)}, bf16[3,512,1024]{2,1,0:T(8,128)(2,1)}, bf16[1024,512]{1,0:T(8,128)(2,1)}, bf16[256,768]{1,0:T(8,128)(2,1)}) custom-call(bf16[3,1024,512]{2,1,0:T(8,128)(2,1)} %get-tuple-element.59.mix_own.mix_other.mix_ref, ...), custom_call_target="tpu_custom_call" | custom-call | tf_op jit(solution)/shard_map/out_project/pallas_call | solution.py:747
  93.4 127.4 %feed.1 = (bf16[3,512,1024]{2,1,0:T(8,128)(2,1)}, bf16[3,512,1024]{2,1,0:T(8,128)(2,1)}, bf16[3,512,1024]{2,1,0:T(8,128)(2,1)}, bf16[4,4,2,32,1152]{4,3,2,1,0:T(...) custom-call(bf16[3,512,1024]{2,1,0:T(8,128)(2,1)} %get-tuple-element, ...), custom_call_target="tpu_custom_call" | custom-call | tf_op jit(solution)/shard_map/feed/pallas_call | solution.py:747
  220.8 64.2 %attend_back.1 = (bf16[3,1024,768]{2,1,0:T(8,128)(2,1)}, bf16[4,4,2,32,512]{4,3,2,1,0:T(8,128)(2,1)}, f32[2,32,768]{2,1,0:T(8,128)}, f32[2,32,768]{2,1,0:T(8,128...) custom-call(s32[3,8]{1,0:T(4,128)} %bitcast.14, bf16[3,1024,768]{2,1,0:T(8,128)(2,1)} %get-tuple-element.57.qkv, ...), custom_call_target="tpu_custom_call" | custom-call | tf_op jit(solution)/shard_map/attend_back/pallas_call | solution.py:747
  285.1 40.1 %back_in.1 = (bf16[3,512,1024]{2,1,0:T(8,128)(2,1)}, f32[2,64,128]{2,1,0:T(8,128)}, bf16[4,4,2,32,768]{4,3,2,1,0:T(8,128)(2,1)}, f32[2,32,512]{2,1,0:T(8,128)}, ...) custom-call(bf16[3,1024,1024]{2,1,0:T(8,128)(2,1)} %get-tuple-element.56.h, ...), custom_call_target="tpu_custom_call" | custom-call | tf_op jit(solution)/shard_map/back_in/pallas_call | solution.py:747
  325.2 7.9 %finish.1 = (bf16[3,512,1024]{2,1,0:T(8,128)(2,1)}, f32[3,512,1024]{2,1,0:T(8,128)}, f32[1,64]{1,0:T(1,128)}, f32[1,64]{1,0:T(1,128)}, f32[64,128]{1,0:T(8,128)}...) custom-call(bf16[3,512,1024]{2,1,0:T(8,128)(2,1)} %get-tuple-element, ...), custom_call_target="tpu_custom_call" | custom-call | tf_op jit(solution)/shard_map/finish/pallas_call | solution.py:747

commit v5 on v4

--- a/solution.py
+++ b/solution.py
@@ -708,7 +708,7 @@
 
     def plan(self, start):
         along = RATE * self.mine.shape[3]
-        times = (start, start + 1.5 + 2 * along / 3, start + 3 + along)
+        times = (start, start + 2.5 + 2 * along / 3, start + 5 + along)
         return list(zip(times, (self.begin, self.second, self.third)))
 
 
@@ -1308,7 +1308,7 @@
 
 FEED_US = (5.2, 6.4, 7.2)
 GATHER_AT = ((0.0, 0.0), (0.0, 8.0), (0.5, 26.0))
-SCATTER_AT = (44.0, 59.0, 71.0, 86.0)
+SCATTER_AT = (52.0, 67.0, 79.0, 90.0)
 BACK_US = 2.4
 OUT_PIECE = 512
 IN_PIECE = 384

time: 339 us -> 331 us (0.976)
  Pallas kernels: 331 us -> 323 us
    pallas_call x7, Pallas kernels: 331 us -> 323 us  [call(): pl.pallas_call(kernel, grid=steps if isinstance(steps, tuple) else (steps...]
where the time goes in v5:
time: 331 us; the launch traced here: 325 us
  Pallas kernels  323 us (98%)
    pallas_call x7, Pallas kernels, call(): pl.pallas_call(kernel, grid=steps if isinstance(steps, tuple) else (steps...  323 us

profile of v5, /device:TPU:0, one launch (start us, length us, event | category | flops | bytes accessed | tf_op | source)
XLA Modules:
  0.0 325.1 jit_solution(13834933633637670402)
XLA Ops:
  0.6 1.3 copy.25
  1.9 34.9 %project.1 = (bf16[3,1024,1024]{2,1,0:T(8,128)(2,1)}, bf16[3,1024,768]{2,1,0:T(8,128)(2,1)}, f32[8,1024]{1,0:T(8,128)}, bf16[1024,768]{1,0:T(8,128)(2,1)}, bf16[64,4736]{1,0:T(8,128)(2,1)}) custom-call(bf16[3,512,1024]{2,1,0:T(8,128)(2,1)} %x.3, bf16[64,128]{1,0:T(8,128)(2,1)} %w_query.3, bf16[64,128]{1,0:T(8,128)(2,1)} %w_key.3, bf16[64,512]{1,0:T(8,128)(2,1)} %w_value.3, ...), custom_call_target="tpu_custom_call" | custom-call | tf_op jit(solution)/shard_map/project/pallas_call | solution.py:747
  36.8 32.8 %attend.1 = (bf16[3,1024,512]{2,1,0:T(8,128)(2,1)}, f32[3,4,8,1024]{3,2,1,0:T(8,128)}, bf16[3,512,1024]{2,1,0:T(8,128)(2,1)}, bf16[1024,1152]{1,0:T(8,128)(2,1)}, bf16[256,768]{1,0:T(8,128)(2,1)}) custom-call(s32[3,8]{1,0:T(4,128)} %bitcast.13, bf16[3,1024,768]{2,1,0:T(8,128)(2,1)} %get-tuple-element.57.qkv, bf16[3,512,1024]{2,1,0:T(8,128)(2,1)} %g_end.1, ...), custom_call_target="tpu_custom_call" | custom-call | tf_op jit(solution)/shard_map/attend/pallas_call | solution.py:747
  69.6 23.8 %out_project.1 = (bf16[3,512,1024]{2,1,0:T(8,128)(2,1)}, bf16[3,512,1024]{2,1,0:T(8,128)(2,1)}, bf16[3,512,1024]{2,1,0:T(8,128)(2,1)}, bf16[1024,512]{1,0:T(8,128)(2,1)}, bf16[256,768]{1,0:T(8,128)(2,1)}) custom-call(bf16[3,1024,512]{2,1,0:T(8,128)(2,1)} %get-tuple-element.59.mix_own.mix_other.mix_ref, ...), custom_call_target="tpu_custom_call" | custom-call | tf_op jit(solution)/shard_map/out_project/pallas_call | solution.py:747
  93.4 121.0 %feed.1 = (bf16[3,512,1024]{2,1,0:T(8,128)(2,1)}, bf16[3,512,1024]{2,1,0:T(8,128)(2,1)}, bf16[3,512,1024]{2,1,0:T(8,128)(2,1)}, bf16[4,4,2,32,1152]{4,3,2,1,0:T(...) custom-call(bf16[3,512,1024]{2,1,0:T(8,128)(2,1)} %get-tuple-element, ...), custom_call_target="tpu_custom_call" | custom-call | tf_op jit(solution)/shard_map/feed/pallas_call | solution.py:747
  214.4 62.2 %attend_back.1 = (bf16[3,1024,768]{2,1,0:T(8,128)(2,1)}, bf16[4,4,2,32,512]{4,3,2,1,0:T(8,128)(2,1)}, f32[2,32,768]{2,1,0:T(8,128)}, f32[2,32,768]{2,1,0:T(8,128...) custom-call(s32[3,8]{1,0:T(4,128)} %bitcast.14, bf16[3,1024,768]{2,1,0:T(8,128)(2,1)} %get-tuple-element.57.qkv, ...), custom_call_target="tpu_custom_call" | custom-call | tf_op jit(solution)/shard_map/attend_back/pallas_call | solution.py:747
  276.6 40.3 %back_in.1 = (bf16[3,512,1024]{2,1,0:T(8,128)(2,1)}, f32[2,64,128]{2,1,0:T(8,128)}, bf16[4,4,2,32,768]{4,3,2,1,0:T(8,128)(2,1)}, f32[2,32,512]{2,1,0:T(8,128)}, ...) custom-call(bf16[3,1024,1024]{2,1,0:T(8,128)(2,1)} %get-tuple-element.56.h, ...), custom_call_target="tpu_custom_call" | custom-call | tf_op jit(solution)/shard_map/back_in/pallas_call | solution.py:747
  316.9 7.9 %finish.1 = (bf16[3,512,1024]{2,1,0:T(8,128)(2,1)}, f32[3,512,1024]{2,1,0:T(8,128)}, f32[1,64]{1,0:T(1,128)}, f32[1,64]{1,0:T(1,128)}, f32[64,128]{1,0:T(8,128)}...) custom-call(bf16[3,512,1024]{2,1,0:T(8,128)(2,1)} %get-tuple-element, ...), custom_call_target="tpu_custom_call" | custom-call | tf_op jit(solution)/shard_map/finish/pallas_call | solution.py:747
